TPU v7x, 512 devices: a whole 4x8x8 slice. The times are simulated.
512 devices in a mesh: segment: 4 (over x_hi, core), lat: 128 (over z, y, x_lo).
Axes of the slice: x: 4 (x_hi: 2, x_lo: 2; x = x_hi * 2 + x_lo), y: 8, z: 8, core: 2. Of those that a mesh axis runs over, the one named last changes fastest.
Arguments:
- fields: bfloat16 [4, 21504, 144], P('segment', 'lat'), may hold values from -6 to 6
- band_rows: int32 [128], replicated, may hold values from 1 to 2, 192 in all
- window_table: int32 [128], replicated, may hold values from -1 to 118, as said below
- level_embed: bfloat16 [2, 1024], replicated, may hold values from -6 to 6
- embed_weight: bfloat16 [144, 1024], replicated, may hold values from -0.5 to 0.5
- attn_weight: bfloat16 [4, 1024, 4096], P('segment', None, 'lat'), may hold values from -0.1875 to 0.1875
- norm_gain: float32 [4, 1024], P('segment'), may hold values from 0.5 to 1.5
- head_weight: bfloat16 [1024, 144], replicated, may hold values from -0.1875 to 0.1875
Outputs:
- decoded: bfloat16 [4, 21504, 144], P('segment', 'lat')
- window_decoded: bfloat16 [4, 18432, 144], P('segment', 'lat')
Inputs may be any that keep to these rules, and one draw needn't show every extreme that they name: `window_table`: each window 0 to 118 appears once, other shards hold -1. `band_rows`: rows of each band sum to 192.
All inputs are finite; a program needn't handle non-finite values.
Results may differ from a plain program's by a relative error of at most 0.025.
Values may be sent and summed in bfloat16 or wider, within the bound.
No kernel may reach another device: no remote copies, remote signals or barrier semaphores. Data moves between devices by JAX's collectives and lax.ppermute only.
A program may use at most 64 MiB of HBM per device.

v0:
```python
import math

import jax
import jax.numpy as jnp
from jax import lax
from jax.experimental import pallas as pl
from jax.experimental.pallas import tpu as pltpu
from jax.sharding import Mesh
from jax.sharding import PartitionSpec as P

HEAD_DIM = 64
LEV = 2
WIN_ROWS = 12
WIN_COLS = 6
WTOK = 144
FEAT = 144
LW = 7
PIECE = WIN_COLS * LEV * FEAT
PACK = 16
BF = jnp.bfloat16
F32 = jnp.float32
LAT = ("z", "y", "xl")
DOUBLING = (4, 2, 1)
OFFS = (0, 4, 2, 6, 1, 5, 3, 7)
MIB = 1 << 20

VMEM = pl.BlockSpec(memory_space=pltpu.VMEM)
SMEM = pl.BlockSpec(memory_space=pltpu.SMEM)
ANY = pl.BlockSpec(memory_space=pl.ANY)


def ring(value, axis, by):
    n = lax.axis_size(axis)
    return lax.ppermute(value, axis, [(i, (i + by) % n) for i in range(n)])


def swap(value, axis, bit):
    n = lax.axis_size(axis)
    return lax.ppermute(value, axis, [(i, i ^ bit) for i in range(n)])


def seventh(window):
    return lax.shift_right_logical(window * 147, 10)


def first_row(window):
    return WIN_ROWS * seventh(jnp.maximum(window, 0)) - WIN_ROWS // 2


def pack_kernel(table, rows_ref, out_ref):
    def shard(j, carry):
        window = jnp.maximum(table[j], 0)
        column = window - LW * seventh(window)
        out_ref[2 * j] = rows_ref[column]
        out_ref[2 * j + 1] = rows_ref[LW + column]
        return carry

    lax.fori_loop(0, table.shape[0], shard, 0, unroll=8)


def pick_kernel(where, bands, table, came_ref, out_ref):
    window = table[where[0]]
    first = first_row(window)
    out_ref[...] = jnp.zeros_like(out_ref)
    count_rows = jnp.where(window >= 0, WIN_ROWS, 0)

    def band(i, row):
        count = bands[i]
        here = (row >= 0) & (row < count_rows)
        out_ref[jnp.where(here, row, WIN_ROWS)] = came_ref[2 * i]
        here = (count > 1) & (row >= -1) & (row + 1 < count_rows)
        out_ref[jnp.where(here, row + 1, WIN_ROWS)] = came_ref[2 * i + 1]
        return row + count

    lax.fori_loop(0, bands.shape[0], band, -first, unroll=8)


def unpick_kernel(where, bands, table, rows_ref, out_ref):
    first = first_row(table[where[0]])

    def band(i, row):
        out_ref[2 * i] = rows_ref[jnp.clip(row, 0, WIN_ROWS - 1)]
        out_ref[2 * i + 1] = rows_ref[jnp.clip(row + 1, 0, WIN_ROWS - 1)]
        return row + bands[i]

    lax.fori_loop(0, bands.shape[0], band, -first, unroll=8)


def unpack_kernel(where, bands, table, came_ref, out_ref):
    mine = where[0]
    start = lax.fori_loop(
        0, bands.shape[0], lambda i, total: total + jnp.where(i < mine, bands[i], 0), jnp.int32(0), unroll=8
    )
    across = lax.div(start + WIN_ROWS // 2, WIN_ROWS)
    across_next = jnp.where(bands[mine] > 1, lax.div(start + 1 + WIN_ROWS // 2, WIN_ROWS), -1)
    out_ref[...] = jnp.zeros_like(out_ref)

    def shard(j, carry):
        window = jnp.maximum(table[j], 0)
        line = jnp.where(table[j] >= 0, seventh(window), -2)
        column = window - LW * seventh(window)
        out_ref[jnp.where(line == across, column, 2 * LW)] = came_ref[2 * j]
        out_ref[jnp.where(line == across_next, LW + column, 2 * LW)] = came_ref[2 * j + 1]
        return carry

    lax.fori_loop(0, table.shape[0], shard, 0, unroll=8)


def to_rows(tokens):
    rows = tokens.reshape(-1, PIECE)
    return jnp.pad(rows, ((0, 0), (0, PACK * 128 - PIECE))).reshape(-1, PACK, 128)


def from_rows(rows):
    return rows.reshape(-1, PACK * 128)[:, :PIECE].reshape(-1, FEAT)


def join_kernel(pos, *refs):
    out_ref, out, turned, sem = refs[-4:]
    pieces = refs[:-4]
    half = len(pieces) // 2
    z, y = pos[1], pos[2]

    def copies(side, index):
        ref = pieces[side * half + index]
        step = (0, -1, -2, -3, 1, 2, 3, 4)[index]
        for slot, sub in enumerate(range(8)):
            if side == 0:
                plane, line = lax.rem(z + step + 8, 8), y ^ OFFS[sub]
            else:
                plane, line = z ^ OFFS[sub], lax.rem(y + step + 8, 8)
            row = pl.multiple_of((plane * 8 + line) * 64, 64)
            yield pltpu.make_async_copy(
                ref.at[pl.ds(slot * 64, 64)], out.at[side, pl.ds(row, 64)], sem
            )

    every = [c for side in range(2) for i in range(half) for c in copies(side, i)]
    for c in every:
        c.start()
    for c in every:
        c.wait()

    @pl.loop(0, 8)
    def _(plane):
        lanes = pl.ds(pl.multiple_of(plane * 512, 512), 512)
        for side in range(2):
            turned[512 * side : 512 * (side + 1), lanes] = out[side, lanes, :].T

    back = pltpu.make_async_copy(turned, out_ref, sem)
    back.start()
    back.wait()


def gather_section(weight, pos, message, arrived, gains):
    mine, _ = lax.optimization_barrier((weight[0].T, message))
    pair = lax.all_gather(mine, "xl", axis=0, tiled=True)
    pair, gains = lax.optimization_barrier((pair, gains))
    a, b = pair[:, :512], pair[:, 512:]
    for bit in DOUBLING:
        a_far, b_far = swap(a, "y", bit), swap(b, "z", bit)
        a, b = jnp.concatenate([a, a_far]), jnp.concatenate([b, b_far])
    a, b, arrived = lax.optimization_barrier((a, b, arrived))
    chains = [("z", 1), ("z", -1), ("y", 1), ("y", -1)]
    got = [[] for _ in chains]
    held = [a, a, b, b]
    for step in range(4):
        for n, (axis, by) in enumerate(chains):
            if step < 3 or by > 0:
                held[n] = ring(held[n], axis, by)
                got[n].append(held[n])
    pieces = []
    for own, ahead, behind in ((a, got[0], got[1]), (b, got[2], got[3])):
        pieces += [own, *ahead[:3], *behind, ahead[3]]
    section = pl.pallas_call(
        join_kernel,
        out_shape=jax.ShapeDtypeStruct((1024, 4096), BF),
        in_specs=[SMEM] + [ANY] * len(pieces),
        out_specs=ANY,
        scratch_shapes=[
            pltpu.VMEM((2, 4096, 512), BF),
            pltpu.VMEM((1024, 4096), BF),
            pltpu.SemaphoreType.DMA(()),
        ],
        compiler_params=pltpu.CompilerParams(vmem_limit_bytes=60 * MIB),
        name="join",
    )(pos, *pieces)
    return section, arrived, gains


def matmul_t(left, right):
    return lax.dot_general(left, right, (((1,), (1,)), ((), ())), preferred_element_type=F32)


def normed_of(wide, gain):
    scale = lax.rsqrt(jnp.mean(wide * wide, axis=-1, keepdims=True) + 1e-06)
    return (wide * scale * gain).astype(BF)


def other_level(value):
    half = WTOK // 2
    parts = [value[half * i : half * (i + 1)] for i in range(value.shape[0] // half)]
    return jnp.concatenate([parts[i ^ 1] for i in range(len(parts))], axis=0)


def column_block(hidden, gain, project):
    wide = hidden.astype(F32)
    normed = normed_of(wide, gain)
    query = project(normed, 0).astype(BF).astype(F32)
    keyed = project(normed, 1).astype(BF).astype(F32)
    product = query * (keyed - other_level(keyed))
    lane = lax.broadcasted_iota(jnp.int32, (1024, 128), 0)
    head = lax.broadcasted_iota(jnp.int32, (1024, 128), 1)
    of_head = (lax.div(lane, HEAD_DIM) == head).astype(BF)
    high = product.astype(BF)
    low = (product - high.astype(F32)).astype(BF)
    gap = (
        jnp.dot(high, of_head, preferred_element_type=F32)
        + jnp.dot(low, of_head, preferred_element_type=F32)
    ) * (1 / math.sqrt(HEAD_DIM))
    small = jnp.exp(-jnp.abs(gap))
    larger = 1.0 / (1.0 + small)
    smaller = small * larger
    own = jnp.where(gap >= 0, larger, smaller).astype(BF)
    far = jnp.where(gap >= 0, smaller, larger).astype(BF)
    valued = project(normed, 2).astype(BF).astype(F32)
    mixed = (matmul_t(own, of_head) * valued + matmul_t(far, of_head) * other_level(valued)).astype(BF)
    return (wide + project(mixed, 3)).astype(BF)


def window_block(hidden, gain, project, bias):
    wide = hidden.astype(F32)
    normed = normed_of(wide, gain)
    query = (project(normed, 0).astype(BF).astype(F32) * (1 / math.sqrt(HEAD_DIM))).astype(BF)
    keyed = project(normed, 1).astype(BF)
    valued = project(normed, 2).astype(BF)
    low = lax.broadcasted_iota(jnp.int32, (WTOK, 128), 1) < HEAD_DIM
    ones = jnp.ones((WTOK, 128), BF)
    slabs = []
    for slab in range(hidden.shape[0] // WTOK):
        here = slice(WTOK * slab, WTOK * (slab + 1))
        mixed = []
        for two in range(8):
            lanes = slice(128 * two, 128 * (two + 1))
            q2, k2 = query[here, lanes], keyed[here, lanes]
            v2 = jnp.concatenate([valued[here, lanes], ones], axis=1)
            outs = []
            for part in range(2):
                q1 = jnp.where(low if part == 0 else ~low, q2, jnp.zeros_like(q2))
                scores = matmul_t(q1, k2) + bias
                top = jnp.max(scores, axis=-1, keepdims=True)
                grown = jnp.exp(scores - top).astype(BF)
                summed = jnp.dot(grown, v2, preferred_element_type=F32)
                outs.append(summed[:, :128] / summed[:, 128:])
            mixed.append(jnp.where(low, outs[0], outs[1]).astype(BF))
        slabs.append(jnp.concatenate(mixed, axis=1))
    mixed = jnp.concatenate(slabs, axis=0)
    return (wide + project(mixed, 3)).astype(BF)


def projections(pos, own_ref, other_ref, weights, sems):
    core = pos[3]

    def load(source, section):
        for part in range(4):
            columns = pl.ds(1024 * part, 1024)
            pltpu.make_async_copy(
                source.at[:, columns], weights.at[section, :, columns], sems.at[section, part]
            ).start()

    @pl.when(core == 0)
    def _():
        load(own_ref, 0)
        load(other_ref, 1)

    @pl.when(core == 1)
    def _():
        load(other_ref, 0)
        load(own_ref, 1)

    def of_section(section):
        def project(left, part):
            columns = pl.ds(1024 * part, 1024)
            pltpu.make_async_copy(
                own_ref.at[:, columns], weights.at[section, :, columns], sems.at[section, part]
            ).wait()
            right = weights[section, :, 1024 * part : 1024 * (part + 1)]
            return jnp.dot(left, right, preferred_element_type=F32)

        return project

    return of_section(0), of_section(1)


def inside(pos, bands, table, token):
    window = table[pos[0]]
    row = first_row(window) + lax.rem(lax.div(token, WIN_COLS), WIN_ROWS)
    return (window >= 0) & (row >= 0) & (row < 3 * bands.shape[0] // 2)


def key_bias(pos, bands, table):
    token = lax.broadcasted_iota(jnp.int32, (1, WTOK), 1)
    return jnp.where(inside(pos, bands, table, token), 0.0, -1e30)


def early_kernel(
    pos, bands, table, raw_ref, far_ref, embed_ref, level_ref, gain_ref, own_ref, other_ref,
    hidden_ref, weights, sems,
):
    first, second = projections(pos, own_ref, other_ref, weights, sems)
    to_token = lax.broadcasted_iota(jnp.int32, (WTOK, WTOK), 0)
    from_token = lax.broadcasted_iota(jnp.int32, (WTOK, WTOK), 1)
    half = WTOK // 2
    to_window = (lax.div(to_token, half) == lax.rem(from_token, LEV)) & (
        lax.rem(to_token, half) == lax.div(from_token, LEV)
    )
    to_window = to_window.astype(BF)
    raws = [jnp.dot(to_window, ref[...], preferred_element_type=F32) for ref in (raw_ref, far_ref)]
    raw = jnp.concatenate(raws, axis=0).astype(BF)
    token = lax.broadcasted_iota(jnp.int32, (2 * WTOK, 1), 0)
    upper = lax.rem(token, WTOK) < half
    level_rows = jnp.where(upper, level_ref[0:1].astype(F32), level_ref[1:2].astype(F32))
    hidden = (jnp.dot(raw, embed_ref[...], preferred_element_type=F32) + level_rows).astype(BF)
    hidden = column_block(hidden, gain_ref[0:1], first)
    hidden_ref[...] = window_block(hidden, gain_ref[1:2], second, key_bias(pos, bands, table))


def late_kernel(
    pos, bands, table, came_ref, gain_ref, head_ref, own_ref, other_ref,
    give_ref, out_ref, rows_ref, weights, sems,
):
    first, second = projections(pos, own_ref, other_ref, weights, sems)
    hidden = window_block(came_ref[...], gain_ref[0:1], first, key_bias(pos, bands, table))
    hidden = column_block(hidden, gain_ref[1:2], second)
    result = jnp.dot(hidden, head_ref[...], preferred_element_type=F32)
    keep = inside(pos, bands, table, lax.broadcasted_iota(jnp.int32, (WTOK, 1), 0))
    to_token = lax.broadcasted_iota(jnp.int32, (WTOK, WTOK), 0)
    from_token = lax.broadcasted_iota(jnp.int32, (WTOK, WTOK), 1)
    half = WTOK // 2
    from_window = (lax.rem(to_token, LEV) == lax.div(from_token, half)) & (
        lax.div(to_token, LEV) == lax.rem(from_token, half)
    )
    from_window = from_window.astype(BF)
    for slab in range(2):
        out = jnp.where(keep, result[WTOK * slab : WTOK * (slab + 1)], 0.0).astype(BF)
        rows = jnp.dot(from_window, out, preferred_element_type=F32).astype(BF)
        if slab == 0:
            give_ref[0], give_ref[1] = out, rows
        else:
            out_ref[...], rows_ref[...] = out, rows


def sections_call(body, shapes, scalars, values, own, other, name):
    return pl.pallas_call(
        body,
        out_shape=tuple(jax.ShapeDtypeStruct(shape, BF) for shape in shapes),
        in_specs=[SMEM] * len(scalars) + [VMEM] * len(values) + [ANY] * 2,
        out_specs=(VMEM,) * len(shapes),
        scratch_shapes=[
            pltpu.VMEM((2, 1024, 4096), BF),
            pltpu.SemaphoreType.DMA((2, 4)),
        ],
        compiler_params=pltpu.CompilerParams(vmem_limit_bytes=60 * MIB),
        name=name,
    )(*scalars, *values, own, other)


def small_call(body, out_rows, scalars, value, name):
    return pl.pallas_call(
        body,
        out_shape=jax.ShapeDtypeStruct((out_rows, PACK, 128), BF),
        in_specs=[SMEM] * len(scalars) + [VMEM],
        out_specs=VMEM,
        name=name,
    )(*scalars, value)


def crossed(value, sources):
    return lax.ppermute(value, ("xh", "xl"), [(x, 3 - x) for x in sources])


def per_device(
    fields, band_rows, window_table, level_embed, embed_weight, attn_weight, norm_gain, head_weight
):
    late, core = lax.axis_index("xh"), lax.axis_index("c")
    is_late = late == 1
    pos = jnp.stack([lax.axis_index(LAT), lax.axis_index("z"), lax.axis_index("y"), core, late])
    lat_count = band_rows.shape[0]
    width = embed_weight.shape[1]
    turned = window_table.reshape(-1, 2)[:, ::-1].reshape(-1)
    table = jnp.where(is_late, turned, window_table)
    scalars = (pos, band_rows, table)

    message = small_call(pack_kernel, 2 * lat_count, (table,), to_rows(fields[0]), "pack")
    arrived = lax.all_to_all(message, LAT, 0, 0, tiled=True)
    gains = lax.all_gather(norm_gain, "c", axis=0, tiled=True)
    own, arrived, gains = gather_section(attn_weight, pos, message, arrived, gains)
    raw_rows = small_call(pick_kernel, WIN_ROWS + 1, scalars, arrived, "pick")
    own_raw = from_rows(raw_rows[:WIN_ROWS])
    far_raw = crossed(own_raw, (2, 3))
    other = swap(own, "c", 1)

    [hidden] = sections_call(
        early_kernel,
        [(2 * WTOK, width)],
        scalars,
        (own_raw, far_raw, embed_weight, level_embed, gains),
        own,
        other,
        "early",
    )
    came = crossed(hidden, (0, 1))
    given, out, rows = sections_call(
        late_kernel,
        [(2, WTOK, FEAT), (WTOK, FEAT), (WTOK, FEAT)],
        scalars,
        (came, gains, head_weight),
        own,
        other,
        "late",
    )
    taken = crossed(given, (2, 3))
    own_rows = jnp.where(is_late, rows, taken[1])
    reply = small_call(unpick_kernel, 2 * lat_count, scalars, to_rows(own_rows), "unpick")
    came_back = lax.all_to_all(reply, LAT, 0, 0, tiled=True)
    window_decoded = jnp.where(is_late, swap(out, "xl", 1), taken[0])[None]
    decoded_rows = small_call(unpack_kernel, 2 * LW + 1, scalars, came_back, "unpack")
    decoded = from_rows(decoded_rows[: 2 * LW])[None]
    return (decoded, window_decoded)


def solution(mesh):
    fine = Mesh(mesh.devices.reshape(2, 2, 8, 8, 2), ("xh", "c", "z", "y", "xl"))
    segment = ("xh", "c")
    placed = (
        P(segment, LAT, None),
        P(),
        P(),
        P(),
        P(),
        P(segment, None, LAT),
        P(segment, None),
        P(),
    )
    return jax.shard_map(
        per_device,
        mesh=fine,
        in_specs=placed,
        out_specs=(P(segment, LAT, None), P(segment, LAT, None)),
        check_vma=False,
    )
```

profile of v0, /device:TPU:12, one launch (start us, length us, event | category | flops | bytes accessed | tf_op | source)
XLA Modules:
  0.0 267.7 jit_solution(5761416600827436927)
XLA Ops:
  6.2 18.0 %all-to-all-start = ((bf16[256,16,128]{2,1,0:T(8,128)(2,1)}), bf16[256,16,128]{2,1,0:T(8,128)(2,1)S(1)}, u32[]{:S(2)}, u32[]{:S(2)}) async-start(bf16[256,16,128]{2,1,0:T(8,128)(2,1)} %pack.1), calls=%async_computation | async-start | bytes 2097152 | tf_op jit(solution)/shard_map/all_to_all | solution.py:394
  26.8 6.5 %all_gather.6 = bf16[64,1024]{1,0:T(8,128)(2,1)S(1)} all-gather(bf16[32,1024]{1,0:T(8,128)(2,1)} %bitcast.46), channel_id=1, replica_groups=mesh['xh'=2,'c'=2,'z'=8,'y'=8,'xl'=2] {'xl'}, dimensions={0}, use_global_device_ids=true | all-gather | bytes 196608 | tf_op jit(solution)/shard_map/all_gather | solution.py:156
  33.3 7.5 %collective-permute-start.3 = (bf16[64,512]{1,0:T(8,128)(2,1)S(1)}, bf16[64,512]{1,0:T(8,128)(2,1)S(1)}, u32[]{:S(2)}, u32[]{:S(2)}) collective-permute-start(bf16[64,512]{1,0:T(8,128)(2,1)S(1)} %get-tuple-element.26), channel_id=1, source_target_pairs={{0,64},{16,80},{32,96},{48,112},{64,0},{80,16},{96,32},{112,48},{1... | collective-permute-start | bytes 196616 | tf_op jit(solution)/shard_map/ppermute | solution.py:39
  40.8 6.0 %collective-permute-start = (bf16[64,512]{1,0:T(8,128)(2,1)S(1)}, bf16[64,512]{1,0:T(8,128)(2,1)S(1)}, u32[]{:S(2)}, u32[]{:S(2)}) collective-permute-start(bf16[64,512]{1,0:T(8,128)(2,1)S(1)} %get-tuple-element.27), channel_id=1, source_target_pairs={{0,8},{2,10},{4,12},{6,14},{8,0},{10,2},{12,4},{14,6},{1,9},{3,11}... | collective-permute-start | bytes 196616 | tf_op jit(solution)/shard_map/ppermute | solution.py:39
  46.8 3.8 %collective-permute-done.3 = bf16[64,512]{1,0:T(8,128)(2,1)S(1)} collective-permute-done((bf16[64,512]{1,0:T(8,128)(2,1)S(1)}, bf16[64,512]{1,0:T(8,128)(2,1)S(1)}, u32[]{:S(2)}, u32[]{:S(2)}) %collective-permute-start.3) | collective-permute-done | bytes 65568 | tf_op jit(solution)/shard_map/ppermute | solution.py:39
  50.7 7.3 %collective-permute-start.4 = (bf16[128,512]{1,0:T(8,128)(2,1)S(1)}, bf16[128,512]{1,0:T(8,128)(2,1)S(1)}, u32[]{:S(2)}, u32[]{:S(2)}) collective-permute-start(bf16[128,512]{1,0:T(8,128)(2,1)S(1)} %pad_maximum_fusion.5), channel_id=1, source_target_pairs={{0,32},{16,48},{32,0},{48,16},{64,96},{80,112},{96,64},{112,80},{1... | collective-permute-start | bytes 393224 | tf_op jit(solution)/shard_map/ppermute | solution.py:39
  58.0 4.2 %collective-permute-start.1 = (bf16[128,512]{1,0:T(8,128)(2,1)S(1)}, bf16[128,512]{1,0:T(8,128)(2,1)S(1)}, u32[]{:S(2)}, u32[]{:S(2)}) collective-permute-start(bf16[128,512]{1,0:T(8,128)(2,1)S(1)} %pad_maximum_fusion.4), channel_id=1, source_target_pairs={{0,4},{2,6},{4,0},{6,2},{8,12},{10,14},{12,8},{14,10},{1,5},{3,7},... | collective-permute-start | bytes 393224 | tf_op jit(solution)/shard_map/ppermute | solution.py:39
  66.6 4.1 %collective-permute-start.2 = (bf16[256,512]{1,0:T(8,128)(2,1)S(1)}, bf16[256,512]{1,0:T(8,128)(2,1)S(1)}, u32[]{:S(2)}, u32[]{:S(2)}) collective-permute-start(bf16[256,512]{1,0:T(8,128)(2,1)S(1)} %pad_maximum_fusion.2), channel_id=1, source_target_pairs={{0,2},{2,0},{4,6},{6,4},{8,10},{10,8},{12,14},{14,12},{1,3},{3,1},... | collective-permute-start | bytes 786440 | tf_op jit(solution)/shard_map/ppermute | solution.py:39
  72.0 4.4 %collective-permute-done.2 = bf16[256,512]{1,0:T(8,128)(2,1)S(1)} collective-permute-done((bf16[256,512]{1,0:T(8,128)(2,1)S(1)}, bf16[256,512]{1,0:T(8,128)(2,1)S(1)}, u32[]{:S(2)}, u32[]{:S(2)}) %collective-permute-start.2) | collective-permute-done | bytes 262176 | tf_op jit(solution)/shard_map/ppermute | solution.py:39
  76.6 3.3 %collective-permute-start.7 = (bf16[512,512]{1,0:T(8,128)(2,1)S(1)}, bf16[512,512]{1,0:T(8,128)(2,1)S(1)}, u32[]{:S(2)}, u32[]{:S(2)}) collective-permute-start(bf16[512,512]{1,0:T(8,128)(2,1)S(1)} %pad_maximum_fusion.refs_0_), channel_id=1, source_target_pairs={{0,16},{16,32},{32,48},{48,64},{64,80},{80,96},{96,112},{112,0},{1... | collective-permute-start | bytes 1572872 | tf_op jit(solution)/shard_map/ppermute | solution.py:34
  79.9 3.8 %collective-permute-start.14 = (bf16[512,512]{1,0:T(8,128)(2,1)S(1)}, bf16[512,512]{1,0:T(8,128)(2,1)S(1)}, u32[]{:S(2)}, u32[]{:S(2)}) collective-permute-start(bf16[512,512]{1,0:T(8,128)(2,1)S(1)} %pad_maximum_fusion.1.refs_8_), channel_id=1, source_target_pairs={{0,2},{2,4},{4,6},{6,8},{8,10},{10,12},{12,14},{14,0},{1,3},{3,5},... | collective-permute-start | bytes 1572872 | tf_op jit(solution)/shard_map/ppermute | solution.py:34
  83.7 4.0 %collective-permute-start.10 = (bf16[512,512]{1,0:T(8,128)(2,1)S(1)}, bf16[512,512]{1,0:T(8,128)(2,1)S(1)}, u32[]{:S(2)}, u32[]{:S(2)}) collective-permute-start(bf16[512,512]{1,0:T(8,128)(2,1)S(1)} %pad_maximum_fusion.refs_0_), channel_id=1, source_target_pairs={{0,112},{16,0},{32,16},{48,32},{64,48},{80,64},{96,80},{112,96},{1... | collective-permute-start | bytes 1572872 | tf_op jit(solution)/shard_map/ppermute | solution.py:34
  89.6 2.5 collective-permute-done.7.refs_1_
  94.5 4.2 %collective-permute-start.15 = (bf16[512,512]{1,0:T(8,128)(2,1)S(1)}, bf16[512,512]{1,0:T(8,128)(2,1)S(1)}, u32[]{:S(2)}, u32[]{:S(2)}) collective-permute-start(bf16[512,512]{1,0:T(8,128)(2,1)S(1)} %collective-permute-done.14.refs_9_), channel_id=1, source_target_pairs={{0,2},{2,4},{4,6},{6,8},{8,10},{10,12},{12,14},{14,0},{1,3},{3,5},... | collective-permute-start | bytes 1572872 | tf_op jit(solution)/shard_map/ppermute | solution.py:34
  98.8 5.1 %collective-permute-start.11 = (bf16[512,512]{1,0:T(8,128)(2,1)S(1)}, bf16[512,512]{1,0:T(8,128)(2,1)}, u32[]{:S(2)}, u32[]{:S(2)}) collective-permute-start(bf16[512,512]{1,0:T(8,128)(2,1)S(1)} %collective-permute-done.10.refs_4_), channel_id=1, source_target_pairs={{0,112},{16,0},{32,16},{48,32},{64,48},{80,64},{96,80},{112,96},{1... | collective-permute-start | bytes 1572872 | tf_op jit(solution)/shard_map/ppermute | solution.py:34
  108.9 5.1 %collective-permute-start.16 = (bf16[512,512]{1,0:T(8,128)(2,1)S(1)}, bf16[512,512]{1,0:T(8,128)(2,1)}, u32[]{:S(2)}, u32[]{:S(2)}) collective-permute-start(bf16[512,512]{1,0:T(8,128)(2,1)S(1)} %collective-permute-done.15.refs_10_), channel_id=1, source_target_pairs={{0,2},{2,4},{4,6},{6,8},{8,10},{10,12},{12,14},{14,0},{1,3},{3,5},... | collective-permute-start | bytes 1572872 | tf_op jit(solution)/shard_map/ppermute | solution.py:34
  114.0 5.1 %collective-permute-start.12 = (bf16[512,512]{1,0:T(8,128)(2,1)}, bf16[512,512]{1,0:T(8,128)(2,1)}, u32[]{:S(2)}, u32[]{:S(2)}) collective-permute-start(bf16[512,512]{1,0:T(8,128)(2,1)} %collective-permute-done.11.refs_5_), channel_id=1, source_target_pairs={{0,112},{16,0},{32,16},{48,32},{64,48},{80,64},{96,80},{112,96},{1... | collective-permute-start | bytes 1572872 | tf_op jit(solution)/shard_map/ppermute | solution.py:34
  123.0 5.3 %collective-permute-start.20 = (bf16[512,512]{1,0:T(8,128)(2,1)}, bf16[512,512]{1,0:T(8,128)(2,1)}, u32[]{:S(2)}, u32[]{:S(2)}) collective-permute-start(bf16[512,512]{1,0:T(8,128)(2,1)} %collective-permute-done.16.refs_11_), channel_id=1, source_target_pairs={{0,2},{2,4},{4,6},{6,8},{8,10},{10,12},{12,14},{14,0},{1,3},{3,5},... | collective-permute-start | bytes 1572872 | tf_op jit(solution)/shard_map/ppermute | solution.py:34
  129.0 2.7 %collective-permute-done.19.refs_14_ = bf16[512,512]{1,0:T(8,128)(2,1)} collective-permute-done((bf16[512,512]{1,0:T(8,128)(2,1)}, bf16[512,512]{1,0:T(8,128)(2,1)}, u32[]{:S(2)}, u32[]{:S(2)}) %collective-permute-start.19) | collective-permute-done | bytes 524320 | tf_op jit(solution)/shard_map/ppermute | solution.py:34
  131.7 3.2 %collective-permute-done.13.refs_7_ = bf16[512,512]{1,0:T(8,128)(2,1)} collective-permute-done((bf16[512,512]{1,0:T(8,128)(2,1)}, bf16[512,512]{1,0:T(8,128)(2,1)}, u32[]{:S(2)}, u32[]{:S(2)}) %collective-permute-start.13) | collective-permute-done | bytes 524320 | tf_op jit(solution)/shard_map/ppermute | solution.py:34
  136.5 10.2 %join.1.own_ref = bf16[1024,4096]{1,0:T(8,128)(2,1)} custom-call(s32[5]{0:T(128)} %stack.23.where.pos, bf16[512,512]{1,0:T(8,128)(2,1)} %copy-done.2, bf16[512,512]{1,0:T(8,128)(2,1)} %copy-done.4, bf16[512,512]{1,0:T(8,128)(2,1)} %copy-done.8, bf16[512,512]{1,0:T(8,128)(2,1)} %collective-permute-done.9.refs_3_, bf16[512,512]{1,0:T(8,128)(2,1)} %copy-done.6, ...), custom_call_target="tpu_custom_call" | custom-call | tf_op jit(solution)/shard_map/join/pallas_call | solution.py:174
  148.6 2.7 pick.1
  152.3 4.1 %collective-permute-start.6 = (bf16[144,144]{1,0:T(8,128)(2,1)S(1)}, bf16[144,144]{1,0:T(8,128)(2,1)S(1)}, u32[]{:S(2)}, u32[]{:S(2)}) collective-permute-start(bf16[144,144]{1,0:T(8,128)(2,1)S(1)} %reshape.32.raw_ref), channel_id=1, source_target_pairs={{256,1},{257,0},{258,3},{259,2},{260,5},{261,4},{262,7},{263,6},{2... | collective-permute-start | bytes 124424 | tf_op jit(solution)/shard_map/ppermute | solution.py:378
  158.4 3.7 %collective-permute-done.21.other_ref = bf16[1024,4096]{1,0:T(8,128)(2,1)} collective-permute-done((bf16[1024,4096]{1,0:T(8,128)(2,1)}, bf16[1024,4096]{1,0:T(8,128)(2,1)}, u32[]{:S(2)}, u32[]{:S(2)}) %collective-permute-start.21) | collective-permute-done | bytes 8388640 | tf_op jit(solution)/shard_map/ppermute | solution.py:39
  162.1 12.8 %early.1 = bf16[288,1024]{1,0:T(8,128)(2,1)} custom-call(s32[5]{0:T(128)} %stack.23.where.pos, s32[128]{0:T(128)} %bands.9, s32[128]{0:T(128)} %broadcast_select_fusion.table, bf16[144,144]{1,0:T(8,128)(2,1)} %copy-done.10, bf16[144,144]{1,0:T(8,128)(2,1)} %copy-done.12, bf16[144,1024]{1,0:T(8,128)(2,1)} %embed_ref.1, bf16[2,1024]{1,0:T(2,128)(2,1)} %level_ref.1, ...), custom_call_target="tpu_custom_call" | custom-call | tf_op jit(solution)/shard_map/early/pallas_call | solution.py:353
  177.5 14.9 %collective-permute-done.22.came_ref = bf16[288,1024]{1,0:T(8,128)(2,1)S(1)} collective-permute-done((bf16[288,1024]{1,0:T(8,128)(2,1)}, bf16[288,1024]{1,0:T(8,128)(2,1)S(1)}, u32[]{:S(2)}, u32[]{:S(2)}) %collective-permute-start.22) | collective-permute-done | bytes 589856 | tf_op jit(solution)/shard_map/ppermute | solution.py:378
  193.3 13.4 %late.1 = (bf16[2,144,144]{2,1,0:T(8,128)(2,1)}, bf16[144,144]{1,0:T(8,128)(2,1)}, bf16[144,144]{1,0:T(8,128)(2,1)}) custom-call(s32[5]{0:T(128)} %stack.23.where.pos, s32[128]{0:T(128)} %bands.9, s32[128]{0:T(128)} %broadcast_select_fusion.table, bf16[288,1024]{1,0:T(8,128)(2,1)} %copy-done.3, f32[2,1024]{1,0:T(2,128)} %bitcast.45, ...), custom_call_target="tpu_custom_call" | custom-call | tf_op jit(solution)/shard_map/late/pallas_call | solution.py:353
  208.2 5.0 %collective-permute-start.24 = (bf16[144,144]{1,0:T(8,128)(2,1)}, bf16[144,144]{1,0:T(8,128)(2,1)S(1)}, u32[]{:S(2)}, u32[]{:S(2)}) collective-permute-start(bf16[144,144]{1,0:T(8,128)(2,1)} %get-tuple-element.19), channel_id=1, source_target_pairs={{0,1},{1,0},{2,3},{3,2},{4,5},{5,4},{6,7},{7,6},{8,9},{9,8},{10,11... | collective-permute-start | bytes 124424 | tf_op jit(solution)/shard_map/ppermute | solution.py:39
  213.3 2.5 collective-permute-done.24
  218.2 2.4 unpick.1
  220.6 42.4 %all_to_all.10.came_ref = bf16[256,16,128]{2,1,0:T(8,128)(2,1)} all-to-all(bf16[256,16,128]{2,1,0:T(8,128)(2,1)} %unpick.1), channel_id=1, replica_groups=mesh['xh'=2,'c'=2,'z'=8,'y'=8,'xl'=2] {'z','y','xl'}, dimensions={0} | all-to-all | bytes 2097152 | tf_op jit(solution)/shard_map/all_to_all | solution.py:424
  263.0 2.9 %unpack.1 = bf16[15,16,128]{2,1,0:T(8,128)(2,1)} custom-call(s32[5]{0:T(128)} %stack.23.where.pos, s32[128]{0:T(128)} %bands.9, s32[128]{0:T(128)} %broadcast_select_fusion.table, bf16[256,16,128]{2,1,0:T(8,128)(2,1)} %all_to_all.10.came_ref), custom_call_target="tpu_custom_call" | custom-call | tf_op jit(solution)/shard_map/unpack/pallas_call | solution.py:368
  (91 shorter events, 43.0 us)
Async XLA Ops:
  6.2 70.3 %all-to-all-start = ((bf16[256,16,128]{2,1,0:T(8,128)(2,1)}), bf16[256,16,128]{2,1,0:T(8,128)(2,1)S(1)}, u32[]{:S(2)}, u32[]{:S(2)}) async-start(bf16[256,16,128]{2,1,0:T(8,128)(2,1)} %pack.1), calls=%async_computation | async-start | bytes 2097152 | tf_op jit(solution)/shard_map/all_to_all | solution.py:394
  33.3 17.4 %collective-permute-start.3 = (bf16[64,512]{1,0:T(8,128)(2,1)S(1)}, bf16[64,512]{1,0:T(8,128)(2,1)S(1)}, u32[]{:S(2)}, u32[]{:S(2)}) collective-permute-start(bf16[64,512]{1,0:T(8,128)(2,1)S(1)} %get-tuple-element.26), channel_id=1, source_target_pairs={{0,64},{16,80},{32,96},{48,112},{64,0},{80,16},{96,32},{112,48},{1... | collective-permute-start | bytes 196616 | tf_op jit(solution)/shard_map/ppermute | solution.py:39
  40.8 17.2 %collective-permute-start = (bf16[64,512]{1,0:T(8,128)(2,1)S(1)}, bf16[64,512]{1,0:T(8,128)(2,1)S(1)}, u32[]{:S(2)}, u32[]{:S(2)}) collective-permute-start(bf16[64,512]{1,0:T(8,128)(2,1)S(1)} %get-tuple-element.27), channel_id=1, source_target_pairs={{0,8},{2,10},{4,12},{6,14},{8,0},{10,2},{12,4},{14,6},{1,9},{3,11}... | collective-permute-start | bytes 196616 | tf_op jit(solution)/shard_map/ppermute | solution.py:39
  50.7 13.0 %collective-permute-start.4 = (bf16[128,512]{1,0:T(8,128)(2,1)S(1)}, bf16[128,512]{1,0:T(8,128)(2,1)S(1)}, u32[]{:S(2)}, u32[]{:S(2)}) collective-permute-start(bf16[128,512]{1,0:T(8,128)(2,1)S(1)} %pad_maximum_fusion.5), channel_id=1, source_target_pairs={{0,32},{16,48},{32,0},{48,16},{64,96},{80,112},{96,64},{112,80},{1... | collective-permute-start | bytes 393224 | tf_op jit(solution)/shard_map/ppermute | solution.py:39
  58.0 8.6 %collective-permute-start.1 = (bf16[128,512]{1,0:T(8,128)(2,1)S(1)}, bf16[128,512]{1,0:T(8,128)(2,1)S(1)}, u32[]{:S(2)}, u32[]{:S(2)}) collective-permute-start(bf16[128,512]{1,0:T(8,128)(2,1)S(1)} %pad_maximum_fusion.4), channel_id=1, source_target_pairs={{0,4},{2,6},{4,0},{6,2},{8,12},{10,14},{12,8},{14,10},{1,5},{3,7},... | collective-permute-start | bytes 393224 | tf_op jit(solution)/shard_map/ppermute | solution.py:39
  63.7 8.3 %collective-permute-start.5 = (bf16[256,512]{1,0:T(8,128)(2,1)S(1)}, bf16[256,512]{1,0:T(8,128)(2,1)S(1)}, u32[]{:S(2)}, u32[]{:S(2)}) collective-permute-start(bf16[256,512]{1,0:T(8,128)(2,1)S(1)} %pad_maximum_fusion.3), channel_id=1, source_target_pairs={{0,16},{16,0},{32,48},{48,32},{64,80},{80,64},{96,112},{112,96},{1... | collective-permute-start | bytes 786440 | tf_op jit(solution)/shard_map/ppermute | solution.py:39
  66.6 9.9 %collective-permute-start.2 = (bf16[256,512]{1,0:T(8,128)(2,1)S(1)}, bf16[256,512]{1,0:T(8,128)(2,1)S(1)}, u32[]{:S(2)}, u32[]{:S(2)}) collective-permute-start(bf16[256,512]{1,0:T(8,128)(2,1)S(1)} %pad_maximum_fusion.2), channel_id=1, source_target_pairs={{0,2},{2,0},{4,6},{6,4},{8,10},{10,8},{12,14},{14,12},{1,3},{3,1},... | collective-permute-start | bytes 786440 | tf_op jit(solution)/shard_map/ppermute | solution.py:39
  72.0 64.4 %copy-start.1 = (bf16[512,512]{1,0:T(8,128)(2,1)}, bf16[512,512]{1,0:T(8,128)(2,1)S(1)}, u32[]{:S(2)}) copy-start(bf16[512,512]{1,0:T(8,128)(2,1)S(1)} %pad_maximum_fusion.1.refs_8_) | copy-start | bytes 1572868
  76.5 59.9 %copy-start.2 = (bf16[512,512]{1,0:T(8,128)(2,1)}, bf16[512,512]{1,0:T(8,128)(2,1)S(1)}, u32[]{:S(2)}) copy-start(bf16[512,512]{1,0:T(8,128)(2,1)S(1)} %pad_maximum_fusion.refs_0_) | copy-start | bytes 1572868
  76.5 70.1 %copy-start = (bf16[256,16,128]{2,1,0:T(8,128)(2,1)}, bf16[256,16,128]{2,1,0:T(8,128)(2,1)S(1)}, u32[]{:S(2)}) copy-start(bf16[256,16,128]{2,1,0:T(8,128)(2,1)S(1)} %all-to-all-done.came_ref) | copy-start | bytes 3145732
  76.6 15.6 %collective-permute-start.7 = (bf16[512,512]{1,0:T(8,128)(2,1)S(1)}, bf16[512,512]{1,0:T(8,128)(2,1)S(1)}, u32[]{:S(2)}, u32[]{:S(2)}) collective-permute-start(bf16[512,512]{1,0:T(8,128)(2,1)S(1)} %pad_maximum_fusion.refs_0_), channel_id=1, source_target_pairs={{0,16},{16,32},{32,48},{48,64},{64,80},{80,96},{96,112},{112,0},{1... | collective-permute-start | bytes 1572872 | tf_op jit(solution)/shard_map/ppermute | solution.py:34
  79.9 14.6 %collective-permute-start.14 = (bf16[512,512]{1,0:T(8,128)(2,1)S(1)}, bf16[512,512]{1,0:T(8,128)(2,1)S(1)}, u32[]{:S(2)}, u32[]{:S(2)}) collective-permute-start(bf16[512,512]{1,0:T(8,128)(2,1)S(1)} %pad_maximum_fusion.1.refs_8_), channel_id=1, source_target_pairs={{0,2},{2,4},{4,6},{6,8},{8,10},{10,12},{12,14},{14,0},{1,3},{3,5},... | collective-permute-start | bytes 1572872 | tf_op jit(solution)/shard_map/ppermute | solution.py:34
  83.7 15.0 %collective-permute-start.10 = (bf16[512,512]{1,0:T(8,128)(2,1)S(1)}, bf16[512,512]{1,0:T(8,128)(2,1)S(1)}, u32[]{:S(2)}, u32[]{:S(2)}) collective-permute-start(bf16[512,512]{1,0:T(8,128)(2,1)S(1)} %pad_maximum_fusion.refs_0_), channel_id=1, source_target_pairs={{0,112},{16,0},{32,16},{48,32},{64,48},{80,64},{96,80},{112,96},{1... | collective-permute-start | bytes 1572872 | tf_op jit(solution)/shard_map/ppermute | solution.py:34
  87.7 16.2 %collective-permute-start.17 = (bf16[512,512]{1,0:T(8,128)(2,1)S(1)}, bf16[512,512]{1,0:T(8,128)(2,1)S(1)}, u32[]{:S(2)}, u32[]{:S(2)}) collective-permute-start(bf16[512,512]{1,0:T(8,128)(2,1)S(1)} %pad_maximum_fusion.1.refs_8_), channel_id=1, source_target_pairs={{0,14},{2,0},{4,2},{6,4},{8,6},{10,8},{12,10},{14,12},{1,15},{3,1}... | collective-permute-start | bytes 1572872 | tf_op jit(solution)/shard_map/ppermute | solution.py:34
  92.2 44.3 %copy-start.4 = (bf16[512,512]{1,0:T(8,128)(2,1)}, bf16[512,512]{1,0:T(8,128)(2,1)S(1)}, u32[]{:S(2)}) copy-start(bf16[512,512]{1,0:T(8,128)(2,1)S(1)} %collective-permute-done.7.refs_1_) | copy-start | bytes 1572868
  92.2 14.7 %collective-permute-start.8 = (bf16[512,512]{1,0:T(8,128)(2,1)S(1)}, bf16[512,512]{1,0:T(8,128)(2,1)S(1)}, u32[]{:S(2)}, u32[]{:S(2)}) collective-permute-start(bf16[512,512]{1,0:T(8,128)(2,1)S(1)} %collective-permute-done.7.refs_1_), channel_id=1, source_target_pairs={{0,16},{16,32},{32,48},{48,64},{64,80},{80,96},{96,112},{112,0},{1... | collective-permute-start | bytes 1572872 | tf_op jit(solution)/shard_map/ppermute | solution.py:34
  94.5 42.0 %copy-start.5 = (bf16[512,512]{1,0:T(8,128)(2,1)}, bf16[512,512]{1,0:T(8,128)(2,1)S(1)}, u32[]{:S(2)}) copy-start(bf16[512,512]{1,0:T(8,128)(2,1)S(1)} %collective-permute-done.14.refs_9_) | copy-start | bytes 1572868
  94.5 14.4 %collective-permute-start.15 = (bf16[512,512]{1,0:T(8,128)(2,1)S(1)}, bf16[512,512]{1,0:T(8,128)(2,1)S(1)}, u32[]{:S(2)}, u32[]{:S(2)}) collective-permute-start(bf16[512,512]{1,0:T(8,128)(2,1)S(1)} %collective-permute-done.14.refs_9_), channel_id=1, source_target_pairs={{0,2},{2,4},{4,6},{6,8},{8,10},{10,12},{12,14},{14,0},{1,3},{3,5},... | collective-permute-start | bytes 1572872 | tf_op jit(solution)/shard_map/ppermute | solution.py:34
  98.8 15.2 %collective-permute-start.11 = (bf16[512,512]{1,0:T(8,128)(2,1)S(1)}, bf16[512,512]{1,0:T(8,128)(2,1)}, u32[]{:S(2)}, u32[]{:S(2)}) collective-permute-start(bf16[512,512]{1,0:T(8,128)(2,1)S(1)} %collective-permute-done.10.refs_4_), channel_id=1, source_target_pairs={{0,112},{16,0},{32,16},{48,32},{64,48},{80,64},{96,80},{112,96},{1... | collective-permute-start | bytes 1572872 | tf_op jit(solution)/shard_map/ppermute | solution.py:34
  103.9 15.2 %collective-permute-start.18 = (bf16[512,512]{1,0:T(8,128)(2,1)S(1)}, bf16[512,512]{1,0:T(8,128)(2,1)}, u32[]{:S(2)}, u32[]{:S(2)}) collective-permute-start(bf16[512,512]{1,0:T(8,128)(2,1)S(1)} %collective-permute-done.17.refs_12_), channel_id=1, source_target_pairs={{0,14},{2,0},{4,2},{6,4},{8,6},{10,8},{12,10},{14,12},{1,15},{3,1}... | collective-permute-start | bytes 1572872 | tf_op jit(solution)/shard_map/ppermute | solution.py:34
  106.9 14.2 %collective-permute-start.9 = (bf16[512,512]{1,0:T(8,128)(2,1)S(1)}, bf16[512,512]{1,0:T(8,128)(2,1)}, u32[]{:S(2)}, u32[]{:S(2)}) collective-permute-start(bf16[512,512]{1,0:T(8,128)(2,1)S(1)} %collective-permute-done.8.refs_2_), channel_id=1, source_target_pairs={{0,16},{16,32},{32,48},{48,64},{64,80},{80,96},{96,112},{112,0},{1... | collective-permute-start | bytes 1572872 | tf_op jit(solution)/shard_map/ppermute | solution.py:34
  108.9 14.2 %collective-permute-start.16 = (bf16[512,512]{1,0:T(8,128)(2,1)S(1)}, bf16[512,512]{1,0:T(8,128)(2,1)}, u32[]{:S(2)}, u32[]{:S(2)}) collective-permute-start(bf16[512,512]{1,0:T(8,128)(2,1)S(1)} %collective-permute-done.15.refs_10_), channel_id=1, source_target_pairs={{0,2},{2,4},{4,6},{6,8},{8,10},{10,12},{12,14},{14,0},{1,3},{3,5},... | collective-permute-start | bytes 1572872 | tf_op jit(solution)/shard_map/ppermute | solution.py:34
  114.0 15.0 %collective-permute-start.12 = (bf16[512,512]{1,0:T(8,128)(2,1)}, bf16[512,512]{1,0:T(8,128)(2,1)}, u32[]{:S(2)}, u32[]{:S(2)}) collective-permute-start(bf16[512,512]{1,0:T(8,128)(2,1)} %collective-permute-done.11.refs_5_), channel_id=1, source_target_pairs={{0,112},{16,0},{32,16},{48,32},{64,48},{80,64},{96,80},{112,96},{1... | collective-permute-start | bytes 1572872 | tf_op jit(solution)/shard_map/ppermute | solution.py:34
  119.2 12.6 %collective-permute-start.19 = (bf16[512,512]{1,0:T(8,128)(2,1)}, bf16[512,512]{1,0:T(8,128)(2,1)}, u32[]{:S(2)}, u32[]{:S(2)}) collective-permute-start(bf16[512,512]{1,0:T(8,128)(2,1)} %collective-permute-done.18.refs_13_), channel_id=1, source_target_pairs={{0,14},{2,0},{4,2},{6,4},{8,6},{10,8},{12,10},{14,12},{1,15},{3,1}... | collective-permute-start | bytes 1572872 | tf_op jit(solution)/shard_map/ppermute | solution.py:34
  121.1 13.8 %collective-permute-start.13 = (bf16[512,512]{1,0:T(8,128)(2,1)}, bf16[512,512]{1,0:T(8,128)(2,1)}, u32[]{:S(2)}, u32[]{:S(2)}) collective-permute-start(bf16[512,512]{1,0:T(8,128)(2,1)} %collective-permute-done.9.refs_3_), channel_id=1, source_target_pairs={{0,16},{16,32},{32,48},{48,64},{64,80},{80,96},{96,112},{112,0},{1... | collective-permute-start | bytes 1572872 | tf_op jit(solution)/shard_map/ppermute | solution.py:34
  123.0 13.4 %collective-permute-start.20 = (bf16[512,512]{1,0:T(8,128)(2,1)}, bf16[512,512]{1,0:T(8,128)(2,1)}, u32[]{:S(2)}, u32[]{:S(2)}) collective-permute-start(bf16[512,512]{1,0:T(8,128)(2,1)} %collective-permute-done.16.refs_11_), channel_id=1, source_target_pairs={{0,2},{2,4},{4,6},{6,8},{8,10},{10,12},{12,14},{14,0},{1,3},{3,5},... | collective-permute-start | bytes 1572872 | tf_op jit(solution)/shard_map/ppermute | solution.py:34
  146.7 15.4 %collective-permute-start.21 = (bf16[1024,4096]{1,0:T(8,128)(2,1)}, bf16[1024,4096]{1,0:T(8,128)(2,1)}, u32[]{:S(2)}, u32[]{:S(2)}) collective-permute-start(bf16[1024,4096]{1,0:T(8,128)(2,1)} %join.1.own_ref), channel_id=1, source_target_pairs={{0,128},{128,0},{1,129},{129,1},{2,130},{130,2},{3,131},{131,3},{4... | collective-permute-start | bytes 25165832 | tf_op jit(solution)/shard_map/ppermute | solution.py:39
  152.3 24.2 %copy-start.11 = (bf16[1024,144]{0,1:T(8,128)(2,1)S(1)}, bf16[1024,144]{0,1:T(8,128)(2,1)}, u32[]{:S(2)}) copy-start(bf16[1024,144]{0,1:T(8,128)(2,1)} %param.15) | copy-start | bytes 884740
  152.3 6.1 %collective-permute-start.6 = (bf16[144,144]{1,0:T(8,128)(2,1)S(1)}, bf16[144,144]{1,0:T(8,128)(2,1)S(1)}, u32[]{:S(2)}, u32[]{:S(2)}) collective-permute-start(bf16[144,144]{1,0:T(8,128)(2,1)S(1)} %reshape.32.raw_ref), channel_id=1, source_target_pairs={{256,1},{257,0},{258,3},{259,2},{260,5},{261,4},{262,7},{263,6},{2... | collective-permute-start | bytes 124424 | tf_op jit(solution)/shard_map/ppermute | solution.py:378
  175.0 17.5 %collective-permute-start.22 = (bf16[288,1024]{1,0:T(8,128)(2,1)}, bf16[288,1024]{1,0:T(8,128)(2,1)S(1)}, u32[]{:S(2)}, u32[]{:S(2)}) collective-permute-start(bf16[288,1024]{1,0:T(8,128)(2,1)} %early.1), channel_id=1, source_target_pairs={{0,257},{1,256},{2,259},{3,258},{4,261},{5,260},{6,263},{7,262},{8... | collective-permute-start | bytes 1769480 | tf_op jit(solution)/shard_map/ppermute | solution.py:378
  206.7 9.2 %collective-permute-start.23 = (bf16[2,144,144]{2,1,0:T(8,128)(2,1)}, bf16[2,144,144]{2,1,0:T(8,128)(2,1)S(1)}, u32[]{:S(2)}, u32[]{:S(2)}) collective-permute-start(bf16[2,144,144]{2,1,0:T(8,128)(2,1)} %get-tuple-element.18), channel_id=1, source_target_pairs={{256,1},{257,0},{258,3},{259,2},{260,5},{261,4},{262,7},{263,6},{2... | collective-permute-start | bytes 248840 | tf_op jit(solution)/shard_map/ppermute | solution.py:378
  208.2 7.6 %collective-permute-start.24 = (bf16[144,144]{1,0:T(8,128)(2,1)}, bf16[144,144]{1,0:T(8,128)(2,1)S(1)}, u32[]{:S(2)}, u32[]{:S(2)}) collective-permute-start(bf16[144,144]{1,0:T(8,128)(2,1)} %get-tuple-element.19), channel_id=1, source_target_pairs={{0,1},{1,0},{2,3},{3,2},{4,5},{5,4},{6,7},{7,6},{8,9},{9,8},{10,11... | collective-permute-start | bytes 124424 | tf_op jit(solution)/shard_map/ppermute | solution.py:39
  (7 other events, 59.0 us)
where the time goes:
time: 269 us; the launch traced here: 268 us
  starting transfers between devices  111 us (41%)
  blocking collectives  50.8 us (19%)
  Pallas kernels  46.7 us (17%)
  waiting for transfers between devices  46.1 us (17%)
  local copies, waits for them, and re-layouts  9.51 us (4%)
    ppermute x14, starting transfers between devices, ring(): return lax.ppermute(value, axis, [(i, (i + by) % n) for i in range(n)])  47.9 us
    all_to_all x1, blocking collectives, per_device(): came_back = lax.all_to_all(reply, LAT, 0, 0, tiled=True)  42.4 us
    ppermute x8, starting transfers between devices, swap(): return lax.ppermute(value, axis, [(i, i ^ bit) for i in range(n)])  38 us
    pallas_call x2, Pallas kernels, sections_call(): pl.pallas_call(body, out_shape=tuple((jax.ShapeDtypeStruct(shape, BF) for...  26.2 us
    ppermute x8, waiting for transfers between devices, swap(): return lax.ppermute(value, axis, [(i, i ^ bit) for i in range(n)])  18.2 us
    all_to_all x1, starting transfers between devices, per_device(): arrived = lax.all_to_all(message, LAT, 0, 0, tiled=True)  18 us
    ppermute x3, waiting for transfers between devices, crossed(): return lax.ppermute(value, ('xh', 'xl'), [(x, 3 - x) for x in sources])  16.9 us
    ppermute x14, waiting for transfers between devices, ring(): return lax.ppermute(value, axis, [(i, (i + by) % n) for i in range(n)])  11.1 us
  transfers between devices with their start and end apart: 26, of which 15 were waited for; matrix products, arithmetic and copies ran while one was open for 1% of the time, Pallas kernels for 1%

commit v1 on v0

--- a/solution.py
+++ b/solution.py
@@ -116,50 +116,59 @@
 
 
 def join_kernel(pos, *refs):
-    out_ref, out, turned, sem = refs[-4:]
-    pieces = refs[:-4]
+    out_ref, held, turned, sems, sent = refs[-5:]
+    pieces = refs[:-5]
     half = len(pieces) // 2
     z, y = pos[1], pos[2]
+    steps = (0, -1, -2, -3, 1, 2, 3, 4)
 
     def copies(side, index):
         ref = pieces[side * half + index]
-        step = (0, -1, -2, -3, 1, 2, 3, 4)[index]
-        for slot, sub in enumerate(range(8)):
+        for sub in range(8):
             if side == 0:
-                plane, line = lax.rem(z + step + 8, 8), y ^ OFFS[sub]
+                plane, line = lax.rem(z + steps[index] + 8, 8), y ^ OFFS[sub]
             else:
-                plane, line = z ^ OFFS[sub], lax.rem(y + step + 8, 8)
+                plane, line = z ^ OFFS[sub], lax.rem(y + steps[index] + 8, 8)
             row = pl.multiple_of((plane * 8 + line) * 64, 64)
             yield pltpu.make_async_copy(
-                ref.at[pl.ds(slot * 64, 64)], out.at[side, pl.ds(row, 64)], sem
+                ref.at[pl.ds(sub * 64, 64)], held.at[side, pl.ds(row, 64)], sems.at[side, index]
             )
 
-    every = [c for side in range(2) for i in range(half) for c in copies(side, i)]
-    for c in every:
-        c.start()
-    for c in every:
+    def turn(side, plane):
+        columns = pl.ds(pl.multiple_of(plane * 512, 512), 512)
+        here = (slice(512 * side, 512 * (side + 1)), columns)
+        turned[here] = held[side, columns, :].T
+        copy = pltpu.make_async_copy(turned.at[here], out_ref.at[here], sent)
+        copy.start()
+        return copy
+
+    every = [[list(copies(side, index)) for index in range(half)] for side in range(2)]
+    for side in range(2):
+        for group in every[side]:
+            for c in group:
+                c.start()
+    leaving = []
+    for index in range(half):
+        for c in every[0][index]:
+            c.wait()
+        leaving.append(turn(0, lax.rem(z + steps[index] + 8, 8)))
+    for group in every[1]:
+        for c in group:
+            c.wait()
+    for plane in range(8):
+        leaving.append(turn(1, plane))
+    for c in leaving:
         c.wait()
 
-    @pl.loop(0, 8)
-    def _(plane):
-        lanes = pl.ds(pl.multiple_of(plane * 512, 512), 512)
-        for side in range(2):
-            turned[512 * side : 512 * (side + 1), lanes] = out[side, lanes, :].T
-
-    back = pltpu.make_async_copy(turned, out_ref, sem)
-    back.start()
-    back.wait()
-
-
-def gather_section(weight, pos, message, arrived, gains):
-    mine, _ = lax.optimization_barrier((weight[0].T, message))
+
+def gather_section(weight, pos, message, gains):
+    mine = weight[0].T
     pair = lax.all_gather(mine, "xl", axis=0, tiled=True)
     pair, gains = lax.optimization_barrier((pair, gains))
     a, b = pair[:, :512], pair[:, 512:]
     for bit in DOUBLING:
         a_far, b_far = swap(a, "y", bit), swap(b, "z", bit)
         a, b = jnp.concatenate([a, a_far]), jnp.concatenate([b, b_far])
-    a, b, arrived = lax.optimization_barrier((a, b, arrived))
     chains = [("z", 1), ("z", -1), ("y", 1), ("y", -1)]
     got = [[] for _ in chains]
     held = [a, a, b, b]
@@ -168,6 +177,9 @@
             if step < 3 or by > 0:
                 held[n] = ring(held[n], axis, by)
                 got[n].append(held[n])
+    *lasts, message = lax.optimization_barrier((*[g[-1] for g in got], message))
+    for g, last in zip(got, lasts):
+        g[-1] = last
     pieces = []
     for own, ahead, behind in ((a, got[0], got[1]), (b, got[2], got[3])):
         pieces += [own, *ahead[:3], *behind, ahead[3]]
@@ -179,12 +191,14 @@
         scratch_shapes=[
             pltpu.VMEM((2, 4096, 512), BF),
             pltpu.VMEM((1024, 4096), BF),
+            pltpu.SemaphoreType.DMA((2, 8)),
             pltpu.SemaphoreType.DMA(()),
         ],
         compiler_params=pltpu.CompilerParams(vmem_limit_bytes=60 * MIB),
+        cost_estimate=pl.CostEstimate(flops=10**10, bytes_accessed=3 << 23, transcendentals=0),
         name="join",
     )(pos, *pieces)
-    return section, arrived, gains
+    return section, message, gains
 
 
 def matmul_t(left, right):
@@ -303,7 +317,7 @@
 
 
 def early_kernel(
-    pos, bands, table, raw_ref, far_ref, embed_ref, level_ref, gain_ref, own_ref, other_ref,
+    pos, bands, table, raw_ref, embed_ref, level_ref, gain_ref, own_ref, other_ref,
     hidden_ref, weights, sems,
 ):
     first, second = projections(pos, own_ref, other_ref, weights, sems)
@@ -313,23 +327,21 @@
     to_window = (lax.div(to_token, half) == lax.rem(from_token, LEV)) & (
         lax.rem(to_token, half) == lax.div(from_token, LEV)
     )
-    to_window = to_window.astype(BF)
-    raws = [jnp.dot(to_window, ref[...], preferred_element_type=F32) for ref in (raw_ref, far_ref)]
-    raw = jnp.concatenate(raws, axis=0).astype(BF)
-    token = lax.broadcasted_iota(jnp.int32, (2 * WTOK, 1), 0)
-    upper = lax.rem(token, WTOK) < half
+    raw = jnp.dot(to_window.astype(BF), raw_ref[...], preferred_element_type=F32).astype(BF)
+    upper = lax.broadcasted_iota(jnp.int32, (WTOK, 1), 0) < half
     level_rows = jnp.where(upper, level_ref[0:1].astype(F32), level_ref[1:2].astype(F32))
-    hidden = (jnp.dot(raw, embed_ref[...], preferred_element_type=F32) + level_rows).astype(BF)
-    hidden = column_block(hidden, gain_ref[0:1], first)
+    embedded = (jnp.dot(raw, embed_ref[...], preferred_element_type=F32) + level_rows).astype(BF)
+    hidden = column_block(embedded, gain_ref[0:1], first)
     hidden_ref[...] = window_block(hidden, gain_ref[1:2], second, key_bias(pos, bands, table))
 
 
 def late_kernel(
-    pos, bands, table, came_ref, gain_ref, head_ref, own_ref, other_ref,
+    pos, bands, table, came_ref, came_too_ref, gain_ref, head_ref, own_ref, other_ref,
     give_ref, out_ref, rows_ref, weights, sems,
 ):
     first, second = projections(pos, own_ref, other_ref, weights, sems)
-    hidden = window_block(came_ref[...], gain_ref[0:1], first, key_bias(pos, bands, table))
+    start = jnp.concatenate([came_ref[...], came_too_ref[...]], axis=0)
+    hidden = window_block(start, gain_ref[0:1], first, key_bias(pos, bands, table))
     hidden = column_block(hidden, gain_ref[1:2], second)
     result = jnp.dot(hidden, head_ref[...], preferred_element_type=F32)
     keep = inside(pos, bands, table, lax.broadcasted_iota(jnp.int32, (WTOK, 1), 0))
@@ -391,29 +403,31 @@
     scalars = (pos, band_rows, table)
 
     message = small_call(pack_kernel, 2 * lat_count, (table,), to_rows(fields[0]), "pack")
+    gains = lax.all_gather(norm_gain, "c", axis=0, tiled=True)
+    own, message, gains = gather_section(attn_weight, pos, message, gains)
     arrived = lax.all_to_all(message, LAT, 0, 0, tiled=True)
-    gains = lax.all_gather(norm_gain, "c", axis=0, tiled=True)
-    own, arrived, gains = gather_section(attn_weight, pos, message, arrived, gains)
+    other = swap(own, "c", 1)
     raw_rows = small_call(pick_kernel, WIN_ROWS + 1, scalars, arrived, "pick")
     own_raw = from_rows(raw_rows[:WIN_ROWS])
     far_raw = crossed(own_raw, (2, 3))
-    other = swap(own, "c", 1)
-
-    [hidden] = sections_call(
-        early_kernel,
-        [(2 * WTOK, width)],
-        scalars,
-        (own_raw, far_raw, embed_weight, level_embed, gains),
-        own,
-        other,
-        "early",
-    )
-    came = crossed(hidden, (0, 1))
+
+    came = []
+    for raw in (own_raw, far_raw):
+        [hidden] = sections_call(
+            early_kernel,
+            [(WTOK, width)],
+            scalars,
+            (raw, embed_weight, level_embed, gains),
+            own,
+            other,
+            "early",
+        )
+        came.append(crossed(hidden, (0, 1)))
     given, out, rows = sections_call(
         late_kernel,
         [(2, WTOK, FEAT), (WTOK, FEAT), (WTOK, FEAT)],
         scalars,
-        (came, gains, head_weight),
+        (*came, gains, head_weight),
         own,
         other,
         "late",

time: 269 us -> 264 us (0.981)
  blocking collectives: 50.8 us -> 83.8 us
  waiting for transfers between devices: 46.1 us -> 24.5 us
  starting transfers between devices: 111 us -> 91.8 us
  Pallas kernels: 46.7 us -> 49.6 us
    all_to_all x0 -> x1, blocking collectives: none -> 40.7 us  [per_device(): arrived = lax.all_to_all(message, LAT, 0, 0, tiled=True)]
    all_to_all x1 -> x0, starting transfers between devices: 18 us -> none  [per_device(): arrived = lax.all_to_all(message, LAT, 0, 0, tiled=True)]
    ppermute x8, waiting for transfers between devices: 18.2 us -> 6.61 us  [swap(): return lax.ppermute(value, axis, [(i, i ^ bit) for i in range(n)])]
    ppermute x3 -> x4, waiting for transfers between devices: 16.9 us -> 7.72 us  [crossed(): return lax.ppermute(value, ('xh', 'xl'), [(x, 3 - x) for x in sources])]
    all_to_all x1, blocking collectives: 42.4 us -> 36.1 us  [per_device(): came_back = lax.all_to_all(reply, LAT, 0, 0, tiled=True)]
    pallas_call x2 -> x3, Pallas kernels: 26.2 us -> 31.3 us  [sections_call(): pl.pallas_call(body, out_shape=tuple((jax.ShapeDtypeStruct(shape, BF) for...]
    ppermute x14, starting transfers between devices: 47.9 us -> 44.6 us  [ring(): return lax.ppermute(value, axis, [(i, (i + by) % n) for i in range(n)])]
    ppermute x3 -> x4, starting transfers between devices: 7.21 us -> 7.02 us  [crossed(): return lax.ppermute(value, ('xh', 'xl'), [(x, 3 - x) for x in sources])]
  transfers between devices with their start and end apart: 26 -> 26, of which waited for: 15 -> 14; matrix products, arithmetic and copies ran while one was open for 1% -> 2% of each run, Pallas kernels for 1% -> 9%
where the time goes in v1:
time: 264 us; the launch traced here: 263 us
  starting transfers between devices  91.8 us (35%)
  blocking collectives  83.8 us (32%)
  Pallas kernels  49.6 us (19%)
  waiting for transfers between devices  24.5 us (9%)
  local copies, waits for them, and re-layouts  9.97 us (4%)
    ppermute x14, starting transfers between devices, ring(): return lax.ppermute(value, axis, [(i, (i + by) % n) for i in range(n)])  44.6 us
    all_to_all x1, blocking collectives, per_device(): arrived = lax.all_to_all(message, LAT, 0, 0, tiled=True)  40.7 us
    ppermute x8, starting transfers between devices, swap(): return lax.ppermute(value, axis, [(i, i ^ bit) for i in range(n)])  40.2 us
    all_to_all x1, blocking collectives, per_device(): came_back = lax.all_to_all(reply, LAT, 0, 0, tiled=True)  36.1 us
    pallas_call x3, Pallas kernels, sections_call(): pl.pallas_call(body, out_shape=tuple((jax.ShapeDtypeStruct(shape, BF) for...  31.3 us
    pallas_call x4, Pallas kernels, small_call(): pl.pallas_call(body, out_shape=jax.ShapeDtypeStruct((out_rows, PACK, 128)...  10.2 us
    ppermute x14, waiting for transfers between devices, ring(): return lax.ppermute(value, axis, [(i, (i + by) % n) for i in range(n)])  10.1 us
    pallas_call x1, Pallas kernels, gather_section(): pl.pallas_call(join_kernel, out_shape=jax.ShapeDtypeStruct((1024, 4096),...  8.13 us
  transfers between devices with their start and end apart: 26, of which 14 were waited for; matrix products, arithmetic and copies ran while one was open for 2% of the time, Pallas kernels for 9%

profile of v1, /device:TPU:12, one launch (start us, length us, event | category | flops | bytes accessed | tf_op | source)
XLA Modules:
  0.0 263.0 jit_solution(12252773024782969784)
XLA Ops:
  0.6 5.2 %all_gather.6 = bf16[64,1024]{1,0:T(8,128)(2,1)S(1)} all-gather(bf16[32,1024]{1,0:T(8,128)(2,1)} %bitcast.47), channel_id=1, replica_groups=mesh['xh'=2,'c'=2,'z'=8,'y'=8,'xl'=2] {'xl'}, dimensions={0}, use_global_device_ids=true | all-gather | bytes 196608 | tf_op jit(solution)/shard_map/all_gather | solution.py:166
  8.3 6.8 %collective-permute-start = (bf16[64,512]{1,0:T(8,128)(2,1)S(1)}, bf16[64,512]{1,0:T(8,128)(2,1)S(1)}, u32[]{:S(2)}, u32[]{:S(2)}) collective-permute-start(bf16[64,512]{1,0:T(8,128)(2,1)S(1)} %get-tuple-element.29), channel_id=1, source_target_pairs={{0,8},{2,10},{4,12},{6,14},{8,0},{10,2},{12,4},{14,6},{1,9},{3,11}... | collective-permute-start | bytes 196616 | tf_op jit(solution)/shard_map/ppermute | solution.py:39
  15.2 10.9 %collective-permute-start.10 = (bf16[64,512]{1,0:T(8,128)(2,1)S(1)}, bf16[64,512]{1,0:T(8,128)(2,1)S(1)}, u32[]{:S(2)}, u32[]{:S(2)}) collective-permute-start(bf16[64,512]{1,0:T(8,128)(2,1)S(1)} %get-tuple-element.28), channel_id=1, source_target_pairs={{0,64},{16,80},{32,96},{48,112},{64,0},{80,16},{96,32},{112,48},{1... | collective-permute-start | bytes 196616 | tf_op jit(solution)/shard_map/ppermute | solution.py:39
  26.1 2.7 %collective-permute-start.1 = (bf16[128,512]{1,0:T(8,128)(2,1)S(1)}, bf16[128,512]{1,0:T(8,128)(2,1)S(1)}, u32[]{:S(2)}, u32[]{:S(2)}) collective-permute-start(bf16[128,512]{1,0:T(8,128)(2,1)S(1)} %pad_maximum_fusion.4), channel_id=1, source_target_pairs={{0,4},{2,6},{4,0},{6,2},{8,12},{10,14},{12,8},{14,10},{1,5},{3,7},... | collective-permute-start | bytes 393224 | tf_op jit(solution)/shard_map/ppermute | solution.py:39
  29.2 4.8 %collective-permute-start.11 = (bf16[128,512]{1,0:T(8,128)(2,1)S(1)}, bf16[128,512]{1,0:T(8,128)(2,1)S(1)}, u32[]{:S(2)}, u32[]{:S(2)}) collective-permute-start(bf16[128,512]{1,0:T(8,128)(2,1)S(1)} %pad_maximum_fusion.5), channel_id=1, source_target_pairs={{0,32},{16,48},{32,0},{48,16},{64,96},{80,112},{96,64},{112,80},{1... | collective-permute-start | bytes 393224 | tf_op jit(solution)/shard_map/ppermute | solution.py:39
  34.2 5.8 %collective-permute-start.2 = (bf16[256,512]{1,0:T(8,128)(2,1)S(1)}, bf16[256,512]{1,0:T(8,128)(2,1)S(1)}, u32[]{:S(2)}, u32[]{:S(2)}) collective-permute-start(bf16[256,512]{1,0:T(8,128)(2,1)S(1)} %pad_maximum_fusion.2), channel_id=1, source_target_pairs={{0,2},{2,0},{4,6},{6,4},{8,10},{10,8},{12,14},{14,12},{1,3},{3,1},... | collective-permute-start | bytes 786440 | tf_op jit(solution)/shard_map/ppermute | solution.py:39
  40.2 3.3 %collective-permute-start.12 = (bf16[256,512]{1,0:T(8,128)(2,1)S(1)}, bf16[256,512]{1,0:T(8,128)(2,1)S(1)}, u32[]{:S(2)}, u32[]{:S(2)}) collective-permute-start(bf16[256,512]{1,0:T(8,128)(2,1)S(1)} %pad_maximum_fusion.3), channel_id=1, source_target_pairs={{0,16},{16,0},{32,48},{48,32},{64,80},{80,64},{96,112},{112,96},{1... | collective-permute-start | bytes 786440 | tf_op jit(solution)/shard_map/ppermute | solution.py:39
  43.5 2.9 %collective-permute-done.2 = bf16[256,512]{1,0:T(8,128)(2,1)S(1)} collective-permute-done((bf16[256,512]{1,0:T(8,128)(2,1)S(1)}, bf16[256,512]{1,0:T(8,128)(2,1)S(1)}, u32[]{:S(2)}, u32[]{:S(2)}) %collective-permute-start.2) | collective-permute-done | bytes 262176 | tf_op jit(solution)/shard_map/ppermute | solution.py:39
  46.5 3.4 %collective-permute-start.3 = (bf16[512,512]{1,0:T(8,128)(2,1)S(1)}, bf16[512,512]{1,0:T(8,128)(2,1)S(1)}, u32[]{:S(2)}, u32[]{:S(2)}) collective-permute-start(bf16[512,512]{1,0:T(8,128)(2,1)S(1)} %pad_maximum_fusion.refs_0_), channel_id=1, source_target_pairs={{0,16},{16,32},{32,48},{48,64},{64,80},{80,96},{96,112},{112,0},{1... | collective-permute-start | bytes 1572872 | tf_op jit(solution)/shard_map/ppermute | solution.py:34
  52.4 7.5 %collective-permute-start.7 = (bf16[512,512]{1,0:T(8,128)(2,1)S(1)}, bf16[512,512]{1,0:T(8,128)(2,1)S(1)}, u32[]{:S(2)}, u32[]{:S(2)}) collective-permute-start(bf16[512,512]{1,0:T(8,128)(2,1)S(1)} %pad_maximum_fusion.refs_0_), channel_id=1, source_target_pairs={{0,112},{16,0},{32,16},{48,32},{64,48},{80,64},{96,80},{112,96},{1... | collective-permute-start | bytes 1572872 | tf_op jit(solution)/shard_map/ppermute | solution.py:34
  59.8 2.5 collective-permute-start.17
  65.3 2.4 collective-permute-start.14
  67.7 5.1 %collective-permute-start.8 = (bf16[512,512]{1,0:T(8,128)(2,1)S(1)}, bf16[512,512]{1,0:T(8,128)(2,1)}, u32[]{:S(2)}, u32[]{:S(2)}) collective-permute-start(bf16[512,512]{1,0:T(8,128)(2,1)S(1)} %collective-permute-done.7.refs_4_), channel_id=1, source_target_pairs={{0,112},{16,0},{32,16},{48,32},{64,48},{80,64},{96,80},{112,96},{1... | collective-permute-start | bytes 1572872 | tf_op jit(solution)/shard_map/ppermute | solution.py:34
  72.8 2.9 %collective-permute-start.18 = (bf16[512,512]{1,0:T(8,128)(2,1)S(1)}, bf16[512,512]{1,0:T(8,128)(2,1)}, u32[]{:S(2)}, u32[]{:S(2)}) collective-permute-start(bf16[512,512]{1,0:T(8,128)(2,1)S(1)} %collective-permute-done.17.refs_12_), channel_id=1, source_target_pairs={{0,14},{2,0},{4,2},{6,4},{8,6},{10,8},{12,10},{14,12},{1,15},{3,1}... | collective-permute-start | bytes 1572872 | tf_op jit(solution)/shard_map/ppermute | solution.py:34
  75.7 2.4 collective-permute-done.4.refs_2_
  82.0 5.1 %collective-permute-start.9 = (bf16[512,512]{1,0:T(8,128)(2,1)}, bf16[512,512]{1,0:T(8,128)(2,1)}, u32[]{:S(2)}, u32[]{:S(2)}) collective-permute-start(bf16[512,512]{1,0:T(8,128)(2,1)} %collective-permute-done.8.refs_5_), channel_id=1, source_target_pairs={{0,112},{16,0},{32,16},{48,32},{64,48},{80,64},{96,80},{112,96},{1... | collective-permute-start | bytes 1572872 | tf_op jit(solution)/shard_map/ppermute | solution.py:34
  87.2 3.9 %collective-permute-start.19 = (bf16[512,512]{1,0:T(8,128)(2,1)}, bf16[512,512]{1,0:T(8,128)(2,1)}, u32[]{:S(2)}, u32[]{:S(2)}) collective-permute-start(bf16[512,512]{1,0:T(8,128)(2,1)} %collective-permute-done.18.refs_13_), channel_id=1, source_target_pairs={{0,14},{2,0},{4,2},{6,4},{8,6},{10,8},{12,10},{14,12},{1,15},{3,1}... | collective-permute-start | bytes 1572872 | tf_op jit(solution)/shard_map/ppermute | solution.py:34
  99.9 2.2 pack.1
  102.8 3.7 %collective-permute-done.6.refs_7_ = bf16[512,512]{1,0:T(8,128)(2,1)} collective-permute-done((bf16[512,512]{1,0:T(8,128)(2,1)}, bf16[512,512]{1,0:T(8,128)(2,1)}, u32[]{:S(2)}, u32[]{:S(2)}) %collective-permute-start.6) | collective-permute-done | bytes 524320 | tf_op jit(solution)/shard_map/ppermute | solution.py:34
  108.2 8.1 %join.1.own_ref = bf16[1024,4096]{1,0:T(8,128)(2,1)} custom-call(s32[5]{0:T(128)} %stack.23.where.pos, bf16[512,512]{1,0:T(8,128)(2,1)} %copy-done.1, bf16[512,512]{1,0:T(8,128)(2,1)} %copy-done.8, bf16[512,512]{1,0:T(8,128)(2,1)} %copy-done.12, bf16[512,512]{1,0:T(8,128)(2,1)} %collective-permute-done.5.refs_3_, bf16[512,512]{1,0:T(8,128)(2,1)} %copy-done.10, ...), custom_call_target="tpu_custom_call" | custom-call | flops 10000000000 | bytes 25165824 | tf_op jit(solution)/shard_map/join/pallas_call | solution.py:186
  118.2 40.7 %all_to_all.10.came_ref = bf16[256,16,128]{2,1,0:T(8,128)(2,1)} all-to-all(bf16[256,16,128]{2,1,0:T(8,128)(2,1)S(1)} %copy-done), channel_id=1, replica_groups=mesh['xh'=2,'c'=2,'z'=8,'y'=8,'xl'=2] {'z','y','xl'}, dimensions={0} | all-to-all | bytes 2097152 | tf_op jit(solution)/shard_map/all_to_all | solution.py:408
  158.9 2.6 %pick.1 = bf16[13,16,128]{2,1,0:T(8,128)(2,1)} custom-call(s32[5]{0:T(128)} %stack.23.where.pos, s32[128]{0:T(128)} %bands.11, s32[128]{0:T(128)} %broadcast_select_fusion.table, bf16[256,16,128]{2,1,0:T(8,128)(2,1)} %all_to_all.10.came_ref), custom_call_target="tpu_custom_call" | custom-call | tf_op jit(solution)/shard_map/pick/pallas_call | solution.py:380
  162.6 2.5 collective-permute-start.22
  165.1 8.9 %early.2 = bf16[144,1024]{1,0:T(8,128)(2,1)} custom-call(s32[5]{0:T(128)} %stack.23.where.pos, s32[128]{0:T(128)} %bands.11, s32[128]{0:T(128)} %broadcast_select_fusion.table, bf16[144,144]{1,0:T(8,128)(2,1)} %copy-done.3, bf16[144,1024]{1,0:T(8,128)(2,1)} %embed_ref.3, bf16[2,1024]{1,0:T(2,128)(2,1)} %level_ref.3, f32[2,1024]{1,0:T(2,128)} %bitcast.44, ...), custom_call_target="tpu_custom_call" | custom-call | tf_op jit(solution)/shard_map/early/pallas_call | solution.py:365
  176.2 8.9 %early.3 = bf16[144,1024]{1,0:T(8,128)(2,1)} custom-call(s32[5]{0:T(128)} %stack.23.where.pos, s32[128]{0:T(128)} %bands.11, s32[128]{0:T(128)} %broadcast_select_fusion.table, bf16[144,144]{1,0:T(8,128)(2,1)} %copy-done.7, bf16[144,1024]{1,0:T(8,128)(2,1)} %embed_ref.3, bf16[2,1024]{1,0:T(2,128)(2,1)} %level_ref.3, f32[2,1024]{1,0:T(2,128)} %bitcast.45, ...), custom_call_target="tpu_custom_call" | custom-call | tf_op jit(solution)/shard_map/early/pallas_call | solution.py:365
  187.6 7.7 %collective-permute-done.23.came_too_ref = bf16[144,1024]{1,0:T(8,128)(2,1)S(1)} collective-permute-done((bf16[144,1024]{1,0:T(8,128)(2,1)}, bf16[144,1024]{1,0:T(8,128)(2,1)S(1)}, u32[]{:S(2)}, u32[]{:S(2)}) %collective-permute-start.23) | collective-permute-done | bytes 294944 | tf_op jit(solution)/shard_map/ppermute | solution.py:390
  196.1 13.4 %late.1 = (bf16[2,144,144]{2,1,0:T(8,128)(2,1)}, bf16[144,144]{1,0:T(8,128)(2,1)}, bf16[144,144]{1,0:T(8,128)(2,1)}) custom-call(s32[5]{0:T(128)} %stack.23.where.pos, s32[128]{0:T(128)} %bands.11, s32[128]{0:T(128)} %broadcast_select_fusion.table, bf16[144,1024]{1,0:T(8,128)(2,1)} %copy-done.5, bf16[144,1024]{1,0:T(8,128)(2,1)} %copy-done.6, ...), custom_call_target="tpu_custom_call" | custom-call | tf_op jit(solution)/shard_map/late/pallas_call | solution.py:365
  211.0 3.8 %collective-permute-start.25 = (bf16[144,144]{1,0:T(8,128)(2,1)}, bf16[144,144]{1,0:T(8,128)(2,1)S(1)}, u32[]{:S(2)}, u32[]{:S(2)}) collective-permute-start(bf16[144,144]{1,0:T(8,128)(2,1)} %get-tuple-element.21), channel_id=1, source_target_pairs={{0,1},{1,0},{2,3},{3,2},{4,5},{5,4},{6,7},{7,6},{8,9},{9,8},{10,11... | collective-permute-start | bytes 124424 | tf_op jit(solution)/shard_map/ppermute | solution.py:39
  214.8 2.6 %collective-permute-done.25 = bf16[144,144]{1,0:T(8,128)(2,1)S(1)} collective-permute-done((bf16[144,144]{1,0:T(8,128)(2,1)}, bf16[144,144]{1,0:T(8,128)(2,1)S(1)}, u32[]{:S(2)}, u32[]{:S(2)}) %collective-permute-start.25) | collective-permute-done | bytes 41504 | tf_op jit(solution)/shard_map/ppermute | solution.py:39
  219.8 2.4 unpick.1
  222.3 36.1 %all_to_all.11.came_ref = bf16[256,16,128]{2,1,0:T(8,128)(2,1)} all-to-all(bf16[256,16,128]{2,1,0:T(8,128)(2,1)} %unpick.1), channel_id=1, replica_groups=mesh['xh'=2,'c'=2,'z'=8,'y'=8,'xl'=2] {'z','y','xl'}, dimensions={0} | all-to-all | bytes 2097152 | tf_op jit(solution)/shard_map/all_to_all | solution.py:438
  258.4 2.9 %unpack.1 = bf16[15,16,128]{2,1,0:T(8,128)(2,1)} custom-call(s32[5]{0:T(128)} %stack.23.where.pos, s32[128]{0:T(128)} %bands.11, s32[128]{0:T(128)} %broadcast_select_fusion.table, bf16[256,16,128]{2,1,0:T(8,128)(2,1)} %all_to_all.11.came_ref), custom_call_target="tpu_custom_call" | custom-call | tf_op jit(solution)/shard_map/unpack/pallas_call | solution.py:380
  (95 shorter events, 37.5 us)
Async XLA Ops:
  8.3 17.8 %collective-permute-start = (bf16[64,512]{1,0:T(8,128)(2,1)S(1)}, bf16[64,512]{1,0:T(8,128)(2,1)S(1)}, u32[]{:S(2)}, u32[]{:S(2)}) collective-permute-start(bf16[64,512]{1,0:T(8,128)(2,1)S(1)} %get-tuple-element.29), channel_id=1, source_target_pairs={{0,8},{2,10},{4,12},{6,14},{8,0},{10,2},{12,4},{14,6},{1,9},{3,11}... | collective-permute-start | bytes 196616 | tf_op jit(solution)/shard_map/ppermute | solution.py:39
  15.2 14.0 %collective-permute-start.10 = (bf16[64,512]{1,0:T(8,128)(2,1)S(1)}, bf16[64,512]{1,0:T(8,128)(2,1)S(1)}, u32[]{:S(2)}, u32[]{:S(2)}) collective-permute-start(bf16[64,512]{1,0:T(8,128)(2,1)S(1)} %get-tuple-element.28), channel_id=1, source_target_pairs={{0,64},{16,80},{32,96},{48,112},{64,0},{80,16},{96,32},{112,48},{1... | collective-permute-start | bytes 196616 | tf_op jit(solution)/shard_map/ppermute | solution.py:39
  26.1 8.1 %collective-permute-start.1 = (bf16[128,512]{1,0:T(8,128)(2,1)S(1)}, bf16[128,512]{1,0:T(8,128)(2,1)S(1)}, u32[]{:S(2)}, u32[]{:S(2)}) collective-permute-start(bf16[128,512]{1,0:T(8,128)(2,1)S(1)} %pad_maximum_fusion.4), channel_id=1, source_target_pairs={{0,4},{2,6},{4,0},{6,2},{8,12},{10,14},{12,8},{14,10},{1,5},{3,7},... | collective-permute-start | bytes 393224 | tf_op jit(solution)/shard_map/ppermute | solution.py:39
  29.2 10.9 %collective-permute-start.11 = (bf16[128,512]{1,0:T(8,128)(2,1)S(1)}, bf16[128,512]{1,0:T(8,128)(2,1)S(1)}, u32[]{:S(2)}, u32[]{:S(2)}) collective-permute-start(bf16[128,512]{1,0:T(8,128)(2,1)S(1)} %pad_maximum_fusion.5), channel_id=1, source_target_pairs={{0,32},{16,48},{32,0},{48,16},{64,96},{80,112},{96,64},{112,80},{1... | collective-permute-start | bytes 393224 | tf_op jit(solution)/shard_map/ppermute | solution.py:39
  34.2 12.2 %collective-permute-start.2 = (bf16[256,512]{1,0:T(8,128)(2,1)S(1)}, bf16[256,512]{1,0:T(8,128)(2,1)S(1)}, u32[]{:S(2)}, u32[]{:S(2)}) collective-permute-start(bf16[256,512]{1,0:T(8,128)(2,1)S(1)} %pad_maximum_fusion.2), channel_id=1, source_target_pairs={{0,2},{2,0},{4,6},{6,4},{8,10},{10,8},{12,14},{14,12},{1,3},{3,1},... | collective-permute-start | bytes 786440 | tf_op jit(solution)/shard_map/ppermute | solution.py:39
  40.2 10.1 %collective-permute-start.12 = (bf16[256,512]{1,0:T(8,128)(2,1)S(1)}, bf16[256,512]{1,0:T(8,128)(2,1)S(1)}, u32[]{:S(2)}, u32[]{:S(2)}) collective-permute-start(bf16[256,512]{1,0:T(8,128)(2,1)S(1)} %pad_maximum_fusion.3), channel_id=1, source_target_pairs={{0,16},{16,0},{32,48},{48,32},{64,80},{80,64},{96,112},{112,96},{1... | collective-permute-start | bytes 786440 | tf_op jit(solution)/shard_map/ppermute | solution.py:39
  46.4 61.7 %copy-start.1 = (bf16[512,512]{1,0:T(8,128)(2,1)}, bf16[512,512]{1,0:T(8,128)(2,1)S(1)}, u32[]{:S(2)}) copy-start(bf16[512,512]{1,0:T(8,128)(2,1)S(1)} %pad_maximum_fusion.refs_0_) | copy-start | bytes 1572868
  46.5 16.3 %collective-permute-start.3 = (bf16[512,512]{1,0:T(8,128)(2,1)S(1)}, bf16[512,512]{1,0:T(8,128)(2,1)S(1)}, u32[]{:S(2)}, u32[]{:S(2)}) collective-permute-start(bf16[512,512]{1,0:T(8,128)(2,1)S(1)} %pad_maximum_fusion.refs_0_), channel_id=1, source_target_pairs={{0,16},{16,32},{32,48},{48,64},{64,80},{80,96},{96,112},{112,0},{1... | collective-permute-start | bytes 1572872 | tf_op jit(solution)/shard_map/ppermute | solution.py:34
  50.3 57.8 %copy-start.2 = (bf16[512,512]{1,0:T(8,128)(2,1)}, bf16[512,512]{1,0:T(8,128)(2,1)S(1)}, u32[]{:S(2)}) copy-start(bf16[512,512]{1,0:T(8,128)(2,1)S(1)} %pad_maximum_fusion.1.refs_8_) | copy-start | bytes 1572868
  50.3 14.9 %collective-permute-start.13 = (bf16[512,512]{1,0:T(8,128)(2,1)S(1)}, bf16[512,512]{1,0:T(8,128)(2,1)S(1)}, u32[]{:S(2)}, u32[]{:S(2)}) collective-permute-start(bf16[512,512]{1,0:T(8,128)(2,1)S(1)} %pad_maximum_fusion.1.refs_8_), channel_id=1, source_target_pairs={{0,2},{2,4},{4,6},{6,8},{8,10},{10,12},{12,14},{14,0},{1,3},{3,5},... | collective-permute-start | bytes 1572872 | tf_op jit(solution)/shard_map/ppermute | solution.py:34
  52.4 15.3 %collective-permute-start.7 = (bf16[512,512]{1,0:T(8,128)(2,1)S(1)}, bf16[512,512]{1,0:T(8,128)(2,1)S(1)}, u32[]{:S(2)}, u32[]{:S(2)}) collective-permute-start(bf16[512,512]{1,0:T(8,128)(2,1)S(1)} %pad_maximum_fusion.refs_0_), channel_id=1, source_target_pairs={{0,112},{16,0},{32,16},{48,32},{64,48},{80,64},{96,80},{112,96},{1... | collective-permute-start | bytes 1572872 | tf_op jit(solution)/shard_map/ppermute | solution.py:34
  59.8 13.0 %collective-permute-start.17 = (bf16[512,512]{1,0:T(8,128)(2,1)S(1)}, bf16[512,512]{1,0:T(8,128)(2,1)S(1)}, u32[]{:S(2)}, u32[]{:S(2)}) collective-permute-start(bf16[512,512]{1,0:T(8,128)(2,1)S(1)} %pad_maximum_fusion.1.refs_8_), channel_id=1, source_target_pairs={{0,14},{2,0},{4,2},{6,4},{8,6},{10,8},{12,10},{14,12},{1,15},{3,1}... | collective-permute-start | bytes 1572872 | tf_op jit(solution)/shard_map/ppermute | solution.py:34
  62.7 45.4 %copy-start.8 = (bf16[512,512]{1,0:T(8,128)(2,1)}, bf16[512,512]{1,0:T(8,128)(2,1)S(1)}, u32[]{:S(2)}) copy-start(bf16[512,512]{1,0:T(8,128)(2,1)S(1)} %collective-permute-done.3.refs_1_) | copy-start | bytes 1572868
  62.7 15.4 %collective-permute-start.4 = (bf16[512,512]{1,0:T(8,128)(2,1)S(1)}, bf16[512,512]{1,0:T(8,128)(2,1)S(1)}, u32[]{:S(2)}, u32[]{:S(2)}) collective-permute-start(bf16[512,512]{1,0:T(8,128)(2,1)S(1)} %collective-permute-done.3.refs_1_), channel_id=1, source_target_pairs={{0,16},{16,32},{32,48},{48,64},{64,80},{80,96},{96,112},{112,0},{1... | collective-permute-start | bytes 1572872 | tf_op jit(solution)/shard_map/ppermute | solution.py:34
  65.3 42.9 %copy-start.9 = (bf16[512,512]{1,0:T(8,128)(2,1)}, bf16[512,512]{1,0:T(8,128)(2,1)S(1)}, u32[]{:S(2)}) copy-start(bf16[512,512]{1,0:T(8,128)(2,1)S(1)} %collective-permute-done.13.refs_9_) | copy-start | bytes 1572868
  65.3 14.8 %collective-permute-start.14 = (bf16[512,512]{1,0:T(8,128)(2,1)S(1)}, bf16[512,512]{1,0:T(8,128)(2,1)S(1)}, u32[]{:S(2)}, u32[]{:S(2)}) collective-permute-start(bf16[512,512]{1,0:T(8,128)(2,1)S(1)} %collective-permute-done.13.refs_9_), channel_id=1, source_target_pairs={{0,2},{2,4},{4,6},{6,8},{8,10},{10,12},{12,14},{14,0},{1,3},{3,5},... | collective-permute-start | bytes 1572872 | tf_op jit(solution)/shard_map/ppermute | solution.py:34
  67.7 28.9 %copy-start.10 = (bf16[512,512]{1,0:T(8,128)(2,1)}, bf16[512,512]{1,0:T(8,128)(2,1)S(1)}, u32[]{:S(2)}) copy-start(bf16[512,512]{1,0:T(8,128)(2,1)S(1)} %collective-permute-done.7.refs_4_) | copy-start | bytes 1572868
  67.7 14.3 %collective-permute-start.8 = (bf16[512,512]{1,0:T(8,128)(2,1)S(1)}, bf16[512,512]{1,0:T(8,128)(2,1)}, u32[]{:S(2)}, u32[]{:S(2)}) collective-permute-start(bf16[512,512]{1,0:T(8,128)(2,1)S(1)} %collective-permute-done.7.refs_4_), channel_id=1, source_target_pairs={{0,112},{16,0},{32,16},{48,32},{64,48},{80,64},{96,80},{112,96},{1... | collective-permute-start | bytes 1572872 | tf_op jit(solution)/shard_map/ppermute | solution.py:34
  72.8 29.3 %copy-start.11 = (bf16[512,512]{1,0:T(8,128)(2,1)}, bf16[512,512]{1,0:T(8,128)(2,1)S(1)}, u32[]{:S(2)}) copy-start(bf16[512,512]{1,0:T(8,128)(2,1)S(1)} %collective-permute-done.17.refs_12_) | copy-start | bytes 1572868
  72.8 14.3 %collective-permute-start.18 = (bf16[512,512]{1,0:T(8,128)(2,1)S(1)}, bf16[512,512]{1,0:T(8,128)(2,1)}, u32[]{:S(2)}, u32[]{:S(2)}) collective-permute-start(bf16[512,512]{1,0:T(8,128)(2,1)S(1)} %collective-permute-done.17.refs_12_), channel_id=1, source_target_pairs={{0,14},{2,0},{4,2},{6,4},{8,6},{10,8},{12,10},{14,12},{1,15},{3,1}... | collective-permute-start | bytes 1572872 | tf_op jit(solution)/shard_map/ppermute | solution.py:34
  78.1 14.5 %collective-permute-start.5 = (bf16[512,512]{1,0:T(8,128)(2,1)S(1)}, bf16[512,512]{1,0:T(8,128)(2,1)}, u32[]{:S(2)}, u32[]{:S(2)}) collective-permute-start(bf16[512,512]{1,0:T(8,128)(2,1)S(1)} %collective-permute-done.4.refs_2_), channel_id=1, source_target_pairs={{0,16},{16,32},{32,48},{48,64},{64,80},{80,96},{96,112},{112,0},{1... | collective-permute-start | bytes 1572872 | tf_op jit(solution)/shard_map/ppermute | solution.py:34
  80.1 14.5 %collective-permute-start.15 = (bf16[512,512]{1,0:T(8,128)(2,1)S(1)}, bf16[512,512]{1,0:T(8,128)(2,1)}, u32[]{:S(2)}, u32[]{:S(2)}) collective-permute-start(bf16[512,512]{1,0:T(8,128)(2,1)S(1)} %collective-permute-done.14.refs_10_), channel_id=1, source_target_pairs={{0,2},{2,4},{4,6},{6,8},{8,10},{10,12},{12,14},{14,0},{1,3},{3,5},... | collective-permute-start | bytes 1572872 | tf_op jit(solution)/shard_map/ppermute | solution.py:34
  82.0 20.8 %collective-permute-start.9 = (bf16[512,512]{1,0:T(8,128)(2,1)}, bf16[512,512]{1,0:T(8,128)(2,1)}, u32[]{:S(2)}, u32[]{:S(2)}) collective-permute-start(bf16[512,512]{1,0:T(8,128)(2,1)} %collective-permute-done.8.refs_5_), channel_id=1, source_target_pairs={{0,112},{16,0},{32,16},{48,32},{64,48},{80,64},{96,80},{112,96},{1... | collective-permute-start | bytes 1572872 | tf_op jit(solution)/shard_map/ppermute | solution.py:34
  87.2 15.7 %collective-permute-start.19 = (bf16[512,512]{1,0:T(8,128)(2,1)}, bf16[512,512]{1,0:T(8,128)(2,1)}, u32[]{:S(2)}, u32[]{:S(2)}) collective-permute-start(bf16[512,512]{1,0:T(8,128)(2,1)} %collective-permute-done.18.refs_13_), channel_id=1, source_target_pairs={{0,14},{2,0},{4,2},{6,4},{8,6},{10,8},{12,10},{14,12},{1,15},{3,1}... | collective-permute-start | bytes 1572872 | tf_op jit(solution)/shard_map/ppermute | solution.py:34
  92.7 13.8 %collective-permute-start.6 = (bf16[512,512]{1,0:T(8,128)(2,1)}, bf16[512,512]{1,0:T(8,128)(2,1)}, u32[]{:S(2)}, u32[]{:S(2)}) collective-permute-start(bf16[512,512]{1,0:T(8,128)(2,1)} %collective-permute-done.5.refs_3_), channel_id=1, source_target_pairs={{0,16},{16,32},{32,48},{48,64},{64,80},{80,96},{96,112},{112,0},{1... | collective-permute-start | bytes 1572872 | tf_op jit(solution)/shard_map/ppermute | solution.py:34
  94.6 13.6 %collective-permute-start.16 = (bf16[512,512]{1,0:T(8,128)(2,1)}, bf16[512,512]{1,0:T(8,128)(2,1)}, u32[]{:S(2)}, u32[]{:S(2)}) collective-permute-start(bf16[512,512]{1,0:T(8,128)(2,1)} %collective-permute-done.15.refs_11_), channel_id=1, source_target_pairs={{0,2},{2,4},{4,6},{6,8},{8,10},{10,12},{12,14},{14,0},{1,3},{3,5},... | collective-permute-start | bytes 1572872 | tf_op jit(solution)/shard_map/ppermute | solution.py:34
  116.3 48.8 %collective-permute-start.20 = (bf16[1024,4096]{1,0:T(8,128)(2,1)}, bf16[1024,4096]{1,0:T(8,128)(2,1)}, u32[]{:S(2)}, u32[]{:S(2)}) collective-permute-start(bf16[1024,4096]{1,0:T(8,128)(2,1)} %join.1.own_ref), channel_id=1, source_target_pairs={{0,128},{128,0},{1,129},{129,1},{2,130},{130,2},{3,131},{131,3},{4... | collective-permute-start | bytes 25165832 | tf_op jit(solution)/shard_map/ppermute | solution.py:39
  162.6 12.9 %collective-permute-start.22 = (bf16[144,144]{1,0:T(8,128)(2,1)S(1)}, bf16[144,144]{1,0:T(8,128)(2,1)S(1)}, u32[]{:S(2)}, u32[]{:S(2)}) collective-permute-start(bf16[144,144]{1,0:T(8,128)(2,1)S(1)} %reshape.32.raw_ref), channel_id=1, source_target_pairs={{256,1},{257,0},{258,3},{259,2},{260,5},{261,4},{262,7},{263,6},{2... | collective-permute-start | bytes 124424 | tf_op jit(solution)/shard_map/ppermute | solution.py:390
  174.1 13.5 %collective-permute-start.21 = (bf16[144,1024]{1,0:T(8,128)(2,1)}, bf16[144,1024]{1,0:T(8,128)(2,1)S(1)}, u32[]{:S(2)}, u32[]{:S(2)}) collective-permute-start(bf16[144,1024]{1,0:T(8,128)(2,1)} %early.2), channel_id=1, source_target_pairs={{0,257},{1,256},{2,259},{3,258},{4,261},{5,260},{6,263},{7,262},{8... | collective-permute-start | bytes 884744 | tf_op jit(solution)/shard_map/ppermute | solution.py:390
  185.1 10.2 %collective-permute-start.23 = (bf16[144,1024]{1,0:T(8,128)(2,1)}, bf16[144,1024]{1,0:T(8,128)(2,1)S(1)}, u32[]{:S(2)}, u32[]{:S(2)}) collective-permute-start(bf16[144,1024]{1,0:T(8,128)(2,1)} %early.3), channel_id=1, source_target_pairs={{0,257},{1,256},{2,259},{3,258},{4,261},{5,260},{6,263},{7,262},{8... | collective-permute-start | bytes 884744 | tf_op jit(solution)/shard_map/ppermute | solution.py:390
  209.5 8.0 %collective-permute-start.24 = (bf16[2,144,144]{2,1,0:T(8,128)(2,1)}, bf16[2,144,144]{2,1,0:T(8,128)(2,1)S(1)}, u32[]{:S(2)}, u32[]{:S(2)}) collective-permute-start(bf16[2,144,144]{2,1,0:T(8,128)(2,1)} %get-tuple-element.20), channel_id=1, source_target_pairs={{256,1},{257,0},{258,3},{259,2},{260,5},{261,4},{262,7},{263,6},{2... | collective-permute-start | bytes 248840 | tf_op jit(solution)/shard_map/ppermute | solution.py:390
  211.0 6.5 %collective-permute-start.25 = (bf16[144,144]{1,0:T(8,128)(2,1)}, bf16[144,144]{1,0:T(8,128)(2,1)S(1)}, u32[]{:S(2)}, u32[]{:S(2)}) collective-permute-start(bf16[144,144]{1,0:T(8,128)(2,1)} %get-tuple-element.21), channel_id=1, source_target_pairs={{0,1},{1,0},{2,3},{3,2},{4,5},{5,4},{6,7},{7,6},{8,9},{9,8},{10,11... | collective-permute-start | bytes 124424 | tf_op jit(solution)/shard_map/ppermute | solution.py:39
  (8 other events, 61.2 us)

commit v2 on v1

--- a/solution.py
+++ b/solution.py
@@ -47,15 +47,30 @@
     return WIN_ROWS * seventh(jnp.maximum(window, 0)) - WIN_ROWS // 2
 
 
-def pack_kernel(table, rows_ref, out_ref):
-    def shard(j, carry):
-        window = jnp.maximum(table[j], 0)
-        column = window - LW * seventh(window)
-        out_ref[2 * j] = rows_ref[column]
-        out_ref[2 * j + 1] = rows_ref[LW + column]
-        return carry
-
-    lax.fori_loop(0, table.shape[0], shard, 0, unroll=8)
+def pack_kernel(where, bands, table, rows_ref, out_ref):
+    column_of_bands, z = lax.rem(where[0], 16), where[1]
+    starts, blocks = [], []
+    total = jnp.int32(0)
+    for far in range(bands.shape[0] // 16):
+        def add(i, sums, base=16 * far):
+            count = bands[base + i]
+            return sums[0] + count, sums[1] + jnp.where(i < column_of_bands, count, 0)
+
+        total, start = lax.fori_loop(0, 16, add, (total, total), unroll=4)
+        starts.append(start)
+        step = z ^ far
+        place = (lax.rem(step, 2) * 4) | (step & 2) | lax.div(step, 4)
+        blocks.append(place * 2 * LW)
+    for shard in range(16):
+        window = jnp.maximum(table[z * 16 + shard], 0)
+        first = first_row(window)
+        block = jnp.int32(0)
+        for start, at in zip(starts, blocks):
+            row = start - first
+            block = jnp.where((row >= -1) & (row < WIN_ROWS), at, block)
+        column = block + window - LW * seventh(window)
+        out_ref[2 * shard] = rows_ref[column]
+        out_ref[2 * shard + 1] = rows_ref[LW + column]
 
 
 def pick_kernel(where, bands, table, came_ref, out_ref):
@@ -67,9 +82,9 @@
     def band(i, row):
         count = bands[i]
         here = (row >= 0) & (row < count_rows)
-        out_ref[jnp.where(here, row, WIN_ROWS)] = came_ref[2 * i]
+        out_ref[jnp.where(here, row, WIN_ROWS)] = came_ref[2 * (i & 15)]
         here = (count > 1) & (row >= -1) & (row + 1 < count_rows)
-        out_ref[jnp.where(here, row + 1, WIN_ROWS)] = came_ref[2 * i + 1]
+        out_ref[jnp.where(here, row + 1, WIN_ROWS)] = came_ref[2 * (i & 15) + 1]
         return row + count
 
     lax.fori_loop(0, bands.shape[0], band, -first, unroll=8)
@@ -161,7 +176,7 @@
         c.wait()
 
 
-def gather_section(weight, pos, message, gains):
+def gather_section(weight, pos, rows, gains, pack):
     mine = weight[0].T
     pair = lax.all_gather(mine, "xl", axis=0, tiled=True)
     pair, gains = lax.optimization_barrier((pair, gains))
@@ -169,6 +184,10 @@
     for bit in DOUBLING:
         a_far, b_far = swap(a, "y", bit), swap(b, "z", bit)
         a, b = jnp.concatenate([a, a_far]), jnp.concatenate([b, b_far])
+    for bit in DOUBLING:
+        rows = jnp.concatenate([rows, swap(rows, "z", bit)])
+    a, b, rows = lax.optimization_barrier((a, b, rows))
+    message = pack(rows)
     chains = [("z", 1), ("z", -1), ("y", 1), ("y", -1)]
     got = [[] for _ in chains]
     held = [a, a, b, b]
@@ -402,10 +421,15 @@
     table = jnp.where(is_late, turned, window_table)
     scalars = (pos, band_rows, table)
 
-    message = small_call(pack_kernel, 2 * lat_count, (table,), to_rows(fields[0]), "pack")
     gains = lax.all_gather(norm_gain, "c", axis=0, tiled=True)
-    own, message, gains = gather_section(attn_weight, pos, message, gains)
-    arrived = lax.all_to_all(message, LAT, 0, 0, tiled=True)
+    own, message, gains = gather_section(
+        attn_weight,
+        pos,
+        to_rows(fields[0]),
+        gains,
+        lambda rows: small_call(pack_kernel, 32, scalars, rows, "pack"),
+    )
+    arrived = lax.all_to_all(message, ("y", "xl"), 0, 0, tiled=True)
     other = swap(own, "c", 1)
     raw_rows = small_call(pick_kernel, WIN_ROWS + 1, scalars, arrived, "pick")
     own_raw = from_rows(raw_rows[:WIN_ROWS])

time: 264 us -> 253 us (0.958)
  blocking collectives: 83.8 us -> 59.6 us
  starting transfers between devices: 91.8 us -> 99.3 us
  waiting for transfers between devices: 24.5 us -> 29.3 us
    all_to_all x1, blocking collectives: 40.7 us -> 15.1 us  [per_device(): arrived = lax.all_to_all(message, ('y', 'xl'), 0, 0, tiled=True)]
    ppermute x8 -> x11, starting transfers between devices: 40.2 us -> 47.1 us  [swap(): return lax.ppermute(value, axis, [(i, i ^ bit) for i in range(n)])]
    ppermute x8 -> x11, waiting for transfers between devices: 6.61 us -> 9.34 us  [swap(): return lax.ppermute(value, axis, [(i, i ^ bit) for i in range(n)])]
  transfers between devices with their start and end apart: 26 -> 29, of which waited for: 14 -> 13; matrix products, arithmetic and copies ran while one was open for 2% -> 2% of each run, Pallas kernels for 9% -> 5%
where the time goes in v2:
time: 253 us; the launch traced here: 251 us
  starting transfers between devices  99.3 us (39%)
  blocking collectives  59.6 us (24%)
  Pallas kernels  49.4 us (20%)
  waiting for transfers between devices  29.3 us (12%)
  local copies, waits for them, and re-layouts  9.26 us (4%)
  other arithmetic  3.1 us (1%)
    ppermute x11, starting transfers between devices, swap(): return lax.ppermute(value, axis, [(i, i ^ bit) for i in range(n)])  47.1 us
    ppermute x14, starting transfers between devices, ring(): return lax.ppermute(value, axis, [(i, (i + by) % n) for i in range(n)])  46 us
    all_to_all x1, blocking collectives, per_device(): came_back = lax.all_to_all(reply, LAT, 0, 0, tiled=True)  37.4 us
    pallas_call x3, Pallas kernels, sections_call(): pl.pallas_call(body, out_shape=tuple((jax.ShapeDtypeStruct(shape, BF) for...  31.2 us
    all_to_all x1, blocking collectives, per_device(): arrived = lax.all_to_all(message, ('y', 'xl'), 0, 0, tiled=True)  15.1 us
    ppermute x14, waiting for transfers between devices, ring(): return lax.ppermute(value, axis, [(i, (i + by) % n) for i in range(n)])  11.2 us
    pallas_call x4, Pallas kernels, small_call(): pl.pallas_call(body, out_shape=jax.ShapeDtypeStruct((out_rows, PACK, 128)...  10.1 us
    ppermute x11, waiting for transfers between devices, swap(): return lax.ppermute(value, axis, [(i, i ^ bit) for i in range(n)])  9.34 us
  transfers between devices with their start and end apart: 29, of which 13 were waited for; matrix products, arithmetic and copies ran while one was open for 2% of the time, Pallas kernels for 5%

profile of v2, /device:TPU:12, one launch (start us, length us, event | category | flops | bytes accessed | tf_op | source)
XLA Modules:
  0.0 251.1 jit_solution(8345987974181727299)
XLA Ops:
  1.8 10.9 %collective-permute-start.6 = (bf16[14,16,128]{2,1,0:T(8,128)(2,1)S(1)}, bf16[14,16,128]{2,1,0:T(8,128)(2,1)S(1)}, u32[]{:S(2)}, u32[]{:S(2)}) collective-permute-start(bf16[14,16,128]{2,1,0:T(8,128)(2,1)S(1)} %slice.38), channel_id=1, source_target_pairs={{0,64},{16,80},{32,96},{48,112},{64,0},{80,16},{96,32},{112,48},{1... | collective-permute-start | bytes 172040 | tf_op jit(solution)/shard_map/ppermute | solution.py:39
  12.8 5.2 %all_gather.6 = bf16[64,1024]{1,0:T(8,128)(2,1)S(1)} all-gather(bf16[32,1024]{1,0:T(8,128)(2,1)} %bitcast.47), channel_id=1, replica_groups=mesh['xh'=2,'c'=2,'z'=8,'y'=8,'xl'=2] {'xl'}, dimensions={0}, use_global_device_ids=true | all-gather | bytes 196608 | tf_op jit(solution)/shard_map/all_gather | solution.py:181
  22.4 6.8 %collective-permute-start = (bf16[64,512]{1,0:T(8,128)(2,1)S(1)}, bf16[64,512]{1,0:T(8,128)(2,1)S(1)}, u32[]{:S(2)}, u32[]{:S(2)}) collective-permute-start(bf16[64,512]{1,0:T(8,128)(2,1)S(1)} %get-tuple-element.35), channel_id=1, source_target_pairs={{0,8},{2,10},{4,12},{6,14},{8,0},{10,2},{12,4},{14,6},{1,9},{3,11}... | collective-permute-start | bytes 196616 | tf_op jit(solution)/shard_map/ppermute | solution.py:39
  29.2 4.3 %collective-permute-start.7 = (bf16[28,16,128]{2,1,0:T(8,128)(2,1)S(1)}, bf16[28,16,128]{2,1,0:T(8,128)(2,1)S(1)}, u32[]{:S(2)}, u32[]{:S(2)}) collective-permute-start(bf16[28,16,128]{2,1,0:T(8,128)(2,1)S(1)} %pad_maximum_fusion.8), channel_id=1, source_target_pairs={{0,32},{16,48},{32,0},{48,16},{64,96},{80,112},{96,64},{112,80},{1... | collective-permute-start | bytes 344072 | tf_op jit(solution)/shard_map/ppermute | solution.py:39
  36.1 4.5 %collective-permute-start.1 = (bf16[128,512]{1,0:T(8,128)(2,1)S(1)}, bf16[128,512]{1,0:T(8,128)(2,1)S(1)}, u32[]{:S(2)}, u32[]{:S(2)}) collective-permute-start(bf16[128,512]{1,0:T(8,128)(2,1)S(1)} %pad_maximum_fusion.6), channel_id=1, source_target_pairs={{0,4},{2,6},{4,0},{6,2},{8,12},{10,14},{12,8},{14,10},{1,5},{3,7},... | collective-permute-start | bytes 393224 | tf_op jit(solution)/shard_map/ppermute | solution.py:39
  40.5 2.5 %collective-permute-done.7 = bf16[28,16,128]{2,1,0:T(8,128)(2,1)S(1)} collective-permute-done((bf16[28,16,128]{2,1,0:T(8,128)(2,1)S(1)}, bf16[28,16,128]{2,1,0:T(8,128)(2,1)S(1)}, u32[]{:S(2)}, u32[]{:S(2)}) %collective-permute-start.7) | collective-permute-done | bytes 114720 | tf_op jit(solution)/shard_map/ppermute | solution.py:39
  45.1 3.9 %collective-permute-start.5 = (bf16[256,512]{1,0:T(8,128)(2,1)S(1)}, bf16[256,512]{1,0:T(8,128)(2,1)S(1)}, u32[]{:S(2)}, u32[]{:S(2)}) collective-permute-start(bf16[256,512]{1,0:T(8,128)(2,1)S(1)} %pad_maximum_fusion.4), channel_id=1, source_target_pairs={{0,16},{16,0},{32,48},{48,32},{64,80},{80,64},{96,112},{112,96},{1... | collective-permute-start | bytes 786440 | tf_op jit(solution)/shard_map/ppermute | solution.py:39
  49.0 3.3 %collective-permute-start.2 = (bf16[256,512]{1,0:T(8,128)(2,1)S(1)}, bf16[256,512]{1,0:T(8,128)(2,1)S(1)}, u32[]{:S(2)}, u32[]{:S(2)}) collective-permute-start(bf16[256,512]{1,0:T(8,128)(2,1)S(1)} %pad_maximum_fusion.3), channel_id=1, source_target_pairs={{0,2},{2,0},{4,6},{6,4},{8,10},{10,8},{12,14},{14,12},{1,3},{3,1},... | collective-permute-start | bytes 786440 | tf_op jit(solution)/shard_map/ppermute | solution.py:39
  54.0 2.7 %collective-permute-done.5 = bf16[256,512]{1,0:T(8,128)(2,1)S(1)} collective-permute-done((bf16[256,512]{1,0:T(8,128)(2,1)S(1)}, bf16[256,512]{1,0:T(8,128)(2,1)S(1)}, u32[]{:S(2)}, u32[]{:S(2)}) %collective-permute-start.5) | collective-permute-done | bytes 262176 | tf_op jit(solution)/shard_map/ppermute | solution.py:39
  57.4 2.8 %collective-permute-start.9 = (bf16[512,512]{1,0:T(8,128)(2,1)S(1)}, bf16[512,512]{1,0:T(8,128)(2,1)S(1)}, u32[]{:S(2)}, u32[]{:S(2)}) collective-permute-start(bf16[512,512]{1,0:T(8,128)(2,1)S(1)} %pad_maximum_fusion.refs_0_), channel_id=1, source_target_pairs={{0,16},{16,32},{32,48},{48,64},{64,80},{80,96},{96,112},{112,0},{1... | collective-permute-start | bytes 1572872 | tf_op jit(solution)/shard_map/ppermute | solution.py:34
  60.2 2.6 %collective-permute-start.16 = (bf16[512,512]{1,0:T(8,128)(2,1)S(1)}, bf16[512,512]{1,0:T(8,128)(2,1)S(1)}, u32[]{:S(2)}, u32[]{:S(2)}) collective-permute-start(bf16[512,512]{1,0:T(8,128)(2,1)S(1)} %pad_maximum_fusion.1.refs_8_), channel_id=1, source_target_pairs={{0,2},{2,4},{4,6},{6,8},{8,10},{10,12},{12,14},{14,0},{1,3},{3,5},... | collective-permute-start | bytes 1572872 | tf_op jit(solution)/shard_map/ppermute | solution.py:34
  62.8 7.1 %collective-permute-start.13 = (bf16[512,512]{1,0:T(8,128)(2,1)S(1)}, bf16[512,512]{1,0:T(8,128)(2,1)S(1)}, u32[]{:S(2)}, u32[]{:S(2)}) collective-permute-start(bf16[512,512]{1,0:T(8,128)(2,1)S(1)} %pad_maximum_fusion.refs_0_), channel_id=1, source_target_pairs={{0,112},{16,0},{32,16},{48,32},{64,48},{80,64},{96,80},{112,96},{1... | collective-permute-start | bytes 1572872 | tf_op jit(solution)/shard_map/ppermute | solution.py:34
  70.0 3.3 %collective-permute-start.20 = (bf16[512,512]{1,0:T(8,128)(2,1)S(1)}, bf16[512,512]{1,0:T(8,128)(2,1)S(1)}, u32[]{:S(2)}, u32[]{:S(2)}) collective-permute-start(bf16[512,512]{1,0:T(8,128)(2,1)S(1)} %pad_maximum_fusion.1.refs_8_), channel_id=1, source_target_pairs={{0,14},{2,0},{4,2},{6,4},{8,6},{10,8},{12,10},{14,12},{1,15},{3,1}... | collective-permute-start | bytes 1572872 | tf_op jit(solution)/shard_map/ppermute | solution.py:34
  73.2 3.0 %collective-permute-done.9.refs_1_ = bf16[512,512]{1,0:T(8,128)(2,1)S(1)} collective-permute-done((bf16[512,512]{1,0:T(8,128)(2,1)S(1)}, bf16[512,512]{1,0:T(8,128)(2,1)S(1)}, u32[]{:S(2)}, u32[]{:S(2)}) %collective-permute-start.9) | collective-permute-done | bytes 524320 | tf_op jit(solution)/shard_map/ppermute | solution.py:34
  78.1 2.6 %collective-permute-start.17 = (bf16[512,512]{1,0:T(8,128)(2,1)S(1)}, bf16[512,512]{1,0:T(8,128)(2,1)S(1)}, u32[]{:S(2)}, u32[]{:S(2)}) collective-permute-start(bf16[512,512]{1,0:T(8,128)(2,1)S(1)} %collective-permute-done.16.refs_9_), channel_id=1, source_target_pairs={{0,2},{2,4},{4,6},{6,8},{8,10},{10,12},{12,14},{14,0},{1,3},{3,5},... | collective-permute-start | bytes 1572872 | tf_op jit(solution)/shard_map/ppermute | solution.py:34
  80.7 5.1 %collective-permute-start.14 = (bf16[512,512]{1,0:T(8,128)(2,1)S(1)}, bf16[512,512]{1,0:T(8,128)(2,1)}, u32[]{:S(2)}, u32[]{:S(2)}) collective-permute-start(bf16[512,512]{1,0:T(8,128)(2,1)S(1)} %collective-permute-done.13.refs_4_), channel_id=1, source_target_pairs={{0,112},{16,0},{32,16},{48,32},{64,48},{80,64},{96,80},{112,96},{1... | collective-permute-start | bytes 1572872 | tf_op jit(solution)/shard_map/ppermute | solution.py:34
  85.9 3.3 %collective-permute-start.21 = (bf16[512,512]{1,0:T(8,128)(2,1)S(1)}, bf16[512,512]{1,0:T(8,128)(2,1)}, u32[]{:S(2)}, u32[]{:S(2)}) collective-permute-start(bf16[512,512]{1,0:T(8,128)(2,1)S(1)} %collective-permute-done.20.refs_12_), channel_id=1, source_target_pairs={{0,14},{2,0},{4,2},{6,4},{8,6},{10,8},{12,10},{14,12},{1,15},{3,1}... | collective-permute-start | bytes 1572872 | tf_op jit(solution)/shard_map/ppermute | solution.py:34
  93.1 2.6 %collective-permute-start.18 = (bf16[512,512]{1,0:T(8,128)(2,1)S(1)}, bf16[512,512]{1,0:T(8,128)(2,1)}, u32[]{:S(2)}, u32[]{:S(2)}) collective-permute-start(bf16[512,512]{1,0:T(8,128)(2,1)S(1)} %collective-permute-done.17.refs_10_), channel_id=1, source_target_pairs={{0,2},{2,4},{4,6},{6,8},{8,10},{10,12},{12,14},{14,0},{1,3},{3,5},... | collective-permute-start | bytes 1572872 | tf_op jit(solution)/shard_map/ppermute | solution.py:34
  95.7 5.1 %collective-permute-start.15 = (bf16[512,512]{1,0:T(8,128)(2,1)}, bf16[512,512]{1,0:T(8,128)(2,1)}, u32[]{:S(2)}, u32[]{:S(2)}) collective-permute-start(bf16[512,512]{1,0:T(8,128)(2,1)} %collective-permute-done.14.refs_5_), channel_id=1, source_target_pairs={{0,112},{16,0},{32,16},{48,32},{64,48},{80,64},{96,80},{112,96},{1... | collective-permute-start | bytes 1572872 | tf_op jit(solution)/shard_map/ppermute | solution.py:34
  100.8 3.3 %collective-permute-start.22 = (bf16[512,512]{1,0:T(8,128)(2,1)}, bf16[512,512]{1,0:T(8,128)(2,1)}, u32[]{:S(2)}, u32[]{:S(2)}) collective-permute-start(bf16[512,512]{1,0:T(8,128)(2,1)} %collective-permute-done.21.refs_13_), channel_id=1, source_target_pairs={{0,14},{2,0},{4,2},{6,4},{8,6},{10,8},{12,10},{14,12},{1,15},{3,1}... | collective-permute-start | bytes 1572872 | tf_op jit(solution)/shard_map/ppermute | solution.py:34
  107.2 2.6 %collective-permute-start.19 = (bf16[512,512]{1,0:T(8,128)(2,1)}, bf16[512,512]{1,0:T(8,128)(2,1)}, u32[]{:S(2)}, u32[]{:S(2)}) collective-permute-start(bf16[512,512]{1,0:T(8,128)(2,1)} %collective-permute-done.18.refs_11_), channel_id=1, source_target_pairs={{0,2},{2,4},{4,6},{6,8},{8,10},{10,12},{12,14},{14,0},{1,3},{3,5},... | collective-permute-start | bytes 1572872 | tf_op jit(solution)/shard_map/ppermute | solution.py:34
  114.3 4.4 %collective-permute-done.12.refs_7_ = bf16[512,512]{1,0:T(8,128)(2,1)} collective-permute-done((bf16[512,512]{1,0:T(8,128)(2,1)}, bf16[512,512]{1,0:T(8,128)(2,1)}, u32[]{:S(2)}, u32[]{:S(2)}) %collective-permute-start.12) | collective-permute-done | bytes 524320 | tf_op jit(solution)/shard_map/ppermute | solution.py:34
  119.5 8.1 %join.1.own_ref = bf16[1024,4096]{1,0:T(8,128)(2,1)} custom-call(s32[5]{0:T(128)} %stack.23.where.pos, bf16[512,512]{1,0:T(8,128)(2,1)} %copy-done.1, bf16[512,512]{1,0:T(8,128)(2,1)} %copy-done.8, bf16[512,512]{1,0:T(8,128)(2,1)} %copy-done.12, bf16[512,512]{1,0:T(8,128)(2,1)} %collective-permute-done.11.refs_3_, bf16[512,512]{1,0:T(8,128)(2,1)} %copy-done.10, ...), custom_call_target="tpu_custom_call" | custom-call | flops 10000000000 | bytes 25165824 | tf_op jit(solution)/shard_map/join/pallas_call | solution.py:205
  129.5 15.1 %all_to_all.10.came_ref = bf16[32,16,128]{2,1,0:T(8,128)(2,1)} all-to-all(bf16[32,16,128]{2,1,0:T(8,128)(2,1)S(1)} %copy-done.2), channel_id=1, replica_groups=mesh['xh'=2,'c'=2,'z'=8,'y'=8,'xl'=2] {'y','xl'}, dimensions={0} | all-to-all | bytes 262144 | tf_op jit(solution)/shard_map/all_to_all | solution.py:432
  152.3 8.9 %early.3 = bf16[144,1024]{1,0:T(8,128)(2,1)} custom-call(s32[5]{0:T(128)} %stack.23.where.pos, s32[128]{0:T(128)} %bands.13, s32[128]{0:T(128)} %broadcast_select_fusion.table, bf16[144,144]{1,0:T(8,128)(2,1)} %copy-done.7, bf16[144,1024]{1,0:T(8,128)(2,1)} %embed_ref.3, bf16[2,1024]{1,0:T(2,128)(2,1)} %level_ref.3, f32[2,1024]{1,0:T(2,128)} %bitcast.44, ...), custom_call_target="tpu_custom_call" | custom-call | tf_op jit(solution)/shard_map/early/pallas_call | solution.py:384
  162.8 8.9 %early.2 = bf16[144,1024]{1,0:T(8,128)(2,1)} custom-call(s32[5]{0:T(128)} %stack.23.where.pos, s32[128]{0:T(128)} %bands.13, s32[128]{0:T(128)} %broadcast_select_fusion.table, bf16[144,144]{1,0:T(8,128)(2,1)} %copy-done.3, bf16[144,1024]{1,0:T(8,128)(2,1)} %embed_ref.3, bf16[2,1024]{1,0:T(2,128)(2,1)} %level_ref.3, f32[2,1024]{1,0:T(2,128)} %bitcast.45, ...), custom_call_target="tpu_custom_call" | custom-call | tf_op jit(solution)/shard_map/early/pallas_call | solution.py:384
  174.0 6.8 %collective-permute-done.24.came_ref = bf16[144,1024]{1,0:T(8,128)(2,1)S(1)} collective-permute-done((bf16[144,1024]{1,0:T(8,128)(2,1)}, bf16[144,1024]{1,0:T(8,128)(2,1)S(1)}, u32[]{:S(2)}, u32[]{:S(2)}) %collective-permute-start.24) | collective-permute-done | bytes 294944 | tf_op jit(solution)/shard_map/ppermute | solution.py:409
  181.5 13.4 %late.1 = (bf16[2,144,144]{2,1,0:T(8,128)(2,1)}, bf16[144,144]{1,0:T(8,128)(2,1)}, bf16[144,144]{1,0:T(8,128)(2,1)}) custom-call(s32[5]{0:T(128)} %stack.23.where.pos, s32[128]{0:T(128)} %bands.13, s32[128]{0:T(128)} %broadcast_select_fusion.table, bf16[144,1024]{1,0:T(8,128)(2,1)} %copy-done.6, bf16[144,1024]{1,0:T(8,128)(2,1)} %copy-done.5, ...), custom_call_target="tpu_custom_call" | custom-call | tf_op jit(solution)/shard_map/late/pallas_call | solution.py:384
  196.5 5.2 %collective-permute-start.28 = (bf16[144,144]{1,0:T(8,128)(2,1)}, bf16[144,144]{1,0:T(8,128)(2,1)S(1)}, u32[]{:S(2)}, u32[]{:S(2)}) collective-permute-start(bf16[144,144]{1,0:T(8,128)(2,1)} %get-tuple-element.27), channel_id=1, source_target_pairs={{0,1},{1,0},{2,3},{3,2},{4,5},{5,4},{6,7},{7,6},{8,9},{9,8},{10,11... | collective-permute-start | bytes 124424 | tf_op jit(solution)/shard_map/ppermute | solution.py:39
  201.7 2.5 %collective-permute-done.28 = bf16[144,144]{1,0:T(8,128)(2,1)S(1)} collective-permute-done((bf16[144,144]{1,0:T(8,128)(2,1)}, bf16[144,144]{1,0:T(8,128)(2,1)S(1)}, u32[]{:S(2)}, u32[]{:S(2)}) %collective-permute-start.28) | collective-permute-done | bytes 41504 | tf_op jit(solution)/shard_map/ppermute | solution.py:39
  209.1 37.4 %all_to_all.11.came_ref = bf16[256,16,128]{2,1,0:T(8,128)(2,1)} all-to-all(bf16[256,16,128]{2,1,0:T(8,128)(2,1)} %unpick.1), channel_id=1, replica_groups=mesh['xh'=2,'c'=2,'z'=8,'y'=8,'xl'=2] {'z','y','xl'}, dimensions={0} | all-to-all | bytes 2097152 | tf_op jit(solution)/shard_map/all_to_all | solution.py:462
  246.4 2.9 %unpack.1 = bf16[15,16,128]{2,1,0:T(8,128)(2,1)} custom-call(s32[5]{0:T(128)} %stack.23.where.pos, s32[128]{0:T(128)} %bands.13, s32[128]{0:T(128)} %broadcast_select_fusion.table, bf16[256,16,128]{2,1,0:T(8,128)(2,1)} %all_to_all.11.came_ref), custom_call_target="tpu_custom_call" | custom-call | tf_op jit(solution)/shard_map/unpack/pallas_call | solution.py:399
  (104 shorter events, 48.9 us)
Async XLA Ops:
  1.8 27.4 %collective-permute-start.6 = (bf16[14,16,128]{2,1,0:T(8,128)(2,1)S(1)}, bf16[14,16,128]{2,1,0:T(8,128)(2,1)S(1)}, u32[]{:S(2)}, u32[]{:S(2)}) collective-permute-start(bf16[14,16,128]{2,1,0:T(8,128)(2,1)S(1)} %slice.38), channel_id=1, source_target_pairs={{0,64},{16,80},{32,96},{48,112},{64,0},{80,16},{96,32},{112,48},{1... | collective-permute-start | bytes 172040 | tf_op jit(solution)/shard_map/ppermute | solution.py:39
  20.4 13.1 %collective-permute-start.3 = (bf16[64,512]{1,0:T(8,128)(2,1)S(1)}, bf16[64,512]{1,0:T(8,128)(2,1)S(1)}, u32[]{:S(2)}, u32[]{:S(2)}) collective-permute-start(bf16[64,512]{1,0:T(8,128)(2,1)S(1)} %get-tuple-element.34), channel_id=1, source_target_pairs={{0,64},{16,80},{32,96},{48,112},{64,0},{80,16},{96,32},{112,48},{1... | collective-permute-start | bytes 196616 | tf_op jit(solution)/shard_map/ppermute | solution.py:39
  22.4 13.7 %collective-permute-start = (bf16[64,512]{1,0:T(8,128)(2,1)S(1)}, bf16[64,512]{1,0:T(8,128)(2,1)S(1)}, u32[]{:S(2)}, u32[]{:S(2)}) collective-permute-start(bf16[64,512]{1,0:T(8,128)(2,1)S(1)} %get-tuple-element.35), channel_id=1, source_target_pairs={{0,8},{2,10},{4,12},{6,14},{8,0},{10,2},{12,4},{14,6},{1,9},{3,11}... | collective-permute-start | bytes 196616 | tf_op jit(solution)/shard_map/ppermute | solution.py:39
  29.2 13.8 %collective-permute-start.7 = (bf16[28,16,128]{2,1,0:T(8,128)(2,1)S(1)}, bf16[28,16,128]{2,1,0:T(8,128)(2,1)S(1)}, u32[]{:S(2)}, u32[]{:S(2)}) collective-permute-start(bf16[28,16,128]{2,1,0:T(8,128)(2,1)S(1)} %pad_maximum_fusion.8), channel_id=1, source_target_pairs={{0,32},{16,48},{32,0},{48,16},{64,96},{80,112},{96,64},{112,80},{1... | collective-permute-start | bytes 344072 | tf_op jit(solution)/shard_map/ppermute | solution.py:39
  33.6 11.5 %collective-permute-start.4 = (bf16[128,512]{1,0:T(8,128)(2,1)S(1)}, bf16[128,512]{1,0:T(8,128)(2,1)S(1)}, u32[]{:S(2)}, u32[]{:S(2)}) collective-permute-start(bf16[128,512]{1,0:T(8,128)(2,1)S(1)} %pad_maximum_fusion.7), channel_id=1, source_target_pairs={{0,32},{16,48},{32,0},{48,16},{64,96},{80,112},{96,64},{112,80},{1... | collective-permute-start | bytes 393224 | tf_op jit(solution)/shard_map/ppermute | solution.py:39
  36.1 13.0 %collective-permute-start.1 = (bf16[128,512]{1,0:T(8,128)(2,1)S(1)}, bf16[128,512]{1,0:T(8,128)(2,1)S(1)}, u32[]{:S(2)}, u32[]{:S(2)}) collective-permute-start(bf16[128,512]{1,0:T(8,128)(2,1)S(1)} %pad_maximum_fusion.6), channel_id=1, source_target_pairs={{0,4},{2,6},{4,0},{6,2},{8,12},{10,14},{12,8},{14,10},{1,5},{3,7},... | collective-permute-start | bytes 393224 | tf_op jit(solution)/shard_map/ppermute | solution.py:39
  43.1 10.1 %collective-permute-start.8 = (bf16[56,16,128]{2,1,0:T(8,128)(2,1)S(1)}, bf16[56,16,128]{2,1,0:T(8,128)(2,1)S(1)}, u32[]{:S(2)}, u32[]{:S(2)}) collective-permute-start(bf16[56,16,128]{2,1,0:T(8,128)(2,1)S(1)} %pad_maximum_fusion.5), channel_id=1, source_target_pairs={{0,16},{16,0},{32,48},{48,32},{64,80},{80,64},{96,112},{112,96},{1... | collective-permute-start | bytes 688136 | tf_op jit(solution)/shard_map/ppermute | solution.py:39
  45.1 11.5 %collective-permute-start.5 = (bf16[256,512]{1,0:T(8,128)(2,1)S(1)}, bf16[256,512]{1,0:T(8,128)(2,1)S(1)}, u32[]{:S(2)}, u32[]{:S(2)}) collective-permute-start(bf16[256,512]{1,0:T(8,128)(2,1)S(1)} %pad_maximum_fusion.4), channel_id=1, source_target_pairs={{0,16},{16,0},{32,48},{48,32},{64,80},{80,64},{96,112},{112,96},{1... | collective-permute-start | bytes 786440 | tf_op jit(solution)/shard_map/ppermute | solution.py:39
  49.0 8.3 %collective-permute-start.2 = (bf16[256,512]{1,0:T(8,128)(2,1)S(1)}, bf16[256,512]{1,0:T(8,128)(2,1)S(1)}, u32[]{:S(2)}, u32[]{:S(2)}) collective-permute-start(bf16[256,512]{1,0:T(8,128)(2,1)S(1)} %pad_maximum_fusion.3), channel_id=1, source_target_pairs={{0,2},{2,0},{4,6},{6,4},{8,10},{10,8},{12,14},{14,12},{1,3},{3,1},... | collective-permute-start | bytes 786440 | tf_op jit(solution)/shard_map/ppermute | solution.py:39
  56.7 62.7 %copy-start = (bf16[512,512]{1,0:T(8,128)(2,1)}, bf16[512,512]{1,0:T(8,128)(2,1)S(1)}, u32[]{:S(2)}) copy-start(bf16[512,512]{1,0:T(8,128)(2,1)S(1)} %pad_maximum_fusion.1.refs_8_) | copy-start | bytes 1572868
  57.4 62.0 %copy-start.1 = (bf16[512,512]{1,0:T(8,128)(2,1)}, bf16[512,512]{1,0:T(8,128)(2,1)S(1)}, u32[]{:S(2)}) copy-start(bf16[512,512]{1,0:T(8,128)(2,1)S(1)} %pad_maximum_fusion.refs_0_) | copy-start | bytes 1572868
  57.4 18.8 %collective-permute-start.9 = (bf16[512,512]{1,0:T(8,128)(2,1)S(1)}, bf16[512,512]{1,0:T(8,128)(2,1)S(1)}, u32[]{:S(2)}, u32[]{:S(2)}) collective-permute-start(bf16[512,512]{1,0:T(8,128)(2,1)S(1)} %pad_maximum_fusion.refs_0_), channel_id=1, source_target_pairs={{0,16},{16,32},{32,48},{48,64},{64,80},{80,96},{96,112},{112,0},{1... | collective-permute-start | bytes 1572872 | tf_op jit(solution)/shard_map/ppermute | solution.py:34
  60.2 17.9 %collective-permute-start.16 = (bf16[512,512]{1,0:T(8,128)(2,1)S(1)}, bf16[512,512]{1,0:T(8,128)(2,1)S(1)}, u32[]{:S(2)}, u32[]{:S(2)}) collective-permute-start(bf16[512,512]{1,0:T(8,128)(2,1)S(1)} %pad_maximum_fusion.1.refs_8_), channel_id=1, source_target_pairs={{0,2},{2,4},{4,6},{6,8},{8,10},{10,12},{12,14},{14,0},{1,3},{3,5},... | collective-permute-start | bytes 1572872 | tf_op jit(solution)/shard_map/ppermute | solution.py:34
  62.8 17.9 %collective-permute-start.13 = (bf16[512,512]{1,0:T(8,128)(2,1)S(1)}, bf16[512,512]{1,0:T(8,128)(2,1)S(1)}, u32[]{:S(2)}, u32[]{:S(2)}) collective-permute-start(bf16[512,512]{1,0:T(8,128)(2,1)S(1)} %pad_maximum_fusion.refs_0_), channel_id=1, source_target_pairs={{0,112},{16,0},{32,16},{48,32},{64,48},{80,64},{96,80},{112,96},{1... | collective-permute-start | bytes 1572872 | tf_op jit(solution)/shard_map/ppermute | solution.py:34
  70.0 15.9 %collective-permute-start.20 = (bf16[512,512]{1,0:T(8,128)(2,1)S(1)}, bf16[512,512]{1,0:T(8,128)(2,1)S(1)}, u32[]{:S(2)}, u32[]{:S(2)}) collective-permute-start(bf16[512,512]{1,0:T(8,128)(2,1)S(1)} %pad_maximum_fusion.1.refs_8_), channel_id=1, source_target_pairs={{0,14},{2,0},{4,2},{6,4},{8,6},{10,8},{12,10},{14,12},{1,15},{3,1}... | collective-permute-start | bytes 1572872 | tf_op jit(solution)/shard_map/ppermute | solution.py:34
  76.2 43.2 %copy-start.8 = (bf16[512,512]{1,0:T(8,128)(2,1)}, bf16[512,512]{1,0:T(8,128)(2,1)S(1)}, u32[]{:S(2)}) copy-start(bf16[512,512]{1,0:T(8,128)(2,1)S(1)} %collective-permute-done.9.refs_1_) | copy-start | bytes 1572868
  76.2 14.9 %collective-permute-start.10 = (bf16[512,512]{1,0:T(8,128)(2,1)S(1)}, bf16[512,512]{1,0:T(8,128)(2,1)S(1)}, u32[]{:S(2)}, u32[]{:S(2)}) collective-permute-start(bf16[512,512]{1,0:T(8,128)(2,1)S(1)} %collective-permute-done.9.refs_1_), channel_id=1, source_target_pairs={{0,16},{16,32},{32,48},{48,64},{64,80},{80,96},{96,112},{112,0},{1... | collective-permute-start | bytes 1572872 | tf_op jit(solution)/shard_map/ppermute | solution.py:34
  78.1 14.9 %collective-permute-start.17 = (bf16[512,512]{1,0:T(8,128)(2,1)S(1)}, bf16[512,512]{1,0:T(8,128)(2,1)S(1)}, u32[]{:S(2)}, u32[]{:S(2)}) collective-permute-start(bf16[512,512]{1,0:T(8,128)(2,1)S(1)} %collective-permute-done.16.refs_9_), channel_id=1, source_target_pairs={{0,2},{2,4},{4,6},{6,8},{8,10},{10,12},{12,14},{14,0},{1,3},{3,5},... | collective-permute-start | bytes 1572872 | tf_op jit(solution)/shard_map/ppermute | solution.py:34
  80.7 14.9 %collective-permute-start.14 = (bf16[512,512]{1,0:T(8,128)(2,1)S(1)}, bf16[512,512]{1,0:T(8,128)(2,1)}, u32[]{:S(2)}, u32[]{:S(2)}) collective-permute-start(bf16[512,512]{1,0:T(8,128)(2,1)S(1)} %collective-permute-done.13.refs_4_), channel_id=1, source_target_pairs={{0,112},{16,0},{32,16},{48,32},{64,48},{80,64},{96,80},{112,96},{1... | collective-permute-start | bytes 1572872 | tf_op jit(solution)/shard_map/ppermute | solution.py:34
  85.9 14.9 %collective-permute-start.21 = (bf16[512,512]{1,0:T(8,128)(2,1)S(1)}, bf16[512,512]{1,0:T(8,128)(2,1)}, u32[]{:S(2)}, u32[]{:S(2)}) collective-permute-start(bf16[512,512]{1,0:T(8,128)(2,1)S(1)} %collective-permute-done.20.refs_12_), channel_id=1, source_target_pairs={{0,14},{2,0},{4,2},{6,4},{8,6},{10,8},{12,10},{14,12},{1,15},{3,1}... | collective-permute-start | bytes 1572872 | tf_op jit(solution)/shard_map/ppermute | solution.py:34
  91.1 14.1 %collective-permute-start.11 = (bf16[512,512]{1,0:T(8,128)(2,1)S(1)}, bf16[512,512]{1,0:T(8,128)(2,1)}, u32[]{:S(2)}, u32[]{:S(2)}) collective-permute-start(bf16[512,512]{1,0:T(8,128)(2,1)S(1)} %collective-permute-done.10.refs_2_), channel_id=1, source_target_pairs={{0,16},{16,32},{32,48},{48,64},{64,80},{80,96},{96,112},{112,0},{1... | collective-permute-start | bytes 1572872 | tf_op jit(solution)/shard_map/ppermute | solution.py:34
  93.1 14.1 %collective-permute-start.18 = (bf16[512,512]{1,0:T(8,128)(2,1)S(1)}, bf16[512,512]{1,0:T(8,128)(2,1)}, u32[]{:S(2)}, u32[]{:S(2)}) collective-permute-start(bf16[512,512]{1,0:T(8,128)(2,1)S(1)} %collective-permute-done.17.refs_10_), channel_id=1, source_target_pairs={{0,2},{2,4},{4,6},{6,8},{8,10},{10,12},{12,14},{14,0},{1,3},{3,5},... | collective-permute-start | bytes 1572872 | tf_op jit(solution)/shard_map/ppermute | solution.py:34
  95.7 18.6 %collective-permute-start.15 = (bf16[512,512]{1,0:T(8,128)(2,1)}, bf16[512,512]{1,0:T(8,128)(2,1)}, u32[]{:S(2)}, u32[]{:S(2)}) collective-permute-start(bf16[512,512]{1,0:T(8,128)(2,1)} %collective-permute-done.14.refs_5_), channel_id=1, source_target_pairs={{0,112},{16,0},{32,16},{48,32},{64,48},{80,64},{96,80},{112,96},{1... | collective-permute-start | bytes 1572872 | tf_op jit(solution)/shard_map/ppermute | solution.py:34
  100.8 13.5 %collective-permute-start.22 = (bf16[512,512]{1,0:T(8,128)(2,1)}, bf16[512,512]{1,0:T(8,128)(2,1)}, u32[]{:S(2)}, u32[]{:S(2)}) collective-permute-start(bf16[512,512]{1,0:T(8,128)(2,1)} %collective-permute-done.21.refs_13_), channel_id=1, source_target_pairs={{0,14},{2,0},{4,2},{6,4},{8,6},{10,8},{12,10},{14,12},{1,15},{3,1}... | collective-permute-start | bytes 1572872 | tf_op jit(solution)/shard_map/ppermute | solution.py:34
  105.3 13.4 %collective-permute-start.12 = (bf16[512,512]{1,0:T(8,128)(2,1)}, bf16[512,512]{1,0:T(8,128)(2,1)}, u32[]{:S(2)}, u32[]{:S(2)}) collective-permute-start(bf16[512,512]{1,0:T(8,128)(2,1)} %collective-permute-done.11.refs_3_), channel_id=1, source_target_pairs={{0,16},{16,32},{32,48},{48,64},{64,80},{80,96},{96,112},{112,0},{1... | collective-permute-start | bytes 1572872 | tf_op jit(solution)/shard_map/ppermute | solution.py:34
  107.2 12.2 %collective-permute-start.19 = (bf16[512,512]{1,0:T(8,128)(2,1)}, bf16[512,512]{1,0:T(8,128)(2,1)}, u32[]{:S(2)}, u32[]{:S(2)}) collective-permute-start(bf16[512,512]{1,0:T(8,128)(2,1)} %collective-permute-done.18.refs_11_), channel_id=1, source_target_pairs={{0,2},{2,4},{4,6},{6,8},{8,10},{10,12},{12,14},{14,0},{1,3},{3,5},... | collective-permute-start | bytes 1572872 | tf_op jit(solution)/shard_map/ppermute | solution.py:34
  127.5 24.1 %collective-permute-start.23 = (bf16[1024,4096]{1,0:T(8,128)(2,1)}, bf16[1024,4096]{1,0:T(8,128)(2,1)}, u32[]{:S(2)}, u32[]{:S(2)}) collective-permute-start(bf16[1024,4096]{1,0:T(8,128)(2,1)} %join.1.own_ref), channel_id=1, source_target_pairs={{0,128},{128,0},{1,129},{129,1},{2,130},{130,2},{3,131},{131,3},{4... | collective-permute-start | bytes 25165832 | tf_op jit(solution)/shard_map/ppermute | solution.py:39
  148.0 3.6 %collective-permute-start.25 = (bf16[144,144]{1,0:T(8,128)(2,1)S(1)}, bf16[144,144]{1,0:T(8,128)(2,1)S(1)}, u32[]{:S(2)}, u32[]{:S(2)}) collective-permute-start(bf16[144,144]{1,0:T(8,128)(2,1)S(1)} %reshape.32.raw_ref), channel_id=1, source_target_pairs={{256,1},{257,0},{258,3},{259,2},{260,5},{261,4},{262,7},{263,6},{2... | collective-permute-start | bytes 124424 | tf_op jit(solution)/shard_map/ppermute | solution.py:409
  161.2 12.8 %collective-permute-start.26 = (bf16[144,1024]{1,0:T(8,128)(2,1)}, bf16[144,1024]{1,0:T(8,128)(2,1)S(1)}, u32[]{:S(2)}, u32[]{:S(2)}) collective-permute-start(bf16[144,1024]{1,0:T(8,128)(2,1)} %early.3), channel_id=1, source_target_pairs={{0,257},{1,256},{2,259},{3,258},{4,261},{5,260},{6,263},{7,262},{8... | collective-permute-start | bytes 884744 | tf_op jit(solution)/shard_map/ppermute | solution.py:409
  171.7 9.1 %collective-permute-start.24 = (bf16[144,1024]{1,0:T(8,128)(2,1)}, bf16[144,1024]{1,0:T(8,128)(2,1)S(1)}, u32[]{:S(2)}, u32[]{:S(2)}) collective-permute-start(bf16[144,1024]{1,0:T(8,128)(2,1)} %early.2), channel_id=1, source_target_pairs={{0,257},{1,256},{2,259},{3,258},{4,261},{5,260},{6,263},{7,262},{8... | collective-permute-start | bytes 884744 | tf_op jit(solution)/shard_map/ppermute | solution.py:409
  194.9 9.4 %collective-permute-start.27 = (bf16[2,144,144]{2,1,0:T(8,128)(2,1)}, bf16[2,144,144]{2,1,0:T(8,128)(2,1)S(1)}, u32[]{:S(2)}, u32[]{:S(2)}) collective-permute-start(bf16[2,144,144]{2,1,0:T(8,128)(2,1)} %get-tuple-element.26), channel_id=1, source_target_pairs={{256,1},{257,0},{258,3},{259,2},{260,5},{261,4},{262,7},{263,6},{2... | collective-permute-start | bytes 248840 | tf_op jit(solution)/shard_map/ppermute | solution.py:409
  196.5 7.8 %collective-permute-start.28 = (bf16[144,144]{1,0:T(8,128)(2,1)}, bf16[144,144]{1,0:T(8,128)(2,1)S(1)}, u32[]{:S(2)}, u32[]{:S(2)}) collective-permute-start(bf16[144,144]{1,0:T(8,128)(2,1)} %get-tuple-element.27), channel_id=1, source_target_pairs={{0,1},{1,0},{2,3},{3,2},{4,5},{5,4},{6,7},{7,6},{8,9},{9,8},{10,11... | collective-permute-start | bytes 124424 | tf_op jit(solution)/shard_map/ppermute | solution.py:39
  (11 other events, 183.8 us)

commit v3 on v2

--- a/solution.py
+++ b/solution.py
@@ -62,7 +62,7 @@
         place = (lax.rem(step, 2) * 4) | (step & 2) | lax.div(step, 4)
         blocks.append(place * 2 * LW)
     for shard in range(16):
-        window = jnp.maximum(table[z * 16 + shard], 0)
+        window = jnp.maximum(table[(z * 16 + shard) ^ where[4]], 0)
         first = first_row(window)
         block = jnp.int32(0)
         for start, at in zip(starts, blocks):
@@ -74,7 +74,7 @@
 
 
 def pick_kernel(where, bands, table, came_ref, out_ref):
-    window = table[where[0]]
+    window = table[where[0] ^ where[4]]
     first = first_row(window)
     out_ref[...] = jnp.zeros_like(out_ref)
     count_rows = jnp.where(window >= 0, WIN_ROWS, 0)
@@ -91,7 +91,7 @@
 
 
 def unpick_kernel(where, bands, table, rows_ref, out_ref):
-    first = first_row(table[where[0]])
+    first = first_row(table[where[0] ^ where[4]])
 
     def band(i, row):
         out_ref[2 * i] = rows_ref[jnp.clip(row, 0, WIN_ROWS - 1)]
@@ -111,8 +111,9 @@
     out_ref[...] = jnp.zeros_like(out_ref)
 
     def shard(j, carry):
-        window = jnp.maximum(table[j], 0)
-        line = jnp.where(table[j] >= 0, seventh(window), -2)
+        held = table[j ^ where[4]]
+        window = jnp.maximum(held, 0)
+        line = jnp.where(held >= 0, seventh(window), -2)
         column = window - LW * seventh(window)
         out_ref[jnp.where(line == across, column, 2 * LW)] = came_ref[2 * j]
         out_ref[jnp.where(line == across_next, LW + column, 2 * LW)] = came_ref[2 * j + 1]
@@ -178,7 +179,8 @@
 
 def gather_section(weight, pos, rows, gains, pack):
     mine = weight[0].T
-    pair = lax.all_gather(mine, "xl", axis=0, tiled=True)
+    theirs, is_left = swap(mine, "xl", 1), lax.axis_index("xl") == 0
+    pair = jnp.concatenate([jnp.where(is_left, mine, theirs), jnp.where(is_left, theirs, mine)])
     pair, gains = lax.optimization_barrier((pair, gains))
     a, b = pair[:, :512], pair[:, 512:]
     for bit in DOUBLING:
@@ -325,7 +327,7 @@
 
 
 def inside(pos, bands, table, token):
-    window = table[pos[0]]
+    window = table[pos[0] ^ pos[4]]
     row = first_row(window) + lax.rem(lax.div(token, WIN_COLS), WIN_ROWS)
     return (window >= 0) & (row >= 0) & (row < 3 * bands.shape[0] // 2)
 
@@ -417,9 +419,7 @@
     pos = jnp.stack([lax.axis_index(LAT), lax.axis_index("z"), lax.axis_index("y"), core, late])
     lat_count = band_rows.shape[0]
     width = embed_weight.shape[1]
-    turned = window_table.reshape(-1, 2)[:, ::-1].reshape(-1)
-    table = jnp.where(is_late, turned, window_table)
-    scalars = (pos, band_rows, table)
+    scalars = (pos, band_rows, window_table)
 
     gains = lax.all_gather(norm_gain, "c", axis=0, tiled=True)
     own, message, gains = gather_section(
@@ -435,8 +435,7 @@
     own_raw = from_rows(raw_rows[:WIN_ROWS])
     far_raw = crossed(own_raw, (2, 3))
 
-    came = []
-    for raw in (own_raw, far_raw):
+    def early(raw):
         [hidden] = sections_call(
             early_kernel,
             [(WTOK, width)],
@@ -446,7 +445,10 @@
             other,
             "early",
         )
-        came.append(crossed(hidden, (0, 1)))
+        return hidden
+
+    too = crossed(early(far_raw), (0, 1))
+    came = [crossed(early(own_raw), (0, 1)), too]
     given, out, rows = sections_call(
         late_kernel,
         [(2, WTOK, FEAT), (WTOK, FEAT), (WTOK, FEAT)],

time: 253 us -> 250 us (0.988)
  blocking collectives: 59.6 us -> 53.6 us
    all_gather x1 -> x0, blocking collectives: 5.15 us -> none  [gather_section(): pair = lax.all_gather(mine, 'xl', axis=0, tiled=True)]
    ppermute x14, waiting for transfers between devices: 11.2 us -> 14.7 us  [ring(): return lax.ppermute(value, axis, [(i, (i + by) % n) for i in range(n)])]
    ppermute x11 -> x12, starting transfers between devices: 47.1 us -> 50.4 us  [swap(): return lax.ppermute(value, axis, [(i, i ^ bit) for i in range(n)])]
    ppermute x11 -> x12, waiting for transfers between devices: 9.34 us -> 7.93 us  [swap(): return lax.ppermute(value, axis, [(i, i ^ bit) for i in range(n)])]
  transfers between devices with their start and end apart: 29 -> 30, of which waited for: 13 -> 13; matrix products, arithmetic and copies ran while one was open for 2% -> 2% of each run, Pallas kernels for 5% -> 5%
where the time goes in v3:
time: 250 us; the launch traced here: 249 us
  starting transfers between devices  101 us (40%)
  blocking collectives  53.6 us (21%)
  Pallas kernels  49.5 us (20%)
  waiting for transfers between devices  31.7 us (13%)
  local copies, waits for them, and re-layouts  8.27 us (3%)
  other arithmetic  3.38 us (1%)
    ppermute x12, starting transfers between devices, swap(): return lax.ppermute(value, axis, [(i, i ^ bit) for i in range(n)])  50.4 us
    ppermute x14, starting transfers between devices, ring(): return lax.ppermute(value, axis, [(i, (i + by) % n) for i in range(n)])  44.3 us
    all_to_all x1, blocking collectives, per_device(): came_back = lax.all_to_all(reply, LAT, 0, 0, tiled=True)  37.7 us
    pallas_call x3, Pallas kernels, sections_call(): pl.pallas_call(body, out_shape=tuple((jax.ShapeDtypeStruct(shape, BF) for...  31.2 us
    ppermute x14, waiting for transfers between devices, ring(): return lax.ppermute(value, axis, [(i, (i + by) % n) for i in range(n)])  14.7 us
    all_to_all x1, blocking collectives, per_device(): arrived = lax.all_to_all(message, ('y', 'xl'), 0, 0, tiled=True)  13.9 us
    pallas_call x4, Pallas kernels, small_call(): pl.pallas_call(body, out_shape=jax.ShapeDtypeStruct((out_rows, PACK, 128)...  10.2 us
    ppermute x4, waiting for transfers between devices, crossed(): return lax.ppermute(value, ('xh', 'xl'), [(x, 3 - x) for x in sources])  9.12 us
  transfers between devices with their start and end apart: 30, of which 13 were waited for; matrix products, arithmetic and copies ran while one was open for 2% of the time, Pallas kernels for 5%

profile of v3, /device:TPU:12, one launch (start us, length us, event | category | flops | bytes accessed | tf_op | source)
XLA Modules:
  0.0 248.6 jit_solution(14697306288298930433)
XLA Ops:
  0.6 3.1 %collective-permute-start = (bf16[32,1024]{1,0:T(8,128)(2,1)}, bf16[32,1024]{1,0:T(8,128)(2,1)S(1)}, u32[]{:S(2)}, u32[]{:S(2)}) collective-permute-start(bf16[32,1024]{1,0:T(8,128)(2,1)} %bitcast.49), channel_id=1, source_target_pairs={{0,1},{1,0},{2,3},{3,2},{4,5},{5,4},{6,7},{7,6},{8,9},{9,8},{10,11... | collective-permute-start | bytes 196616 | tf_op jit(solution)/shard_map/ppermute | solution.py:39
  4.9 10.9 %collective-permute-start.7 = (bf16[14,16,128]{2,1,0:T(8,128)(2,1)S(1)}, bf16[14,16,128]{2,1,0:T(8,128)(2,1)S(1)}, u32[]{:S(2)}, u32[]{:S(2)}) collective-permute-start(bf16[14,16,128]{2,1,0:T(8,128)(2,1)S(1)} %slice.38), channel_id=1, source_target_pairs={{0,64},{16,80},{32,96},{48,112},{64,0},{80,16},{96,32},{112,48},{1... | collective-permute-start | bytes 172040 | tf_op jit(solution)/shard_map/ppermute | solution.py:39
  21.3 4.3 %collective-permute-start.8 = (bf16[28,16,128]{2,1,0:T(8,128)(2,1)S(1)}, bf16[28,16,128]{2,1,0:T(8,128)(2,1)S(1)}, u32[]{:S(2)}, u32[]{:S(2)}) collective-permute-start(bf16[28,16,128]{2,1,0:T(8,128)(2,1)S(1)} %pad_maximum_fusion.9), channel_id=1, source_target_pairs={{0,32},{16,48},{32,0},{48,16},{64,96},{80,112},{96,64},{112,80},{1... | collective-permute-start | bytes 344072 | tf_op jit(solution)/shard_map/ppermute | solution.py:39
  25.6 6.8 %collective-permute-start.1 = (bf16[64,512]{1,0:T(8,128)(2,1)S(1)}, bf16[64,512]{1,0:T(8,128)(2,1)S(1)}, u32[]{:S(2)}, u32[]{:S(2)}) collective-permute-start(bf16[64,512]{1,0:T(8,128)(2,1)S(1)} %get-tuple-element.35), channel_id=1, source_target_pairs={{0,8},{2,10},{4,12},{6,14},{8,0},{10,2},{12,4},{14,6},{1,9},{3,11}... | collective-permute-start | bytes 196616 | tf_op jit(solution)/shard_map/ppermute | solution.py:39
  32.4 2.6 %collective-permute-start.5 = (bf16[128,512]{1,0:T(8,128)(2,1)S(1)}, bf16[128,512]{1,0:T(8,128)(2,1)S(1)}, u32[]{:S(2)}, u32[]{:S(2)}) collective-permute-start(bf16[128,512]{1,0:T(8,128)(2,1)S(1)} %pad_maximum_fusion.8), channel_id=1, source_target_pairs={{0,32},{16,48},{32,0},{48,16},{64,96},{80,112},{96,64},{112,80},{1... | collective-permute-start | bytes 393224 | tf_op jit(solution)/shard_map/ppermute | solution.py:39
  35.6 4.5 %collective-permute-start.2 = (bf16[128,512]{1,0:T(8,128)(2,1)S(1)}, bf16[128,512]{1,0:T(8,128)(2,1)S(1)}, u32[]{:S(2)}, u32[]{:S(2)}) collective-permute-start(bf16[128,512]{1,0:T(8,128)(2,1)S(1)} %pad_maximum_fusion.7), channel_id=1, source_target_pairs={{0,4},{2,6},{4,0},{6,2},{8,12},{10,14},{12,8},{14,10},{1,5},{3,7},... | collective-permute-start | bytes 393224 | tf_op jit(solution)/shard_map/ppermute | solution.py:39
  40.2 3.4 %collective-permute-start.9 = (bf16[56,16,128]{2,1,0:T(8,128)(2,1)S(1)}, bf16[56,16,128]{2,1,0:T(8,128)(2,1)S(1)}, u32[]{:S(2)}, u32[]{:S(2)}) collective-permute-start(bf16[56,16,128]{2,1,0:T(8,128)(2,1)S(1)} %pad_maximum_fusion.5), channel_id=1, source_target_pairs={{0,16},{16,0},{32,48},{48,32},{64,80},{80,64},{96,112},{112,96},{1... | collective-permute-start | bytes 688136 | tf_op jit(solution)/shard_map/ppermute | solution.py:39
  43.6 2.5 collective-permute-start.6
  46.1 3.5 %collective-permute-start.3 = (bf16[256,512]{1,0:T(8,128)(2,1)S(1)}, bf16[256,512]{1,0:T(8,128)(2,1)S(1)}, u32[]{:S(2)}, u32[]{:S(2)}) collective-permute-start(bf16[256,512]{1,0:T(8,128)(2,1)S(1)} %pad_maximum_fusion.3), channel_id=1, source_target_pairs={{0,2},{2,0},{4,6},{6,4},{8,10},{10,8},{12,14},{14,12},{1,3},{3,1},... | collective-permute-start | bytes 786440 | tf_op jit(solution)/shard_map/ppermute | solution.py:39
  50.7 3.2 %collective-permute-done.6 = bf16[256,512]{1,0:T(8,128)(2,1)S(1)} collective-permute-done((bf16[256,512]{1,0:T(8,128)(2,1)S(1)}, bf16[256,512]{1,0:T(8,128)(2,1)S(1)}, u32[]{:S(2)}, u32[]{:S(2)}) %collective-permute-start.6) | collective-permute-done | bytes 262176 | tf_op jit(solution)/shard_map/ppermute | solution.py:39
  55.3 3.2 %collective-permute-start.10 = (bf16[512,512]{1,0:T(8,128)(2,1)S(1)}, bf16[512,512]{1,0:T(8,128)(2,1)S(1)}, u32[]{:S(2)}, u32[]{:S(2)}) collective-permute-start(bf16[512,512]{1,0:T(8,128)(2,1)S(1)} %pad_maximum_fusion.refs_0_), channel_id=1, source_target_pairs={{0,16},{16,32},{32,48},{48,64},{64,80},{80,96},{96,112},{112,0},{1... | collective-permute-start | bytes 1572872 | tf_op jit(solution)/shard_map/ppermute | solution.py:34
  58.5 2.5 collective-permute-start.17
  61.0 5.1 %collective-permute-start.14 = (bf16[512,512]{1,0:T(8,128)(2,1)S(1)}, bf16[512,512]{1,0:T(8,128)(2,1)S(1)}, u32[]{:S(2)}, u32[]{:S(2)}) collective-permute-start(bf16[512,512]{1,0:T(8,128)(2,1)S(1)} %pad_maximum_fusion.refs_0_), channel_id=1, source_target_pairs={{0,112},{16,0},{32,16},{48,32},{64,48},{80,64},{96,80},{112,96},{1... | collective-permute-start | bytes 1572872 | tf_op jit(solution)/shard_map/ppermute | solution.py:34
  66.1 3.9 %collective-permute-start.21 = (bf16[512,512]{1,0:T(8,128)(2,1)S(1)}, bf16[512,512]{1,0:T(8,128)(2,1)S(1)}, u32[]{:S(2)}, u32[]{:S(2)}) collective-permute-start(bf16[512,512]{1,0:T(8,128)(2,1)S(1)} %pad_maximum_fusion.1.refs_8_), channel_id=1, source_target_pairs={{0,14},{2,0},{4,2},{6,4},{8,6},{10,8},{12,10},{14,12},{1,15},{3,1}... | collective-permute-start | bytes 1572872 | tf_op jit(solution)/shard_map/ppermute | solution.py:34
  70.0 3.3 %collective-permute-done.10.refs_1_ = bf16[512,512]{1,0:T(8,128)(2,1)S(1)} collective-permute-done((bf16[512,512]{1,0:T(8,128)(2,1)S(1)}, bf16[512,512]{1,0:T(8,128)(2,1)S(1)}, u32[]{:S(2)}, u32[]{:S(2)}) %collective-permute-start.10) | collective-permute-done | bytes 524320 | tf_op jit(solution)/shard_map/ppermute | solution.py:34
  77.2 5.1 %collective-permute-start.15 = (bf16[512,512]{1,0:T(8,128)(2,1)S(1)}, bf16[512,512]{1,0:T(8,128)(2,1)}, u32[]{:S(2)}, u32[]{:S(2)}) collective-permute-start(bf16[512,512]{1,0:T(8,128)(2,1)S(1)} %collective-permute-done.14.refs_4_), channel_id=1, source_target_pairs={{0,112},{16,0},{32,16},{48,32},{64,48},{80,64},{96,80},{112,96},{1... | collective-permute-start | bytes 1572872 | tf_op jit(solution)/shard_map/ppermute | solution.py:34
  82.3 3.9 %collective-permute-start.22 = (bf16[512,512]{1,0:T(8,128)(2,1)S(1)}, bf16[512,512]{1,0:T(8,128)(2,1)}, u32[]{:S(2)}, u32[]{:S(2)}) collective-permute-start(bf16[512,512]{1,0:T(8,128)(2,1)S(1)} %collective-permute-done.21.refs_12_), channel_id=1, source_target_pairs={{0,14},{2,0},{4,2},{6,4},{8,6},{10,8},{12,10},{14,12},{1,15},{3,1}... | collective-permute-start | bytes 1572872 | tf_op jit(solution)/shard_map/ppermute | solution.py:34
  92.4 5.1 %collective-permute-start.16 = (bf16[512,512]{1,0:T(8,128)(2,1)}, bf16[512,512]{1,0:T(8,128)(2,1)}, u32[]{:S(2)}, u32[]{:S(2)}) collective-permute-start(bf16[512,512]{1,0:T(8,128)(2,1)} %collective-permute-done.15.refs_5_), channel_id=1, source_target_pairs={{0,112},{16,0},{32,16},{48,32},{64,48},{80,64},{96,80},{112,96},{1... | collective-permute-start | bytes 1572872 | tf_op jit(solution)/shard_map/ppermute | solution.py:34
  97.6 3.9 %collective-permute-start.23 = (bf16[512,512]{1,0:T(8,128)(2,1)}, bf16[512,512]{1,0:T(8,128)(2,1)}, u32[]{:S(2)}, u32[]{:S(2)}) collective-permute-start(bf16[512,512]{1,0:T(8,128)(2,1)} %collective-permute-done.22.refs_13_), channel_id=1, source_target_pairs={{0,14},{2,0},{4,2},{6,4},{8,6},{10,8},{12,10},{14,12},{1,15},{3,1}... | collective-permute-start | bytes 1572872 | tf_op jit(solution)/shard_map/ppermute | solution.py:34
  110.5 6.2 %collective-permute-done.13.refs_7_ = bf16[512,512]{1,0:T(8,128)(2,1)} collective-permute-done((bf16[512,512]{1,0:T(8,128)(2,1)}, bf16[512,512]{1,0:T(8,128)(2,1)}, u32[]{:S(2)}, u32[]{:S(2)}) %collective-permute-start.13) | collective-permute-done | bytes 524320 | tf_op jit(solution)/shard_map/ppermute | solution.py:34
  117.5 8.1 %join.1.own_ref = bf16[1024,4096]{1,0:T(8,128)(2,1)} custom-call(s32[5]{0:T(128)} %stack.23.where.pos, bf16[512,512]{1,0:T(8,128)(2,1)} %copy-done.1, bf16[512,512]{1,0:T(8,128)(2,1)} %copy-done.8, bf16[512,512]{1,0:T(8,128)(2,1)} %copy-done.12, bf16[512,512]{1,0:T(8,128)(2,1)} %collective-permute-done.12.refs_3_, bf16[512,512]{1,0:T(8,128)(2,1)} %copy-done.10, ...), custom_call_target="tpu_custom_call" | custom-call | flops 10000000000 | bytes 25165824 | tf_op jit(solution)/shard_map/join/pallas_call | solution.py:207
  127.5 13.9 %all_to_all.10.came_ref = bf16[32,16,128]{2,1,0:T(8,128)(2,1)} all-to-all(bf16[32,16,128]{2,1,0:T(8,128)(2,1)S(1)} %copy-done.2), channel_id=1, replica_groups=mesh['xh'=2,'c'=2,'z'=8,'y'=8,'xl'=2] {'y','xl'}, dimensions={0} | all-to-all | bytes 262144 | tf_op jit(solution)/shard_map/all_to_all | solution.py:432
  141.4 2.4 pick.1
  149.2 8.9 %early.3 = bf16[144,1024]{1,0:T(8,128)(2,1)} custom-call(s32[5]{0:T(128)} %stack.23.where.pos, s32[128]{0:T(128)} %bands.13, s32[128]{0:T(128)} %table.13, bf16[144,144]{1,0:T(8,128)(2,1)} %copy-done.7, bf16[144,1024]{1,0:T(8,128)(2,1)} %embed_ref.3, bf16[2,1024]{1,0:T(2,128)(2,1)} %level_ref.3, f32[2,1024]{1,0:T(2,128)} %bitcast.46, ...), custom_call_target="tpu_custom_call" | custom-call | tf_op jit(solution)/shard_map/early/pallas_call | solution.py:386
  159.7 8.9 %early.2 = bf16[144,1024]{1,0:T(8,128)(2,1)} custom-call(s32[5]{0:T(128)} %stack.23.where.pos, s32[128]{0:T(128)} %bands.13, s32[128]{0:T(128)} %table.13, bf16[144,144]{1,0:T(8,128)(2,1)} %copy-done.3, bf16[144,1024]{1,0:T(8,128)(2,1)} %embed_ref.3, bf16[2,1024]{1,0:T(2,128)(2,1)} %level_ref.3, f32[2,1024]{1,0:T(2,128)} %bitcast.47, ...), custom_call_target="tpu_custom_call" | custom-call | tf_op jit(solution)/shard_map/early/pallas_call | solution.py:386
  170.9 7.1 %collective-permute-done.25.came_ref = bf16[144,1024]{1,0:T(8,128)(2,1)S(1)} collective-permute-done((bf16[144,1024]{1,0:T(8,128)(2,1)}, bf16[144,1024]{1,0:T(8,128)(2,1)S(1)}, u32[]{:S(2)}, u32[]{:S(2)}) %collective-permute-start.25) | collective-permute-done | bytes 294944 | tf_op jit(solution)/shard_map/ppermute | solution.py:411
  178.8 13.4 %late.1 = (bf16[2,144,144]{2,1,0:T(8,128)(2,1)}, bf16[144,144]{1,0:T(8,128)(2,1)}, bf16[144,144]{1,0:T(8,128)(2,1)}) custom-call(s32[5]{0:T(128)} %stack.23.where.pos, s32[128]{0:T(128)} %bands.13, s32[128]{0:T(128)} %table.13, bf16[144,1024]{1,0:T(8,128)(2,1)} %copy-done.6, bf16[144,1024]{1,0:T(8,128)(2,1)} %copy-done.5, f32[2,1024]{1,0:T(2,128)} %bitcast.48, ...), custom_call_target="tpu_custom_call" | custom-call | tf_op jit(solution)/shard_map/late/pallas_call | solution.py:386
  193.8 5.0 %collective-permute-start.29 = (bf16[144,144]{1,0:T(8,128)(2,1)}, bf16[144,144]{1,0:T(8,128)(2,1)S(1)}, u32[]{:S(2)}, u32[]{:S(2)}) collective-permute-start(bf16[144,144]{1,0:T(8,128)(2,1)} %get-tuple-element.27), channel_id=1, source_target_pairs={{0,1},{1,0},{2,3},{3,2},{4,5},{5,4},{6,7},{7,6},{8,9},{9,8},{10,11... | collective-permute-start | bytes 124424 | tf_op jit(solution)/shard_map/ppermute | solution.py:39
  198.8 2.5 %collective-permute-done.29 = bf16[144,144]{1,0:T(8,128)(2,1)S(1)} collective-permute-done((bf16[144,144]{1,0:T(8,128)(2,1)}, bf16[144,144]{1,0:T(8,128)(2,1)S(1)}, u32[]{:S(2)}, u32[]{:S(2)}) %collective-permute-start.29) | collective-permute-done | bytes 41504 | tf_op jit(solution)/shard_map/ppermute | solution.py:39
  203.7 2.5 unpick.1
  206.1 37.7 %all_to_all.11.came_ref = bf16[256,16,128]{2,1,0:T(8,128)(2,1)} all-to-all(bf16[256,16,128]{2,1,0:T(8,128)(2,1)} %unpick.1), channel_id=1, replica_groups=mesh['xh'=2,'c'=2,'z'=8,'y'=8,'xl'=2] {'z','y','xl'}, dimensions={0} | all-to-all | bytes 2097152 | tf_op jit(solution)/shard_map/all_to_all | solution.py:464
  243.9 3.0 %unpack.1 = bf16[15,16,128]{2,1,0:T(8,128)(2,1)} custom-call(s32[5]{0:T(128)} %stack.23.where.pos, s32[128]{0:T(128)} %bands.13, s32[128]{0:T(128)} %table.13, bf16[256,16,128]{2,1,0:T(8,128)(2,1)} %all_to_all.11.came_ref), custom_call_target="tpu_custom_call" | custom-call | tf_op jit(solution)/shard_map/unpack/pallas_call | solution.py:401
  (103 shorter events, 46.8 us)
Async XLA Ops:
  0.6 17.8 %collective-permute-start = (bf16[32,1024]{1,0:T(8,128)(2,1)}, bf16[32,1024]{1,0:T(8,128)(2,1)S(1)}, u32[]{:S(2)}, u32[]{:S(2)}) collective-permute-start(bf16[32,1024]{1,0:T(8,128)(2,1)} %bitcast.49), channel_id=1, source_target_pairs={{0,1},{1,0},{2,3},{3,2},{4,5},{5,4},{6,7},{7,6},{8,9},{9,8},{10,11... | collective-permute-start | bytes 196616 | tf_op jit(solution)/shard_map/ppermute | solution.py:39
  4.9 16.3 %collective-permute-start.7 = (bf16[14,16,128]{2,1,0:T(8,128)(2,1)S(1)}, bf16[14,16,128]{2,1,0:T(8,128)(2,1)S(1)}, u32[]{:S(2)}, u32[]{:S(2)}) collective-permute-start(bf16[14,16,128]{2,1,0:T(8,128)(2,1)S(1)} %slice.38), channel_id=1, source_target_pairs={{0,64},{16,80},{32,96},{48,112},{64,0},{80,16},{96,32},{112,48},{1... | collective-permute-start | bytes 172040 | tf_op jit(solution)/shard_map/ppermute | solution.py:39
  19.3 13.1 %collective-permute-start.4 = (bf16[64,512]{1,0:T(8,128)(2,1)S(1)}, bf16[64,512]{1,0:T(8,128)(2,1)S(1)}, u32[]{:S(2)}, u32[]{:S(2)}) collective-permute-start(bf16[64,512]{1,0:T(8,128)(2,1)S(1)} %get-tuple-element.34), channel_id=1, source_target_pairs={{0,64},{16,80},{32,96},{48,112},{64,0},{80,16},{96,32},{112,48},{1... | collective-permute-start | bytes 196616 | tf_op jit(solution)/shard_map/ppermute | solution.py:39
  21.3 18.9 %collective-permute-start.8 = (bf16[28,16,128]{2,1,0:T(8,128)(2,1)S(1)}, bf16[28,16,128]{2,1,0:T(8,128)(2,1)S(1)}, u32[]{:S(2)}, u32[]{:S(2)}) collective-permute-start(bf16[28,16,128]{2,1,0:T(8,128)(2,1)S(1)} %pad_maximum_fusion.9), channel_id=1, source_target_pairs={{0,32},{16,48},{32,0},{48,16},{64,96},{80,112},{96,64},{112,80},{1... | collective-permute-start | bytes 344072 | tf_op jit(solution)/shard_map/ppermute | solution.py:39
  25.6 10.1 %collective-permute-start.1 = (bf16[64,512]{1,0:T(8,128)(2,1)S(1)}, bf16[64,512]{1,0:T(8,128)(2,1)S(1)}, u32[]{:S(2)}, u32[]{:S(2)}) collective-permute-start(bf16[64,512]{1,0:T(8,128)(2,1)S(1)} %get-tuple-element.35), channel_id=1, source_target_pairs={{0,8},{2,10},{4,12},{6,14},{8,0},{10,2},{12,4},{14,6},{1,9},{3,11}... | collective-permute-start | bytes 196616 | tf_op jit(solution)/shard_map/ppermute | solution.py:39
  32.4 11.2 %collective-permute-start.5 = (bf16[128,512]{1,0:T(8,128)(2,1)S(1)}, bf16[128,512]{1,0:T(8,128)(2,1)S(1)}, u32[]{:S(2)}, u32[]{:S(2)}) collective-permute-start(bf16[128,512]{1,0:T(8,128)(2,1)S(1)} %pad_maximum_fusion.8), channel_id=1, source_target_pairs={{0,32},{16,48},{32,0},{48,16},{64,96},{80,112},{96,64},{112,80},{1... | collective-permute-start | bytes 393224 | tf_op jit(solution)/shard_map/ppermute | solution.py:39
  35.6 10.4 %collective-permute-start.2 = (bf16[128,512]{1,0:T(8,128)(2,1)S(1)}, bf16[128,512]{1,0:T(8,128)(2,1)S(1)}, u32[]{:S(2)}, u32[]{:S(2)}) collective-permute-start(bf16[128,512]{1,0:T(8,128)(2,1)S(1)} %pad_maximum_fusion.7), channel_id=1, source_target_pairs={{0,4},{2,6},{4,0},{6,2},{8,12},{10,14},{12,8},{14,10},{1,5},{3,7},... | collective-permute-start | bytes 393224 | tf_op jit(solution)/shard_map/ppermute | solution.py:39
  40.2 9.7 %collective-permute-start.9 = (bf16[56,16,128]{2,1,0:T(8,128)(2,1)S(1)}, bf16[56,16,128]{2,1,0:T(8,128)(2,1)S(1)}, u32[]{:S(2)}, u32[]{:S(2)}) collective-permute-start(bf16[56,16,128]{2,1,0:T(8,128)(2,1)S(1)} %pad_maximum_fusion.5), channel_id=1, source_target_pairs={{0,16},{16,0},{32,48},{48,32},{64,80},{80,64},{96,112},{112,96},{1... | collective-permute-start | bytes 688136 | tf_op jit(solution)/shard_map/ppermute | solution.py:39
  43.6 10.3 %collective-permute-start.6 = (bf16[256,512]{1,0:T(8,128)(2,1)S(1)}, bf16[256,512]{1,0:T(8,128)(2,1)S(1)}, u32[]{:S(2)}, u32[]{:S(2)}) collective-permute-start(bf16[256,512]{1,0:T(8,128)(2,1)S(1)} %pad_maximum_fusion.4), channel_id=1, source_target_pairs={{0,16},{16,0},{32,48},{48,32},{64,80},{80,64},{96,112},{112,96},{1... | collective-permute-start | bytes 786440 | tf_op jit(solution)/shard_map/ppermute | solution.py:39
  46.1 9.1 %collective-permute-start.3 = (bf16[256,512]{1,0:T(8,128)(2,1)S(1)}, bf16[256,512]{1,0:T(8,128)(2,1)S(1)}, u32[]{:S(2)}, u32[]{:S(2)}) collective-permute-start(bf16[256,512]{1,0:T(8,128)(2,1)S(1)} %pad_maximum_fusion.3), channel_id=1, source_target_pairs={{0,2},{2,0},{4,6},{6,4},{8,10},{10,8},{12,14},{14,12},{1,3},{3,1},... | collective-permute-start | bytes 786440 | tf_op jit(solution)/shard_map/ppermute | solution.py:39
  53.9 63.5 %copy-start = (bf16[512,512]{1,0:T(8,128)(2,1)}, bf16[512,512]{1,0:T(8,128)(2,1)S(1)}, u32[]{:S(2)}) copy-start(bf16[512,512]{1,0:T(8,128)(2,1)S(1)} %pad_maximum_fusion.1.refs_8_) | copy-start | bytes 1572868
  55.3 62.2 %copy-start.1 = (bf16[512,512]{1,0:T(8,128)(2,1)}, bf16[512,512]{1,0:T(8,128)(2,1)S(1)}, u32[]{:S(2)}) copy-start(bf16[512,512]{1,0:T(8,128)(2,1)S(1)} %pad_maximum_fusion.refs_0_) | copy-start | bytes 1572868
  55.3 18.0 %collective-permute-start.10 = (bf16[512,512]{1,0:T(8,128)(2,1)S(1)}, bf16[512,512]{1,0:T(8,128)(2,1)S(1)}, u32[]{:S(2)}, u32[]{:S(2)}) collective-permute-start(bf16[512,512]{1,0:T(8,128)(2,1)S(1)} %pad_maximum_fusion.refs_0_), channel_id=1, source_target_pairs={{0,16},{16,32},{32,48},{48,64},{64,80},{80,96},{96,112},{112,0},{1... | collective-permute-start | bytes 1572872 | tf_op jit(solution)/shard_map/ppermute | solution.py:34
  58.5 16.7 %collective-permute-start.17 = (bf16[512,512]{1,0:T(8,128)(2,1)S(1)}, bf16[512,512]{1,0:T(8,128)(2,1)S(1)}, u32[]{:S(2)}, u32[]{:S(2)}) collective-permute-start(bf16[512,512]{1,0:T(8,128)(2,1)S(1)} %pad_maximum_fusion.1.refs_8_), channel_id=1, source_target_pairs={{0,2},{2,4},{4,6},{6,8},{8,10},{10,12},{12,14},{14,0},{1,3},{3,5},... | collective-permute-start | bytes 1572872 | tf_op jit(solution)/shard_map/ppermute | solution.py:34
  61.0 16.2 %collective-permute-start.14 = (bf16[512,512]{1,0:T(8,128)(2,1)S(1)}, bf16[512,512]{1,0:T(8,128)(2,1)S(1)}, u32[]{:S(2)}, u32[]{:S(2)}) collective-permute-start(bf16[512,512]{1,0:T(8,128)(2,1)S(1)} %pad_maximum_fusion.refs_0_), channel_id=1, source_target_pairs={{0,112},{16,0},{32,16},{48,32},{64,48},{80,64},{96,80},{112,96},{1... | collective-permute-start | bytes 1572872 | tf_op jit(solution)/shard_map/ppermute | solution.py:34
  66.1 16.2 %collective-permute-start.21 = (bf16[512,512]{1,0:T(8,128)(2,1)S(1)}, bf16[512,512]{1,0:T(8,128)(2,1)S(1)}, u32[]{:S(2)}, u32[]{:S(2)}) collective-permute-start(bf16[512,512]{1,0:T(8,128)(2,1)S(1)} %pad_maximum_fusion.1.refs_8_), channel_id=1, source_target_pairs={{0,14},{2,0},{4,2},{6,4},{8,6},{10,8},{12,10},{14,12},{1,15},{3,1}... | collective-permute-start | bytes 1572872 | tf_op jit(solution)/shard_map/ppermute | solution.py:34
  73.3 15.3 %collective-permute-start.11 = (bf16[512,512]{1,0:T(8,128)(2,1)S(1)}, bf16[512,512]{1,0:T(8,128)(2,1)S(1)}, u32[]{:S(2)}, u32[]{:S(2)}) collective-permute-start(bf16[512,512]{1,0:T(8,128)(2,1)S(1)} %collective-permute-done.10.refs_1_), channel_id=1, source_target_pairs={{0,16},{16,32},{32,48},{48,64},{64,80},{80,96},{96,112},{112,0},{1... | collective-permute-start | bytes 1572872 | tf_op jit(solution)/shard_map/ppermute | solution.py:34
  75.2 15.2 %collective-permute-start.18 = (bf16[512,512]{1,0:T(8,128)(2,1)S(1)}, bf16[512,512]{1,0:T(8,128)(2,1)S(1)}, u32[]{:S(2)}, u32[]{:S(2)}) collective-permute-start(bf16[512,512]{1,0:T(8,128)(2,1)S(1)} %collective-permute-done.17.refs_9_), channel_id=1, source_target_pairs={{0,2},{2,4},{4,6},{6,8},{8,10},{10,12},{12,14},{14,0},{1,3},{3,5},... | collective-permute-start | bytes 1572872 | tf_op jit(solution)/shard_map/ppermute | solution.py:34
  77.2 15.2 %collective-permute-start.15 = (bf16[512,512]{1,0:T(8,128)(2,1)S(1)}, bf16[512,512]{1,0:T(8,128)(2,1)}, u32[]{:S(2)}, u32[]{:S(2)}) collective-permute-start(bf16[512,512]{1,0:T(8,128)(2,1)S(1)} %collective-permute-done.14.refs_4_), channel_id=1, source_target_pairs={{0,112},{16,0},{32,16},{48,32},{64,48},{80,64},{96,80},{112,96},{1... | collective-permute-start | bytes 1572872 | tf_op jit(solution)/shard_map/ppermute | solution.py:34
  82.3 15.2 %collective-permute-start.22 = (bf16[512,512]{1,0:T(8,128)(2,1)S(1)}, bf16[512,512]{1,0:T(8,128)(2,1)}, u32[]{:S(2)}, u32[]{:S(2)}) collective-permute-start(bf16[512,512]{1,0:T(8,128)(2,1)S(1)} %collective-permute-done.21.refs_12_), channel_id=1, source_target_pairs={{0,14},{2,0},{4,2},{6,4},{8,6},{10,8},{12,10},{14,12},{1,15},{3,1}... | collective-permute-start | bytes 1572872 | tf_op jit(solution)/shard_map/ppermute | solution.py:34
  88.5 14.4 %collective-permute-start.12 = (bf16[512,512]{1,0:T(8,128)(2,1)S(1)}, bf16[512,512]{1,0:T(8,128)(2,1)}, u32[]{:S(2)}, u32[]{:S(2)}) collective-permute-start(bf16[512,512]{1,0:T(8,128)(2,1)S(1)} %collective-permute-done.11.refs_2_), channel_id=1, source_target_pairs={{0,16},{16,32},{32,48},{48,64},{64,80},{80,96},{96,112},{112,0},{1... | collective-permute-start | bytes 1572872 | tf_op jit(solution)/shard_map/ppermute | solution.py:34
  90.5 14.4 %collective-permute-start.19 = (bf16[512,512]{1,0:T(8,128)(2,1)S(1)}, bf16[512,512]{1,0:T(8,128)(2,1)}, u32[]{:S(2)}, u32[]{:S(2)}) collective-permute-start(bf16[512,512]{1,0:T(8,128)(2,1)S(1)} %collective-permute-done.18.refs_10_), channel_id=1, source_target_pairs={{0,2},{2,4},{4,6},{6,8},{8,10},{10,12},{12,14},{14,0},{1,3},{3,5},... | collective-permute-start | bytes 1572872 | tf_op jit(solution)/shard_map/ppermute | solution.py:34
  92.4 17.4 %collective-permute-start.16 = (bf16[512,512]{1,0:T(8,128)(2,1)}, bf16[512,512]{1,0:T(8,128)(2,1)}, u32[]{:S(2)}, u32[]{:S(2)}) collective-permute-start(bf16[512,512]{1,0:T(8,128)(2,1)} %collective-permute-done.15.refs_5_), channel_id=1, source_target_pairs={{0,112},{16,0},{32,16},{48,32},{64,48},{80,64},{96,80},{112,96},{1... | collective-permute-start | bytes 1572872 | tf_op jit(solution)/shard_map/ppermute | solution.py:34
  97.6 12.9 %collective-permute-start.23 = (bf16[512,512]{1,0:T(8,128)(2,1)}, bf16[512,512]{1,0:T(8,128)(2,1)}, u32[]{:S(2)}, u32[]{:S(2)}) collective-permute-start(bf16[512,512]{1,0:T(8,128)(2,1)} %collective-permute-done.22.refs_13_), channel_id=1, source_target_pairs={{0,14},{2,0},{4,2},{6,4},{8,6},{10,8},{12,10},{14,12},{1,15},{3,1}... | collective-permute-start | bytes 1572872 | tf_op jit(solution)/shard_map/ppermute | solution.py:34
  103.0 13.7 %collective-permute-start.13 = (bf16[512,512]{1,0:T(8,128)(2,1)}, bf16[512,512]{1,0:T(8,128)(2,1)}, u32[]{:S(2)}, u32[]{:S(2)}) collective-permute-start(bf16[512,512]{1,0:T(8,128)(2,1)} %collective-permute-done.12.refs_3_), channel_id=1, source_target_pairs={{0,16},{16,32},{32,48},{48,64},{64,80},{80,96},{96,112},{112,0},{1... | collective-permute-start | bytes 1572872 | tf_op jit(solution)/shard_map/ppermute | solution.py:34
  104.9 12.5 %collective-permute-start.20 = (bf16[512,512]{1,0:T(8,128)(2,1)}, bf16[512,512]{1,0:T(8,128)(2,1)}, u32[]{:S(2)}, u32[]{:S(2)}) collective-permute-start(bf16[512,512]{1,0:T(8,128)(2,1)} %collective-permute-done.19.refs_11_), channel_id=1, source_target_pairs={{0,2},{2,4},{4,6},{6,8},{8,10},{10,12},{12,14},{14,0},{1,3},{3,5},... | collective-permute-start | bytes 1572872 | tf_op jit(solution)/shard_map/ppermute | solution.py:34
  125.6 22.9 %collective-permute-start.24 = (bf16[1024,4096]{1,0:T(8,128)(2,1)}, bf16[1024,4096]{1,0:T(8,128)(2,1)}, u32[]{:S(2)}, u32[]{:S(2)}) collective-permute-start(bf16[1024,4096]{1,0:T(8,128)(2,1)} %join.1.own_ref), channel_id=1, source_target_pairs={{0,128},{128,0},{1,129},{129,1},{2,130},{130,2},{3,131},{131,3},{4... | collective-permute-start | bytes 25165832 | tf_op jit(solution)/shard_map/ppermute | solution.py:39
  144.8 3.7 %collective-permute-start.26 = (bf16[144,144]{1,0:T(8,128)(2,1)S(1)}, bf16[144,144]{1,0:T(8,128)(2,1)S(1)}, u32[]{:S(2)}, u32[]{:S(2)}) collective-permute-start(bf16[144,144]{1,0:T(8,128)(2,1)S(1)} %reshape.24.raw_ref), channel_id=1, source_target_pairs={{256,1},{257,0},{258,3},{259,2},{260,5},{261,4},{262,7},{263,6},{2... | collective-permute-start | bytes 124424 | tf_op jit(solution)/shard_map/ppermute | solution.py:411
  158.1 12.8 %collective-permute-start.27 = (bf16[144,1024]{1,0:T(8,128)(2,1)}, bf16[144,1024]{1,0:T(8,128)(2,1)S(1)}, u32[]{:S(2)}, u32[]{:S(2)}) collective-permute-start(bf16[144,1024]{1,0:T(8,128)(2,1)} %early.3), channel_id=1, source_target_pairs={{0,257},{1,256},{2,259},{3,258},{4,261},{5,260},{6,263},{7,262},{8... | collective-permute-start | bytes 884744 | tf_op jit(solution)/shard_map/ppermute | solution.py:411
  168.6 9.5 %collective-permute-start.25 = (bf16[144,1024]{1,0:T(8,128)(2,1)}, bf16[144,1024]{1,0:T(8,128)(2,1)S(1)}, u32[]{:S(2)}, u32[]{:S(2)}) collective-permute-start(bf16[144,1024]{1,0:T(8,128)(2,1)} %early.2), channel_id=1, source_target_pairs={{0,257},{1,256},{2,259},{3,258},{4,261},{5,260},{6,263},{7,262},{8... | collective-permute-start | bytes 884744 | tf_op jit(solution)/shard_map/ppermute | solution.py:411
  192.2 9.1 %collective-permute-start.28 = (bf16[2,144,144]{2,1,0:T(8,128)(2,1)}, bf16[2,144,144]{2,1,0:T(8,128)(2,1)S(1)}, u32[]{:S(2)}, u32[]{:S(2)}) collective-permute-start(bf16[2,144,144]{2,1,0:T(8,128)(2,1)} %get-tuple-element.26), channel_id=1, source_target_pairs={{256,1},{257,0},{258,3},{259,2},{260,5},{261,4},{262,7},{263,6},{2... | collective-permute-start | bytes 248840 | tf_op jit(solution)/shard_map/ppermute | solution.py:411
  193.8 7.5 %collective-permute-start.29 = (bf16[144,144]{1,0:T(8,128)(2,1)}, bf16[144,144]{1,0:T(8,128)(2,1)S(1)}, u32[]{:S(2)}, u32[]{:S(2)}) collective-permute-start(bf16[144,144]{1,0:T(8,128)(2,1)} %get-tuple-element.27), channel_id=1, source_target_pairs={{0,1},{1,0},{2,3},{3,2},{4,5},{5,4},{6,7},{7,6},{8,9},{9,8},{10,11... | collective-permute-start | bytes 124424 | tf_op jit(solution)/shard_map/ppermute | solution.py:39
  (12 other events, 234.7 us)

commit v4 on v3

--- a/solution.py
+++ b/solution.py
@@ -136,18 +136,19 @@
     pieces = refs[:-5]
     half = len(pieces) // 2
     z, y = pos[1], pos[2]
-    steps = (0, -1, -2, -3, 1, 2, 3, 4)
+    steps = (0, -1, -2, -3, 1, 2, 3, 4, 4)
 
     def copies(side, index):
         ref = pieces[side * half + index]
-        for sub in range(8):
+        subs = range(8) if index < 7 else (range(4) if index == 7 else range(4, 8))
+        for slot, sub in enumerate(subs):
             if side == 0:
                 plane, line = lax.rem(z + steps[index] + 8, 8), y ^ OFFS[sub]
             else:
                 plane, line = z ^ OFFS[sub], lax.rem(y + steps[index] + 8, 8)
             row = pl.multiple_of((plane * 8 + line) * 64, 64)
             yield pltpu.make_async_copy(
-                ref.at[pl.ds(sub * 64, 64)], held.at[side, pl.ds(row, 64)], sems.at[side, index]
+                ref.at[pl.ds(slot * 64, 64)], held.at[side, pl.ds(row, 64)], sems.at[side, index]
             )
 
     def turn(side, plane):
@@ -167,7 +168,8 @@
     for index in range(half):
         for c in every[0][index]:
             c.wait()
-        leaving.append(turn(0, lax.rem(z + steps[index] + 8, 8)))
+        if index != 7:
+            leaving.append(turn(0, lax.rem(z + steps[index] + 8, 8)))
     for group in every[1]:
         for c in group:
             c.wait()
@@ -195,15 +197,17 @@
     held = [a, a, b, b]
     for step in range(4):
         for n, (axis, by) in enumerate(chains):
-            if step < 3 or by > 0:
-                held[n] = ring(held[n], axis, by)
-                got[n].append(held[n])
+            value = held[n]
+            if step == 3:
+                value = value[:256] if by > 0 else value[256:]
+            held[n] = ring(value, axis, by)
+            got[n].append(held[n])
     *lasts, message = lax.optimization_barrier((*[g[-1] for g in got], message))
     for g, last in zip(got, lasts):
         g[-1] = last
     pieces = []
     for own, ahead, behind in ((a, got[0], got[1]), (b, got[2], got[3])):
-        pieces += [own, *ahead[:3], *behind, ahead[3]]
+        pieces += [own, *ahead[:3], *behind[:3], ahead[3], behind[3]]
     section = pl.pallas_call(
         join_kernel,
         out_shape=jax.ShapeDtypeStruct((1024, 4096), BF),
@@ -212,7 +216,7 @@
         scratch_shapes=[
             pltpu.VMEM((2, 4096, 512), BF),
             pltpu.VMEM((1024, 4096), BF),
-            pltpu.SemaphoreType.DMA((2, 8)),
+            pltpu.SemaphoreType.DMA((2, 9)),
             pltpu.SemaphoreType.DMA(()),
         ],
         compiler_params=pltpu.CompilerParams(vmem_limit_bytes=60 * MIB),

time: 250 us -> 254 us (1.016)
  starting transfers between devices: 101 us -> 110 us
  waiting for transfers between devices: 31.7 us -> 25.1 us
    ppermute x14 -> x16, starting transfers between devices: 44.3 us -> 53.4 us  [ring(): return lax.ppermute(value, axis, [(i, (i + by) % n) for i in range(n)])]
    ppermute x14 -> x16, waiting for transfers between devices: 14.7 us -> 8.37 us  [ring(): return lax.ppermute(value, axis, [(i, (i + by) % n) for i in range(n)])]
    unnamed x38 -> x52, local copies, waits for them, and re-layouts: 4.79 us -> 5.57 us
  transfers between devices with their start and end apart: 30 -> 32, of which waited for: 13 -> 11; matrix products, arithmetic and copies ran while one was open for 2% -> 2% of each run, Pallas kernels for 5% -> 5%
where the time goes in v4:
time: 254 us; the launch traced here: 252 us
  starting transfers between devices  110 us (43%)
  blocking collectives  54 us (21%)
  Pallas kernels  49.5 us (19%)
  waiting for transfers between devices  25.1 us (10%)
  local copies, waits for them, and re-layouts  9.09 us (4%)
  other arithmetic  3.39 us (1%)
    ppermute x16, starting transfers between devices, ring(): return lax.ppermute(value, axis, [(i, (i + by) % n) for i in range(n)])  53.4 us
    ppermute x12, starting transfers between devices, swap(): return lax.ppermute(value, axis, [(i, i ^ bit) for i in range(n)])  50.5 us
    all_to_all x1, blocking collectives, per_device(): came_back = lax.all_to_all(reply, LAT, 0, 0, tiled=True)  36.2 us
    pallas_call x3, Pallas kernels, sections_call(): pl.pallas_call(body, out_shape=tuple((jax.ShapeDtypeStruct(shape, BF) for...  31.2 us
    all_to_all x1, blocking collectives, per_device(): arrived = lax.all_to_all(message, ('y', 'xl'), 0, 0, tiled=True)  15.8 us
    pallas_call x4, Pallas kernels, small_call(): pl.pallas_call(body, out_shape=jax.ShapeDtypeStruct((out_rows, PACK, 128)...  10.2 us
    ppermute x4, waiting for transfers between devices, crossed(): return lax.ppermute(value, ('xh', 'xl'), [(x, 3 - x) for x in sources])  8.79 us
    ppermute x16, waiting for transfers between devices, ring(): return lax.ppermute(value, axis, [(i, (i + by) % n) for i in range(n)])  8.37 us
  transfers between devices with their start and end apart: 32, of which 11 were waited for; matrix products, arithmetic and copies ran while one was open for 2% of the time, Pallas kernels for 5%

profile of v4, /device:TPU:12, one launch (start us, length us, event | category | flops | bytes accessed | tf_op | source)
XLA Modules:
  0.0 252.3 jit_solution(11600195506888868696)
XLA Ops:
  0.6 3.1 %collective-permute-start = (bf16[32,1024]{1,0:T(8,128)(2,1)}, bf16[32,1024]{1,0:T(8,128)(2,1)S(1)}, u32[]{:S(2)}, u32[]{:S(2)}) collective-permute-start(bf16[32,1024]{1,0:T(8,128)(2,1)} %bitcast.49), channel_id=1, source_target_pairs={{0,1},{1,0},{2,3},{3,2},{4,5},{5,4},{6,7},{7,6},{8,9},{9,8},{10,11... | collective-permute-start | bytes 196616 | tf_op jit(solution)/shard_map/ppermute | solution.py:39
  4.9 10.9 %collective-permute-start.7 = (bf16[14,16,128]{2,1,0:T(8,128)(2,1)S(1)}, bf16[14,16,128]{2,1,0:T(8,128)(2,1)S(1)}, u32[]{:S(2)}, u32[]{:S(2)}) collective-permute-start(bf16[14,16,128]{2,1,0:T(8,128)(2,1)S(1)} %slice.58), channel_id=1, source_target_pairs={{0,64},{16,80},{32,96},{48,112},{64,0},{80,16},{96,32},{112,48},{1... | collective-permute-start | bytes 172040 | tf_op jit(solution)/shard_map/ppermute | solution.py:39
  21.3 4.3 %collective-permute-start.8 = (bf16[28,16,128]{2,1,0:T(8,128)(2,1)S(1)}, bf16[28,16,128]{2,1,0:T(8,128)(2,1)S(1)}, u32[]{:S(2)}, u32[]{:S(2)}) collective-permute-start(bf16[28,16,128]{2,1,0:T(8,128)(2,1)S(1)} %pad_maximum_fusion.9), channel_id=1, source_target_pairs={{0,32},{16,48},{32,0},{48,16},{64,96},{80,112},{96,64},{112,80},{1... | collective-permute-start | bytes 344072 | tf_op jit(solution)/shard_map/ppermute | solution.py:39
  25.6 6.8 %collective-permute-start.1 = (bf16[64,512]{1,0:T(8,128)(2,1)S(1)}, bf16[64,512]{1,0:T(8,128)(2,1)S(1)}, u32[]{:S(2)}, u32[]{:S(2)}) collective-permute-start(bf16[64,512]{1,0:T(8,128)(2,1)S(1)} %get-tuple-element.35), channel_id=1, source_target_pairs={{0,8},{2,10},{4,12},{6,14},{8,0},{10,2},{12,4},{14,6},{1,9},{3,11}... | collective-permute-start | bytes 196616 | tf_op jit(solution)/shard_map/ppermute | solution.py:39
  32.4 2.6 %collective-permute-start.5 = (bf16[128,512]{1,0:T(8,128)(2,1)S(1)}, bf16[128,512]{1,0:T(8,128)(2,1)S(1)}, u32[]{:S(2)}, u32[]{:S(2)}) collective-permute-start(bf16[128,512]{1,0:T(8,128)(2,1)S(1)} %pad_maximum_fusion.8), channel_id=1, source_target_pairs={{0,32},{16,48},{32,0},{48,16},{64,96},{80,112},{96,64},{112,80},{1... | collective-permute-start | bytes 393224 | tf_op jit(solution)/shard_map/ppermute | solution.py:39
  35.6 4.5 %collective-permute-start.2 = (bf16[128,512]{1,0:T(8,128)(2,1)S(1)}, bf16[128,512]{1,0:T(8,128)(2,1)S(1)}, u32[]{:S(2)}, u32[]{:S(2)}) collective-permute-start(bf16[128,512]{1,0:T(8,128)(2,1)S(1)} %pad_maximum_fusion.7), channel_id=1, source_target_pairs={{0,4},{2,6},{4,0},{6,2},{8,12},{10,14},{12,8},{14,10},{1,5},{3,7},... | collective-permute-start | bytes 393224 | tf_op jit(solution)/shard_map/ppermute | solution.py:39
  40.2 3.4 %collective-permute-start.9 = (bf16[56,16,128]{2,1,0:T(8,128)(2,1)S(1)}, bf16[56,16,128]{2,1,0:T(8,128)(2,1)S(1)}, u32[]{:S(2)}, u32[]{:S(2)}) collective-permute-start(bf16[56,16,128]{2,1,0:T(8,128)(2,1)S(1)} %pad_maximum_fusion.5), channel_id=1, source_target_pairs={{0,16},{16,0},{32,48},{48,32},{64,80},{80,64},{96,112},{112,96},{1... | collective-permute-start | bytes 688136 | tf_op jit(solution)/shard_map/ppermute | solution.py:39
  43.6 2.5 collective-permute-start.6
  46.1 3.5 %collective-permute-start.3 = (bf16[256,512]{1,0:T(8,128)(2,1)S(1)}, bf16[256,512]{1,0:T(8,128)(2,1)S(1)}, u32[]{:S(2)}, u32[]{:S(2)}) collective-permute-start(bf16[256,512]{1,0:T(8,128)(2,1)S(1)} %pad_maximum_fusion.3), channel_id=1, source_target_pairs={{0,2},{2,0},{4,6},{6,4},{8,10},{10,8},{12,14},{14,12},{1,3},{3,1},... | collective-permute-start | bytes 786440 | tf_op jit(solution)/shard_map/ppermute | solution.py:39
  50.7 3.2 %collective-permute-done.6 = bf16[256,512]{1,0:T(8,128)(2,1)S(1)} collective-permute-done((bf16[256,512]{1,0:T(8,128)(2,1)S(1)}, bf16[256,512]{1,0:T(8,128)(2,1)S(1)}, u32[]{:S(2)}, u32[]{:S(2)}) %collective-permute-start.6) | collective-permute-done | bytes 262176 | tf_op jit(solution)/shard_map/ppermute | solution.py:39
  55.3 3.2 %collective-permute-start.10 = (bf16[512,512]{1,0:T(8,128)(2,1)S(1)}, bf16[512,512]{1,0:T(8,128)(2,1)S(1)}, u32[]{:S(2)}, u32[]{:S(2)}) collective-permute-start(bf16[512,512]{1,0:T(8,128)(2,1)S(1)} %pad_maximum_fusion.refs_0_), channel_id=1, source_target_pairs={{0,16},{16,32},{32,48},{48,64},{64,80},{80,96},{96,112},{112,0},{1... | collective-permute-start | bytes 1572872 | tf_op jit(solution)/shard_map/ppermute | solution.py:34
  58.5 5.6 %collective-permute-start.14 = (bf16[512,512]{1,0:T(8,128)(2,1)S(1)}, bf16[512,512]{1,0:T(8,128)(2,1)S(1)}, u32[]{:S(2)}, u32[]{:S(2)}) collective-permute-start(bf16[512,512]{1,0:T(8,128)(2,1)S(1)} %pad_maximum_fusion.refs_0_), channel_id=1, source_target_pairs={{0,112},{16,0},{32,16},{48,32},{64,48},{80,64},{96,80},{112,96},{1... | collective-permute-start | bytes 1572872 | tf_op jit(solution)/shard_map/ppermute | solution.py:34
  66.1 3.9 %collective-permute-start.22 = (bf16[512,512]{1,0:T(8,128)(2,1)S(1)}, bf16[512,512]{1,0:T(8,128)(2,1)S(1)}, u32[]{:S(2)}, u32[]{:S(2)}) collective-permute-start(bf16[512,512]{1,0:T(8,128)(2,1)S(1)} %pad_maximum_fusion.1.refs_9_), channel_id=1, source_target_pairs={{0,14},{2,0},{4,2},{6,4},{8,6},{10,8},{12,10},{14,12},{1,15},{3,1}... | collective-permute-start | bytes 1572872 | tf_op jit(solution)/shard_map/ppermute | solution.py:34
  70.0 3.3 %collective-permute-done.10.refs_1_ = bf16[512,512]{1,0:T(8,128)(2,1)S(1)} collective-permute-done((bf16[512,512]{1,0:T(8,128)(2,1)S(1)}, bf16[512,512]{1,0:T(8,128)(2,1)S(1)}, u32[]{:S(2)}, u32[]{:S(2)}) %collective-permute-start.10) | collective-permute-done | bytes 524320 | tf_op jit(solution)/shard_map/ppermute | solution.py:34
  75.2 5.1 %collective-permute-start.15 = (bf16[512,512]{1,0:T(8,128)(2,1)S(1)}, bf16[512,512]{1,0:T(8,128)(2,1)S(1)}, u32[]{:S(2)}, u32[]{:S(2)}) collective-permute-start(bf16[512,512]{1,0:T(8,128)(2,1)S(1)} %collective-permute-done.14.refs_4_), channel_id=1, source_target_pairs={{0,112},{16,0},{32,16},{48,32},{64,48},{80,64},{96,80},{112,96},{1... | collective-permute-start | bytes 1572872 | tf_op jit(solution)/shard_map/ppermute | solution.py:34
  82.3 3.9 %collective-permute-start.23 = (bf16[512,512]{1,0:T(8,128)(2,1)S(1)}, bf16[512,512]{1,0:T(8,128)(2,1)S(1)}, u32[]{:S(2)}, u32[]{:S(2)}) collective-permute-start(bf16[512,512]{1,0:T(8,128)(2,1)S(1)} %collective-permute-done.22.refs_13_), channel_id=1, source_target_pairs={{0,14},{2,0},{4,2},{6,4},{8,6},{10,8},{12,10},{14,12},{1,15},{3,1}... | collective-permute-start | bytes 1572872 | tf_op jit(solution)/shard_map/ppermute | solution.py:34
  90.5 5.1 %collective-permute-start.16 = (bf16[512,512]{1,0:T(8,128)(2,1)S(1)}, bf16[512,512]{1,0:T(8,128)(2,1)S(1)}, u32[]{:S(2)}, u32[]{:S(2)}) collective-permute-start(bf16[512,512]{1,0:T(8,128)(2,1)S(1)} %collective-permute-done.15.refs_5_), channel_id=1, source_target_pairs={{0,112},{16,0},{32,16},{48,32},{64,48},{80,64},{96,80},{112,96},{1... | collective-permute-start | bytes 1572872 | tf_op jit(solution)/shard_map/ppermute | solution.py:34
  97.6 3.9 %collective-permute-start.24 = (bf16[512,512]{1,0:T(8,128)(2,1)S(1)}, bf16[512,512]{1,0:T(8,128)(2,1)S(1)}, u32[]{:S(2)}, u32[]{:S(2)}) collective-permute-start(bf16[512,512]{1,0:T(8,128)(2,1)S(1)} %collective-permute-done.23.refs_14_), channel_id=1, source_target_pairs={{0,14},{2,0},{4,2},{6,4},{8,6},{10,8},{12,10},{14,12},{1,15},{3,1}... | collective-permute-start | bytes 1572872 | tf_op jit(solution)/shard_map/ppermute | solution.py:34
  104.9 5.1 %collective-permute-start.17 = (bf16[256,512]{1,0:T(8,128)(2,1)S(1)}, bf16[256,512]{1,0:T(8,128)(2,1)}, u32[]{:S(2)}, u32[]{:S(2)}) collective-permute-start(bf16[256,512]{1,0:T(8,128)(2,1)S(1)} %slice.49), channel_id=1, source_target_pairs={{0,112},{16,0},{32,16},{48,32},{64,48},{80,64},{96,80},{112,96},{1... | collective-permute-start | bytes 786440 | tf_op jit(solution)/shard_map/ppermute | solution.py:34
  112.8 3.9 %collective-permute-start.25 = (bf16[256,512]{1,0:T(8,128)(2,1)S(1)}, bf16[256,512]{1,0:T(8,128)(2,1)}, u32[]{:S(2)}, u32[]{:S(2)}) collective-permute-start(bf16[256,512]{1,0:T(8,128)(2,1)S(1)} %slice.51), channel_id=1, source_target_pairs={{0,14},{2,0},{4,2},{6,4},{8,6},{10,8},{12,10},{14,12},{1,15},{3,1}... | collective-permute-start | bytes 786440 | tf_op jit(solution)/shard_map/ppermute | solution.py:34
  121.2 8.1 %join.1.own_ref = bf16[1024,4096]{1,0:T(8,128)(2,1)} custom-call(s32[5]{0:T(128)} %stack.23.where.pos, bf16[512,512]{1,0:T(8,128)(2,1)} %copy-done.1, bf16[512,512]{1,0:T(8,128)(2,1)} %copy-done.12, bf16[512,512]{1,0:T(8,128)(2,1)} %copy-done.16, bf16[512,512]{1,0:T(8,128)(2,1)} %copy-done.7, bf16[512,512]{1,0:T(8,128)(2,1)} %copy-done.13, ...), custom_call_target="tpu_custom_call" | custom-call | flops 10000000000 | bytes 25165824 | tf_op jit(solution)/shard_map/join/pallas_call | solution.py:211
  131.3 15.8 %all_to_all.10.came_ref = bf16[32,16,128]{2,1,0:T(8,128)(2,1)} all-to-all(bf16[32,16,128]{2,1,0:T(8,128)(2,1)S(1)} %copy-done.2), channel_id=1, replica_groups=mesh['xh'=2,'c'=2,'z'=8,'y'=8,'xl'=2] {'y','xl'}, dimensions={0} | all-to-all | bytes 262144 | tf_op jit(solution)/shard_map/all_to_all | solution.py:436
  147.1 2.4 pick.1
  154.5 8.9 %early.3 = bf16[144,1024]{1,0:T(8,128)(2,1)} custom-call(s32[5]{0:T(128)} %stack.23.where.pos, s32[128]{0:T(128)} %bands.13, s32[128]{0:T(128)} %table.13, bf16[144,144]{1,0:T(8,128)(2,1)} %copy-done.11, bf16[144,1024]{1,0:T(8,128)(2,1)} %embed_ref.3, bf16[2,1024]{1,0:T(2,128)(2,1)} %level_ref.3, f32[2,1024]{1,0:T(2,128)} %bitcast.46, ...), custom_call_target="tpu_custom_call" | custom-call | tf_op jit(solution)/shard_map/early/pallas_call | solution.py:390
  165.0 8.9 %early.2 = bf16[144,1024]{1,0:T(8,128)(2,1)} custom-call(s32[5]{0:T(128)} %stack.23.where.pos, s32[128]{0:T(128)} %bands.13, s32[128]{0:T(128)} %table.13, bf16[144,144]{1,0:T(8,128)(2,1)} %copy-done.3, bf16[144,1024]{1,0:T(8,128)(2,1)} %embed_ref.3, bf16[2,1024]{1,0:T(2,128)(2,1)} %level_ref.3, f32[2,1024]{1,0:T(2,128)} %bitcast.47, ...), custom_call_target="tpu_custom_call" | custom-call | tf_op jit(solution)/shard_map/early/pallas_call | solution.py:390
  176.3 6.8 %collective-permute-done.27.came_ref = bf16[144,1024]{1,0:T(8,128)(2,1)S(1)} collective-permute-done((bf16[144,1024]{1,0:T(8,128)(2,1)}, bf16[144,1024]{1,0:T(8,128)(2,1)S(1)}, u32[]{:S(2)}, u32[]{:S(2)}) %collective-permute-start.27) | collective-permute-done | bytes 294944 | tf_op jit(solution)/shard_map/ppermute | solution.py:415
  183.8 13.4 %late.1 = (bf16[2,144,144]{2,1,0:T(8,128)(2,1)}, bf16[144,144]{1,0:T(8,128)(2,1)}, bf16[144,144]{1,0:T(8,128)(2,1)}) custom-call(s32[5]{0:T(128)} %stack.23.where.pos, s32[128]{0:T(128)} %bands.13, s32[128]{0:T(128)} %table.13, bf16[144,1024]{1,0:T(8,128)(2,1)} %copy-done.6, bf16[144,1024]{1,0:T(8,128)(2,1)} %copy-done.5, f32[2,1024]{1,0:T(2,128)} %bitcast.48, ...), custom_call_target="tpu_custom_call" | custom-call | tf_op jit(solution)/shard_map/late/pallas_call | solution.py:390
  198.8 5.2 %collective-permute-start.31 = (bf16[144,144]{1,0:T(8,128)(2,1)}, bf16[144,144]{1,0:T(8,128)(2,1)S(1)}, u32[]{:S(2)}, u32[]{:S(2)}) collective-permute-start(bf16[144,144]{1,0:T(8,128)(2,1)} %get-tuple-element.27), channel_id=1, source_target_pairs={{0,1},{1,0},{2,3},{3,2},{4,5},{5,4},{6,7},{7,6},{8,9},{9,8},{10,11... | collective-permute-start | bytes 124424 | tf_op jit(solution)/shard_map/ppermute | solution.py:39
  204.0 2.5 %collective-permute-done.31 = bf16[144,144]{1,0:T(8,128)(2,1)S(1)} collective-permute-done((bf16[144,144]{1,0:T(8,128)(2,1)}, bf16[144,144]{1,0:T(8,128)(2,1)S(1)}, u32[]{:S(2)}, u32[]{:S(2)}) %collective-permute-start.31) | collective-permute-done | bytes 41504 | tf_op jit(solution)/shard_map/ppermute | solution.py:39
  208.9 2.4 unpick.1
  211.3 36.2 %all_to_all.11.came_ref = bf16[256,16,128]{2,1,0:T(8,128)(2,1)} all-to-all(bf16[256,16,128]{2,1,0:T(8,128)(2,1)} %unpick.1), channel_id=1, replica_groups=mesh['xh'=2,'c'=2,'z'=8,'y'=8,'xl'=2] {'z','y','xl'}, dimensions={0} | all-to-all | bytes 2097152 | tf_op jit(solution)/shard_map/all_to_all | solution.py:468
  247.6 3.0 %unpack.1 = bf16[15,16,128]{2,1,0:T(8,128)(2,1)} custom-call(s32[5]{0:T(128)} %stack.23.where.pos, s32[128]{0:T(128)} %bands.13, s32[128]{0:T(128)} %table.13, bf16[256,16,128]{2,1,0:T(8,128)(2,1)} %all_to_all.11.came_ref), custom_call_target="tpu_custom_call" | custom-call | tf_op jit(solution)/shard_map/unpack/pallas_call | solution.py:405
  (125 shorter events, 49.2 us)
Async XLA Ops:
  0.6 17.8 %collective-permute-start = (bf16[32,1024]{1,0:T(8,128)(2,1)}, bf16[32,1024]{1,0:T(8,128)(2,1)S(1)}, u32[]{:S(2)}, u32[]{:S(2)}) collective-permute-start(bf16[32,1024]{1,0:T(8,128)(2,1)} %bitcast.49), channel_id=1, source_target_pairs={{0,1},{1,0},{2,3},{3,2},{4,5},{5,4},{6,7},{7,6},{8,9},{9,8},{10,11... | collective-permute-start | bytes 196616 | tf_op jit(solution)/shard_map/ppermute | solution.py:39
  4.9 16.3 %collective-permute-start.7 = (bf16[14,16,128]{2,1,0:T(8,128)(2,1)S(1)}, bf16[14,16,128]{2,1,0:T(8,128)(2,1)S(1)}, u32[]{:S(2)}, u32[]{:S(2)}) collective-permute-start(bf16[14,16,128]{2,1,0:T(8,128)(2,1)S(1)} %slice.58), channel_id=1, source_target_pairs={{0,64},{16,80},{32,96},{48,112},{64,0},{80,16},{96,32},{112,48},{1... | collective-permute-start | bytes 172040 | tf_op jit(solution)/shard_map/ppermute | solution.py:39
  19.3 13.1 %collective-permute-start.4 = (bf16[64,512]{1,0:T(8,128)(2,1)S(1)}, bf16[64,512]{1,0:T(8,128)(2,1)S(1)}, u32[]{:S(2)}, u32[]{:S(2)}) collective-permute-start(bf16[64,512]{1,0:T(8,128)(2,1)S(1)} %get-tuple-element.34), channel_id=1, source_target_pairs={{0,64},{16,80},{32,96},{48,112},{64,0},{80,16},{96,32},{112,48},{1... | collective-permute-start | bytes 196616 | tf_op jit(solution)/shard_map/ppermute | solution.py:39
  21.3 18.9 %collective-permute-start.8 = (bf16[28,16,128]{2,1,0:T(8,128)(2,1)S(1)}, bf16[28,16,128]{2,1,0:T(8,128)(2,1)S(1)}, u32[]{:S(2)}, u32[]{:S(2)}) collective-permute-start(bf16[28,16,128]{2,1,0:T(8,128)(2,1)S(1)} %pad_maximum_fusion.9), channel_id=1, source_target_pairs={{0,32},{16,48},{32,0},{48,16},{64,96},{80,112},{96,64},{112,80},{1... | collective-permute-start | bytes 344072 | tf_op jit(solution)/shard_map/ppermute | solution.py:39
  25.6 10.1 %collective-permute-start.1 = (bf16[64,512]{1,0:T(8,128)(2,1)S(1)}, bf16[64,512]{1,0:T(8,128)(2,1)S(1)}, u32[]{:S(2)}, u32[]{:S(2)}) collective-permute-start(bf16[64,512]{1,0:T(8,128)(2,1)S(1)} %get-tuple-element.35), channel_id=1, source_target_pairs={{0,8},{2,10},{4,12},{6,14},{8,0},{10,2},{12,4},{14,6},{1,9},{3,11}... | collective-permute-start | bytes 196616 | tf_op jit(solution)/shard_map/ppermute | solution.py:39
  32.4 11.2 %collective-permute-start.5 = (bf16[128,512]{1,0:T(8,128)(2,1)S(1)}, bf16[128,512]{1,0:T(8,128)(2,1)S(1)}, u32[]{:S(2)}, u32[]{:S(2)}) collective-permute-start(bf16[128,512]{1,0:T(8,128)(2,1)S(1)} %pad_maximum_fusion.8), channel_id=1, source_target_pairs={{0,32},{16,48},{32,0},{48,16},{64,96},{80,112},{96,64},{112,80},{1... | collective-permute-start | bytes 393224 | tf_op jit(solution)/shard_map/ppermute | solution.py:39
  35.6 10.4 %collective-permute-start.2 = (bf16[128,512]{1,0:T(8,128)(2,1)S(1)}, bf16[128,512]{1,0:T(8,128)(2,1)S(1)}, u32[]{:S(2)}, u32[]{:S(2)}) collective-permute-start(bf16[128,512]{1,0:T(8,128)(2,1)S(1)} %pad_maximum_fusion.7), channel_id=1, source_target_pairs={{0,4},{2,6},{4,0},{6,2},{8,12},{10,14},{12,8},{14,10},{1,5},{3,7},... | collective-permute-start | bytes 393224 | tf_op jit(solution)/shard_map/ppermute | solution.py:39
  40.2 9.7 %collective-permute-start.9 = (bf16[56,16,128]{2,1,0:T(8,128)(2,1)S(1)}, bf16[56,16,128]{2,1,0:T(8,128)(2,1)S(1)}, u32[]{:S(2)}, u32[]{:S(2)}) collective-permute-start(bf16[56,16,128]{2,1,0:T(8,128)(2,1)S(1)} %pad_maximum_fusion.5), channel_id=1, source_target_pairs={{0,16},{16,0},{32,48},{48,32},{64,80},{80,64},{96,112},{112,96},{1... | collective-permute-start | bytes 688136 | tf_op jit(solution)/shard_map/ppermute | solution.py:39
  43.6 10.3 %collective-permute-start.6 = (bf16[256,512]{1,0:T(8,128)(2,1)S(1)}, bf16[256,512]{1,0:T(8,128)(2,1)S(1)}, u32[]{:S(2)}, u32[]{:S(2)}) collective-permute-start(bf16[256,512]{1,0:T(8,128)(2,1)S(1)} %pad_maximum_fusion.4), channel_id=1, source_target_pairs={{0,16},{16,0},{32,48},{48,32},{64,80},{80,64},{96,112},{112,96},{1... | collective-permute-start | bytes 786440 | tf_op jit(solution)/shard_map/ppermute | solution.py:39
  46.1 9.1 %collective-permute-start.3 = (bf16[256,512]{1,0:T(8,128)(2,1)S(1)}, bf16[256,512]{1,0:T(8,128)(2,1)S(1)}, u32[]{:S(2)}, u32[]{:S(2)}) collective-permute-start(bf16[256,512]{1,0:T(8,128)(2,1)S(1)} %pad_maximum_fusion.3), channel_id=1, source_target_pairs={{0,2},{2,0},{4,6},{6,4},{8,10},{10,8},{12,14},{14,12},{1,3},{3,1},... | collective-permute-start | bytes 786440 | tf_op jit(solution)/shard_map/ppermute | solution.py:39
  55.3 18.0 %collective-permute-start.10 = (bf16[512,512]{1,0:T(8,128)(2,1)S(1)}, bf16[512,512]{1,0:T(8,128)(2,1)S(1)}, u32[]{:S(2)}, u32[]{:S(2)}) collective-permute-start(bf16[512,512]{1,0:T(8,128)(2,1)S(1)} %pad_maximum_fusion.refs_0_), channel_id=1, source_target_pairs={{0,16},{16,32},{32,48},{48,64},{64,80},{80,96},{96,112},{112,0},{1... | collective-permute-start | bytes 1572872 | tf_op jit(solution)/shard_map/ppermute | solution.py:34
  58.5 16.7 %collective-permute-start.14 = (bf16[512,512]{1,0:T(8,128)(2,1)S(1)}, bf16[512,512]{1,0:T(8,128)(2,1)S(1)}, u32[]{:S(2)}, u32[]{:S(2)}) collective-permute-start(bf16[512,512]{1,0:T(8,128)(2,1)S(1)} %pad_maximum_fusion.refs_0_), channel_id=1, source_target_pairs={{0,112},{16,0},{32,16},{48,32},{64,48},{80,64},{96,80},{112,96},{1... | collective-permute-start | bytes 1572872 | tf_op jit(solution)/shard_map/ppermute | solution.py:34
  64.2 16.2 %collective-permute-start.18 = (bf16[512,512]{1,0:T(8,128)(2,1)S(1)}, bf16[512,512]{1,0:T(8,128)(2,1)S(1)}, u32[]{:S(2)}, u32[]{:S(2)}) collective-permute-start(bf16[512,512]{1,0:T(8,128)(2,1)S(1)} %pad_maximum_fusion.1.refs_9_), channel_id=1, source_target_pairs={{0,2},{2,4},{4,6},{6,8},{8,10},{10,12},{12,14},{14,0},{1,3},{3,5},... | collective-permute-start | bytes 1572872 | tf_op jit(solution)/shard_map/ppermute | solution.py:34
  66.1 16.2 %collective-permute-start.22 = (bf16[512,512]{1,0:T(8,128)(2,1)S(1)}, bf16[512,512]{1,0:T(8,128)(2,1)S(1)}, u32[]{:S(2)}, u32[]{:S(2)}) collective-permute-start(bf16[512,512]{1,0:T(8,128)(2,1)S(1)} %pad_maximum_fusion.1.refs_9_), channel_id=1, source_target_pairs={{0,14},{2,0},{4,2},{6,4},{8,6},{10,8},{12,10},{14,12},{1,15},{3,1}... | collective-permute-start | bytes 1572872 | tf_op jit(solution)/shard_map/ppermute | solution.py:34
  73.3 15.3 %collective-permute-start.11 = (bf16[512,512]{1,0:T(8,128)(2,1)S(1)}, bf16[512,512]{1,0:T(8,128)(2,1)S(1)}, u32[]{:S(2)}, u32[]{:S(2)}) collective-permute-start(bf16[512,512]{1,0:T(8,128)(2,1)S(1)} %collective-permute-done.10.refs_1_), channel_id=1, source_target_pairs={{0,16},{16,32},{32,48},{48,64},{64,80},{80,96},{96,112},{112,0},{1... | collective-permute-start | bytes 1572872 | tf_op jit(solution)/shard_map/ppermute | solution.py:34
  75.2 15.2 %collective-permute-start.15 = (bf16[512,512]{1,0:T(8,128)(2,1)S(1)}, bf16[512,512]{1,0:T(8,128)(2,1)S(1)}, u32[]{:S(2)}, u32[]{:S(2)}) collective-permute-start(bf16[512,512]{1,0:T(8,128)(2,1)S(1)} %collective-permute-done.14.refs_4_), channel_id=1, source_target_pairs={{0,112},{16,0},{32,16},{48,32},{64,48},{80,64},{96,80},{112,96},{1... | collective-permute-start | bytes 1572872 | tf_op jit(solution)/shard_map/ppermute | solution.py:34
  80.4 15.2 %collective-permute-start.19 = (bf16[512,512]{1,0:T(8,128)(2,1)S(1)}, bf16[512,512]{1,0:T(8,128)(2,1)S(1)}, u32[]{:S(2)}, u32[]{:S(2)}) collective-permute-start(bf16[512,512]{1,0:T(8,128)(2,1)S(1)} %collective-permute-done.18.refs_10_), channel_id=1, source_target_pairs={{0,2},{2,4},{4,6},{6,8},{8,10},{10,12},{12,14},{14,0},{1,3},{3,5},... | collective-permute-start | bytes 1572872 | tf_op jit(solution)/shard_map/ppermute | solution.py:34
  82.3 15.2 %collective-permute-start.23 = (bf16[512,512]{1,0:T(8,128)(2,1)S(1)}, bf16[512,512]{1,0:T(8,128)(2,1)S(1)}, u32[]{:S(2)}, u32[]{:S(2)}) collective-permute-start(bf16[512,512]{1,0:T(8,128)(2,1)S(1)} %collective-permute-done.22.refs_13_), channel_id=1, source_target_pairs={{0,14},{2,0},{4,2},{6,4},{8,6},{10,8},{12,10},{14,12},{1,15},{3,1}... | collective-permute-start | bytes 1572872 | tf_op jit(solution)/shard_map/ppermute | solution.py:34
  88.5 14.3 %collective-permute-start.12 = (bf16[512,512]{1,0:T(8,128)(2,1)S(1)}, bf16[512,512]{1,0:T(8,128)(2,1)S(1)}, u32[]{:S(2)}, u32[]{:S(2)}) collective-permute-start(bf16[512,512]{1,0:T(8,128)(2,1)S(1)} %collective-permute-done.11.refs_2_), channel_id=1, source_target_pairs={{0,16},{16,32},{32,48},{48,64},{64,80},{80,96},{96,112},{112,0},{1... | collective-permute-start | bytes 1572872 | tf_op jit(solution)/shard_map/ppermute | solution.py:34
  90.5 14.3 %collective-permute-start.16 = (bf16[512,512]{1,0:T(8,128)(2,1)S(1)}, bf16[512,512]{1,0:T(8,128)(2,1)S(1)}, u32[]{:S(2)}, u32[]{:S(2)}) collective-permute-start(bf16[512,512]{1,0:T(8,128)(2,1)S(1)} %collective-permute-done.15.refs_5_), channel_id=1, source_target_pairs={{0,112},{16,0},{32,16},{48,32},{64,48},{80,64},{96,80},{112,96},{1... | collective-permute-start | bytes 1572872 | tf_op jit(solution)/shard_map/ppermute | solution.py:34
  95.6 14.4 %collective-permute-start.20 = (bf16[512,512]{1,0:T(8,128)(2,1)S(1)}, bf16[512,512]{1,0:T(8,128)(2,1)S(1)}, u32[]{:S(2)}, u32[]{:S(2)}) collective-permute-start(bf16[512,512]{1,0:T(8,128)(2,1)S(1)} %collective-permute-done.19.refs_11_), channel_id=1, source_target_pairs={{0,2},{2,4},{4,6},{6,8},{8,10},{10,12},{12,14},{14,0},{1,3},{3,5},... | collective-permute-start | bytes 1572872 | tf_op jit(solution)/shard_map/ppermute | solution.py:34
  97.6 14.4 %collective-permute-start.24 = (bf16[512,512]{1,0:T(8,128)(2,1)S(1)}, bf16[512,512]{1,0:T(8,128)(2,1)S(1)}, u32[]{:S(2)}, u32[]{:S(2)}) collective-permute-start(bf16[512,512]{1,0:T(8,128)(2,1)S(1)} %collective-permute-done.23.refs_14_), channel_id=1, source_target_pairs={{0,14},{2,0},{4,2},{6,4},{8,6},{10,8},{12,10},{14,12},{1,15},{3,1}... | collective-permute-start | bytes 1572872 | tf_op jit(solution)/shard_map/ppermute | solution.py:34
  102.9 16.8 %collective-permute-start.13 = (bf16[256,512]{1,0:T(8,128)(2,1)S(1)}, bf16[256,512]{1,0:T(8,128)(2,1)S(1)}, u32[]{:S(2)}, u32[]{:S(2)}) collective-permute-start(bf16[256,512]{1,0:T(8,128)(2,1)S(1)} %slice.48), channel_id=1, source_target_pairs={{0,16},{16,32},{32,48},{48,64},{64,80},{80,96},{96,112},{112,0},{1... | collective-permute-start | bytes 786440 | tf_op jit(solution)/shard_map/ppermute | solution.py:34
  104.9 14.8 %collective-permute-start.17 = (bf16[256,512]{1,0:T(8,128)(2,1)S(1)}, bf16[256,512]{1,0:T(8,128)(2,1)}, u32[]{:S(2)}, u32[]{:S(2)}) collective-permute-start(bf16[256,512]{1,0:T(8,128)(2,1)S(1)} %slice.49), channel_id=1, source_target_pairs={{0,112},{16,0},{32,16},{48,32},{64,48},{80,64},{96,80},{112,96},{1... | collective-permute-start | bytes 786440 | tf_op jit(solution)/shard_map/ppermute | solution.py:34
  110.1 9.6 %collective-permute-start.21 = (bf16[256,512]{1,0:T(8,128)(2,1)S(1)}, bf16[256,512]{1,0:T(8,128)(2,1)}, u32[]{:S(2)}, u32[]{:S(2)}) collective-permute-start(bf16[256,512]{1,0:T(8,128)(2,1)S(1)} %slice.50), channel_id=1, source_target_pairs={{0,2},{2,4},{4,6},{6,8},{8,10},{10,12},{12,14},{14,0},{1,3},{3,5},... | collective-permute-start | bytes 786440 | tf_op jit(solution)/shard_map/ppermute | solution.py:34
  112.8 8.4 %collective-permute-start.25 = (bf16[256,512]{1,0:T(8,128)(2,1)S(1)}, bf16[256,512]{1,0:T(8,128)(2,1)}, u32[]{:S(2)}, u32[]{:S(2)}) collective-permute-start(bf16[256,512]{1,0:T(8,128)(2,1)S(1)} %slice.51), channel_id=1, source_target_pairs={{0,14},{2,0},{4,2},{6,4},{8,6},{10,8},{12,10},{14,12},{1,15},{3,1}... | collective-permute-start | bytes 786440 | tf_op jit(solution)/shard_map/ppermute | solution.py:34
  129.4 24.5 %collective-permute-start.26 = (bf16[1024,4096]{1,0:T(8,128)(2,1)}, bf16[1024,4096]{1,0:T(8,128)(2,1)}, u32[]{:S(2)}, u32[]{:S(2)}) collective-permute-start(bf16[1024,4096]{1,0:T(8,128)(2,1)} %join.1.own_ref), channel_id=1, source_target_pairs={{0,128},{128,0},{1,129},{129,1},{2,130},{130,2},{3,131},{131,3},{4... | collective-permute-start | bytes 25165832 | tf_op jit(solution)/shard_map/ppermute | solution.py:39
  150.5 3.4 %collective-permute-start.28 = (bf16[144,144]{1,0:T(8,128)(2,1)S(1)}, bf16[144,144]{1,0:T(8,128)(2,1)S(1)}, u32[]{:S(2)}, u32[]{:S(2)}) collective-permute-start(bf16[144,144]{1,0:T(8,128)(2,1)S(1)} %reshape.24.raw_ref), channel_id=1, source_target_pairs={{256,1},{257,0},{258,3},{259,2},{260,5},{261,4},{262,7},{263,6},{2... | collective-permute-start | bytes 124424 | tf_op jit(solution)/shard_map/ppermute | solution.py:415
  163.4 12.9 %collective-permute-start.29 = (bf16[144,1024]{1,0:T(8,128)(2,1)}, bf16[144,1024]{1,0:T(8,128)(2,1)S(1)}, u32[]{:S(2)}, u32[]{:S(2)}) collective-permute-start(bf16[144,1024]{1,0:T(8,128)(2,1)} %early.3), channel_id=1, source_target_pairs={{0,257},{1,256},{2,259},{3,258},{4,261},{5,260},{6,263},{7,262},{8... | collective-permute-start | bytes 884744 | tf_op jit(solution)/shard_map/ppermute | solution.py:415
  174.0 9.2 %collective-permute-start.27 = (bf16[144,1024]{1,0:T(8,128)(2,1)}, bf16[144,1024]{1,0:T(8,128)(2,1)S(1)}, u32[]{:S(2)}, u32[]{:S(2)}) collective-permute-start(bf16[144,1024]{1,0:T(8,128)(2,1)} %early.2), channel_id=1, source_target_pairs={{0,257},{1,256},{2,259},{3,258},{4,261},{5,260},{6,263},{7,262},{8... | collective-permute-start | bytes 884744 | tf_op jit(solution)/shard_map/ppermute | solution.py:415
  197.3 9.3 %collective-permute-start.30 = (bf16[2,144,144]{2,1,0:T(8,128)(2,1)}, bf16[2,144,144]{2,1,0:T(8,128)(2,1)S(1)}, u32[]{:S(2)}, u32[]{:S(2)}) collective-permute-start(bf16[2,144,144]{2,1,0:T(8,128)(2,1)} %get-tuple-element.26), channel_id=1, source_target_pairs={{256,1},{257,0},{258,3},{259,2},{260,5},{261,4},{262,7},{263,6},{2... | collective-permute-start | bytes 248840 | tf_op jit(solution)/shard_map/ppermute | solution.py:415
  198.8 7.7 %collective-permute-start.31 = (bf16[144,144]{1,0:T(8,128)(2,1)}, bf16[144,144]{1,0:T(8,128)(2,1)S(1)}, u32[]{:S(2)}, u32[]{:S(2)}) collective-permute-start(bf16[144,144]{1,0:T(8,128)(2,1)} %get-tuple-element.27), channel_id=1, source_target_pairs={{0,1},{1,0},{2,3},{3,2},{4,5},{5,4},{6,7},{7,6},{8,9},{9,8},{10,11... | collective-permute-start | bytes 124424 | tf_op jit(solution)/shard_map/ppermute | solution.py:39
  (21 other events, 385.7 us)
